TPU v7x, 32 devices: a whole 2x2x4 slice. The times are simulated.
32 devices in a mesh: seq: 16 (over z, y, core), dp: 2 (over x).
Axes of the slice: x: 2, y: 2, z: 4, core: 2. Of those that a mesh axis runs over, the one named last changes fastest.
Arguments:
- genome: bfloat16 [2, 32768, 512], P('dp', 'seq'), may hold values from -6 to 6
- conv_weight: bfloat16 [3, 512, 512], replicated, may hold values from -0.15625 to 0.15625
- upstream: bfloat16 [2, 32768, 512], P('dp', 'seq'), may hold values from -6 to 6
Outputs:
- output: bfloat16 [2, 32768, 512], P('dp', 'seq')
- grad_genome: bfloat16 [2, 32768, 512], P('dp', 'seq')
- grad_weight: float32 [3, 512, 512], replicated
All inputs are finite; a program needn't handle non-finite values.
Results may differ from a plain program's by a relative error of at most 0.0035.
Values may be sent and summed in bfloat16 or wider, within the bound.
No kernel may reach another device: no remote copies, remote signals or barrier semaphores. Data moves between devices by JAX's collectives and lax.ppermute only.
A program may use at most 128 MiB of HBM per device.

v0:
```python
import jax
import jax.numpy as jnp
from jax import lax
from jax.sharding import PartitionSpec as P

DILATION_BINS = 4096


def passed_along(value, axis, steps):
    count = lax.axis_size(axis)
    leading, last = (max(0, -steps), min(count, count - steps))
    return lax.ppermute(value, axis, [(source, source + steps) for source in range(leading, last)])


def mixing(left, right):
    return jnp.einsum("gbc,cd->gbd", left, right, preferred_element_type=jnp.float32)


def mixing_back(left, right):
    return jnp.einsum("gbd,cd->gbc", left, right, preferred_element_type=jnp.float32)


def outer_sum(left, right):
    return jnp.einsum("gbc,gbd->cd", left, right, preferred_element_type=jnp.float32)


def layer_arithmetic(
    genome, upstream, act, act_prev, act_next, up_prev, up_next, slope_fn, conv_weight
):
    conv = (
        mixing(act_prev, conv_weight[0])
        + mixing(act, conv_weight[1])
        + mixing(act_next, conv_weight[2])
    )
    output = (genome.astype(jnp.float32) + conv).astype(jnp.bfloat16)
    grad_act = (
        mixing_back(up_next, conv_weight[0])
        + mixing_back(upstream, conv_weight[1])
        + mixing_back(up_prev, conv_weight[2])
    )
    grad_genome = (upstream.astype(jnp.float32) + slope_fn(grad_act)[0]).astype(jnp.bfloat16)
    partial_gradient = jnp.stack(
        [outer_sum(act_prev, upstream), outer_sum(act, upstream), outer_sum(act_next, upstream)]
    )
    return (output, grad_genome, partial_gradient)


def per_device(genome, conv_weight, upstream):
    channel_groups, bin_positions, chans = genome.shape
    act_full, slope_fn = jax.vjp(jax.nn.gelu, genome.astype(jnp.float32))
    act = act_full.astype(jnp.bfloat16)
    tap_offset = DILATION_BINS // bin_positions
    act_prev, up_prev = passed_along((act, upstream), "seq", tap_offset)
    act_next, up_next = passed_along((act, upstream), "seq", -tap_offset)
    output, grad_genome, partial_gradient = layer_arithmetic(
        genome, upstream, act, act_prev, act_next, up_prev, up_next, slope_fn, conv_weight
    )
    grad_weight = lax.psum(partial_gradient, ("seq", "dp"))
    return (output, grad_genome, grad_weight)


def solution(mesh):
    return jax.shard_map(
        per_device,
        mesh=mesh,
        in_specs=(P("dp", "seq", None), P(), P("dp", "seq", None)),
        out_specs=(P("dp", "seq", None), P("dp", "seq", None), P()),
        check_vma=False,
    )
```

profile of v0, /device:TPU:1, one launch (start us, length us, event | category | flops | bytes accessed | tf_op | source)
XLA Modules:
  0.0 310.0 jit_solution(10332365631051062214)
XLA Ops:
  7.2 0.0 all-reduce.2.cloned.1.call-start
  7.2 0.0 copy-start.4
  7.2 3.1 %fusion.8 = bf16[1,2048,512]{2,1,0:T(8,128)(2,1)S(1)} fusion(bf16[1,2048,512]{2,1,0:T(8,128)(2,1)} %param.3), kind=kLoop, calls=%fused_computation.14 | loop fusion | flops 10485760 | bytes 4194304 | tf_op jit(solution)/shard_map/convert_element_type | solution.py:51
  10.4 0.0 copy-start.1
  10.4 4.2 %collective-permute-start = (bf16[1,2048,512]{2,1,0:T(8,128)(2,1)S(1)}, bf16[1,2048,512]{2,1,0:T(8,128)(2,1)S(1)}, u32[]{:S(2)}, u32[]{:S(2)}) collective-permute-start(bf16[1,2048,512]{2,1,0:T(8,128)(2,1)S(1)} %fusion.8), channel_id=1, source_target_pairs={{0,4},{2,6},{4,8},{6,10},{8,12},{10,14},{12,16},{14,18},{16,20},{1... | collective-permute-start | bytes 6291464 | tf_op jit(solution)/shard_map/ppermute | solution.py:12
  14.6 1.3 collective-permute-start.1
  15.9 1.3 collective-permute-start.2
  17.2 6.1 %collective-permute-start.3 = (bf16[1,2048,512]{2,1,0:T(8,128)(2,1)}, bf16[1,2048,512]{2,1,0:T(8,128)(2,1)}, u32[]{:S(2)}, u32[]{:S(2)}) collective-permute-start(bf16[1,2048,512]{2,1,0:T(8,128)(2,1)} %param.5), channel_id=1, source_target_pairs={{0,4},{2,6},{4,8},{6,10},{8,12},{10,14},{12,16},{14,18},{16,20},{1... | collective-permute-start | bytes 6291464 | tf_op jit(solution)/shard_map/ppermute | solution.py:12
  23.3 4.8 %fusion.21 = f32[2048,512]{1,0:T(8,128)} fusion(bf16[1,2048,512]{2,1,0:T(8,128)(2,1)} %param.5, bf16[3,512,512]{2,1,0:T(8,128)(2,1)S(1)} %copy-done.4), kind=kOutput, calls=%fused_computation.29 | convolution fusion | flops 1073741824 | bytes 6815744 | tf_op jit(solution)/shard_map/gbd,cd->gbc/dot_general | solution.py:20
  28.1 3.6 %fusion.31 = f32[2048,512]{1,0:T(8,128)} fusion(bf16[3,512,512]{2,1,0:T(8,128)(2,1)S(1)} %copy-done.4, bf16[1,2048,512]{2,1,0:T(8,128)(2,1)S(1)} %copy-done.1), kind=kOutput, calls=%fused_computation.37 | convolution fusion | flops 1084227584 | bytes 6815744 | tf_op jit(solution)/shard_map/gbc,cd->gbd/dot_general | solution.py:16
  31.8 3.5 %fusion.43 = f32[1,512,512]{2,1,0:T(8,128)S(1)} fusion(bf16[1,2048,512]{2,1,0:T(8,128)(2,1)} %param.5, bf16[1,2048,512]{2,1,0:T(8,128)(2,1)S(1)} %copy-done.1), kind=kOutput, calls=%fused_computation.43 | convolution fusion | flops 1084227584 | bytes 5242880 | tf_op jit(solution)/shard_map/gbc,gbd->cd/dot_general | solution.py:24
  35.3 113.3 %collective-permute-done = bf16[1,2048,512]{2,1,0:T(8,128)(2,1)S(1)} collective-permute-done((bf16[1,2048,512]{2,1,0:T(8,128)(2,1)S(1)}, bf16[1,2048,512]{2,1,0:T(8,128)(2,1)S(1)}, u32[]{:S(2)}, u32[]{:S(2)}) %collective-permute-start) | collective-permute-done | bytes 2097184 | tf_op jit(solution)/shard_map/ppermute | solution.py:12
  148.6 1.3 copy-done.3
  150.0 2.9 fusion.38
  152.8 0.0 collective-permute-done.1
  152.8 0.0 copy-start.6
  152.9 1.3 copy-done.6
  154.2 2.9 fusion.48
  157.0 2.0 pad_maximum_fusion
  159.0 0.0 all-reduce.2.cloned.1.call-update
  159.0 0.0 copy-start.5
  159.1 0.0 copy-start.7
  159.1 3.1 %fusion.34 = f32[2048,512]{1,0:T(8,128)S(1)} fusion(bf16[1,2048,512]{2,1,0:T(8,128)(2,1)} %copy-done.3, bf16[3,512,512]{2,1,0:T(8,128)(2,1)} %param.4), kind=kOutput, calls=%fused_computation.40 | convolution fusion | flops 1073741824 | bytes 6815744 | tf_op jit(solution)/shard_map/gbc,cd->gbd/dot_general | solution.py:16
  162.2 0.3 copy-done.5
  162.5 0.7 copy-done.7
  163.2 3.2 %fusion.9 = bf16[1,2048,512]{2,1,0:T(8,128)(2,1)} fusion(bf16[1,2048,512]{2,1,0:T(8,128)(2,1)S(1)} %copy-done.1, f32[2048,512]{1,0:T(8,128)S(1)} %fusion.34, f32[2048,512]{1,0:T(8,128)S(1)} %copy-done.2, bf16[1,2048,512]{2,1,0:T(8,128)(2,1)S(1)} %copy-done.7, bf16[3,512,512]{2,1,0:T(8,128)(2,1)S(1)} %copy-done.5), kind=kOutput, calls=%fused_computation.15 | convolution fusion | flops 1078984704 | bytes 15204352 | tf_op jit(solution)/shard_map/gbc,cd->gbd/dot_general | solution.py:16
  166.3 0.0 collective-permute-done.2
  166.3 3.0 fusion.23
  169.4 30.7 %collective-permute-done.3 = bf16[1,2048,512]{2,1,0:T(8,128)(2,1)} collective-permute-done((bf16[1,2048,512]{2,1,0:T(8,128)(2,1)}, bf16[1,2048,512]{2,1,0:T(8,128)(2,1)}, u32[]{:S(2)}, u32[]{:S(2)}) %collective-permute-start.3) | collective-permute-done | bytes 2097184 | tf_op jit(solution)/shard_map/ppermute | solution.py:12
  200.0 7.0 %fusion.4 = bf16[1,2048,512]{2,1,0:T(8,128)(2,1)} fusion(bf16[1,2048,512]{2,1,0:T(8,128)(2,1)S(1)} %copy-done.1, f32[2048,512]{1,0:T(8,128)S(1)} %fusion.23, f32[2048,512]{1,0:T(8,128)S(1)} %copy-done, bf16[1,2048,512]{2,1,0:T(8,128)(2,1)} %param.5, bf16[1,2048,512]{2,1,0:T(8,128)(2,1)} %collective-permute-done.3, bf16[3,512,512]{2,1,0:T(8,128)(2,1)S(1)} %copy-done.5), kind=kOutput, calls=%fused_computation.10 | convolution fusion | flops 1099956224 | bytes 17301504 | tf_op jit(solution)/shard_map/gbd,cd->gbc/dot_general | solution.py:20
  207.1 92.3 %all-reduce.2.cloned.1.call-done = f32[3,512,512]{2,1,0:T(8,128)} async-done(((f32[3,512,512]{2,1,0:T(8,128)}), f32[3,512,512]{2,1,0:T(8,128)}) %all-reduce.2.cloned.1.call-update) | async-done | bytes 3145744 | tf_op jit(solution)/shard_map/psum | solution.py:58
  299.3 3.9 %copy.7 = f32[3,512,512]{2,1,0:T(8,128)} copy(f32[3,512,512]{2,1,0:T(8,128)} %all-reduce.2.cloned.1.call-done) | data formatting | bytes 6291456
  (7 shorter events, 0.0 us)
Async XLA Ops:
  7.2 292.2 %all-reduce.2.cloned.1.call-start = ((), (), s32[]{:S(2)}) async-start(), calls=%async_computation | async-start | bytes 6291456 | tf_op jit(solution)/shard_map/psum | solution.py:58
  7.2 16.1 %copy-start.4 = (bf16[3,512,512]{2,1,0:T(8,128)(2,1)S(1)}, bf16[3,512,512]{2,1,0:T(8,128)(2,1)}, u32[]{:S(2)}) copy-start(bf16[3,512,512]{2,1,0:T(8,128)(2,1)} %param.4) | copy-start | bytes 4718596
  10.4 17.8 %copy-start.1 = (bf16[1,2048,512]{2,1,0:T(8,128)(2,1)S(1)}, bf16[1,2048,512]{2,1,0:T(8,128)(2,1)}, u32[]{:S(2)}) copy-start(bf16[1,2048,512]{2,1,0:T(8,128)(2,1)} %param.3) | copy-start | bytes 6291460
  10.4 138.3 %collective-permute-start = (bf16[1,2048,512]{2,1,0:T(8,128)(2,1)S(1)}, bf16[1,2048,512]{2,1,0:T(8,128)(2,1)S(1)}, u32[]{:S(2)}, u32[]{:S(2)}) collective-permute-start(bf16[1,2048,512]{2,1,0:T(8,128)(2,1)S(1)} %fusion.8), channel_id=1, source_target_pairs={{0,4},{2,6},{4,8},{6,10},{8,12},{10,14},{12,16},{14,18},{16,20},{1... | collective-permute-start | bytes 6291464 | tf_op jit(solution)/shard_map/ppermute | solution.py:12
  14.6 138.2 %collective-permute-start.1 = (bf16[1,2048,512]{2,1,0:T(8,128)(2,1)S(1)}, bf16[1,2048,512]{2,1,0:T(8,128)(2,1)S(1)}, u32[]{:S(2)}, u32[]{:S(2)}) collective-permute-start(bf16[1,2048,512]{2,1,0:T(8,128)(2,1)S(1)} %fusion.8), channel_id=1, source_target_pairs={{4,0},{6,2},{8,4},{10,6},{12,8},{14,10},{16,12},{18,14},{20,16},{2... | collective-permute-start | bytes 6291464 | tf_op jit(solution)/shard_map/ppermute | solution.py:12
  15.9 150.4 %collective-permute-start.2 = (bf16[1,2048,512]{2,1,0:T(8,128)(2,1)}, bf16[1,2048,512]{2,1,0:T(8,128)(2,1)}, u32[]{:S(2)}, u32[]{:S(2)}) collective-permute-start(bf16[1,2048,512]{2,1,0:T(8,128)(2,1)} %param.5), channel_id=1, source_target_pairs={{4,0},{6,2},{8,4},{10,6},{12,8},{14,10},{16,12},{18,14},{20,16},{2... | collective-permute-start | bytes 6291464 | tf_op jit(solution)/shard_map/ppermute | solution.py:12
  17.2 182.8 %collective-permute-start.3 = (bf16[1,2048,512]{2,1,0:T(8,128)(2,1)}, bf16[1,2048,512]{2,1,0:T(8,128)(2,1)}, u32[]{:S(2)}, u32[]{:S(2)}) collective-permute-start(bf16[1,2048,512]{2,1,0:T(8,128)(2,1)} %param.5), channel_id=1, source_target_pairs={{0,4},{2,6},{4,8},{6,10},{8,12},{10,14},{12,16},{14,18},{16,20},{1... | collective-permute-start | bytes 6291464 | tf_op jit(solution)/shard_map/ppermute | solution.py:12
  148.6 1.3 copy-start.3
  152.8 1.3 copy-start.6
  159.0 3.1 %copy-start.2 = (f32[2048,512]{1,0:T(8,128)S(1)}, f32[2048,512]{1,0:T(8,128)}, u32[]{:S(2)}) copy-start(f32[2048,512]{1,0:T(8,128)} %fusion.31) | copy-start | bytes 12582916
  159.0 3.5 %copy-start.5 = (bf16[3,512,512]{2,1,0:T(8,128)(2,1)S(1)}, bf16[3,512,512]{2,1,0:T(8,128)(2,1)}, u32[]{:S(2)}) copy-start(bf16[3,512,512]{2,1,0:T(8,128)(2,1)} %param.4) | copy-start | bytes 4718596
  159.1 4.1 %copy-start.7 = (bf16[1,2048,512]{2,1,0:T(8,128)(2,1)S(1)}, bf16[1,2048,512]{2,1,0:T(8,128)(2,1)}, u32[]{:S(2)}) copy-start(bf16[1,2048,512]{2,1,0:T(8,128)(2,1)} %copy-done.6) | copy-start | bytes 6291460
  166.3 33.7 %copy-start = (f32[2048,512]{1,0:T(8,128)S(1)}, f32[2048,512]{1,0:T(8,128)}, u32[]{:S(2)}) copy-start(f32[2048,512]{1,0:T(8,128)} %fusion.21) | copy-start | bytes 12582916
Sparse Core Ops, SparseCore 0:
  159.2 140.1 all-reduce.1
where the time goes:
time: 313 us; the launch traced here: 310 us
  waiting for transfers between devices  236 us (75%)
  matrix products  34.1 us (11%)
  between operations  14.1 us (5%)
  starting transfers between devices  12.9 us (4%)
  local copies, waits for them, and re-layouts  7.49 us (2%)
  other arithmetic  5.11 us (2%)
    ppermute x4, waiting for transfers between devices, passed_along(): lax.ppermute(value, axis, [(source, source + steps) for source in range(l...  144 us
    psum x1, waiting for transfers between devices, per_device(): grad_weight = lax.psum(partial_gradient, ('seq', 'dp'))  92.3 us
    dot_general x3, matrix products, mixing_back(): jnp.einsum('gbd,cd->gbc', left, right, preferred_element_type=jnp.float32)  14.9 us
    ppermute x4, starting transfers between devices, passed_along(): lax.ppermute(value, axis, [(source, source + steps) for source in range(l...  12.9 us
    dot_general x3, matrix products, mixing(): jnp.einsum('gbc,cd->gbd', left, right, preferred_element_type=jnp.float32)  9.9 us
    dot_general x3, matrix products, outer_sum(): jnp.einsum('gbc,gbd->cd', left, right, preferred_element_type=jnp.float32)  9.28 us
    unnamed x17, local copies, waits for them, and re-layouts  7.49 us
  transfers between devices with their start and end apart: 5, of which 3 were waited for; matrix products, arithmetic and copies ran while one was open for 12% of the time, Pallas kernels for 0%

commit v1 on v0

v1 whole, which is shorter than its diff:
```python
import jax
import jax.numpy as jnp
from jax import lax
from jax.sharding import PartitionSpec as P

DILATION_BINS = 4096
BF16, F32 = jnp.bfloat16, jnp.float32


def rows_of(value, start, size, dim=0):
    return lax.dynamic_slice_in_dim(value, start, size, dim)


def mixing(left, right):
    return jnp.einsum("bc,cd->bd", left, right, preferred_element_type=F32)


def mixing_back(left, right):
    return jnp.einsum("bd,cd->bc", left, right, preferred_element_type=F32)


def outer_sum(left, right):
    return jnp.einsum("bc,bd->cd", left, right, preferred_element_type=F32)


class Group:
    def __init__(self, axis, position, count, pairs_of_shift):
        self.axis, self.position, self.count, self.pairs = axis, position, count, pairs_of_shift

    def scatter_sum(self, value):
        size = value.shape[1] // self.count
        total = rows_of(value, self.position * size, size, 1)
        for shift in range(1, self.count):
            there = lax.rem(self.position + shift, self.count)
            total = total + lax.ppermute(rows_of(value, there * size, size, 1), self.axis, self.pairs(shift))
        return total

    def gather(self, value):
        size = value.shape[1]
        whole = jnp.zeros((value.shape[0], size * self.count, value.shape[2]), value.dtype)
        whole = lax.dynamic_update_slice_in_dim(whole, value, self.position * size, 1)
        for shift in range(1, self.count):
            source = lax.rem(self.position + self.count - shift, self.count)
            part = lax.ppermute(value, self.axis, self.pairs(shift))
            whole = lax.dynamic_update_slice_in_dim(whole, part, source * size, 1)
        return whole


def per_device(genome, conv_weight, upstream):
    genome, upstream = genome[0], upstream[0]
    bins, chans = genome.shape
    half, cols = bins // 2, chans // 2
    count = lax.axis_size("seq")
    index = lax.axis_index("seq")
    tap = DILATION_BINS // bins
    side = lax.rem(index // tap, 2)
    is_even = side == 0
    own_start, oth_start = side * half, (1 - side) * half

    def even(i):
        return (i // tap) % 2 == 0

    swap_pairs = [(i, i + tap if even(i) else i - tap) for i in range(count)]
    outer_pairs = [(i, i - 2 * tap if even(i) else i + 2 * tap) for i in range(count)]
    outer_pairs = [(i, j) for i, j in outer_pairs if 0 <= j < count]
    inner_pairs = [(j, i) for i, j in outer_pairs]

    def swap(value):
        return lax.ppermute(value, "seq", swap_pairs)

    def outward(value):
        return lax.ppermute(value, "seq", outer_pairs)

    def inward(value):
        return lax.ppermute(value, "seq", inner_pairs)

    w_mid = conv_weight[1]
    w_far = jnp.where(is_even, conv_weight[0], conv_weight[2])
    w_near = jnp.where(is_even, conv_weight[2], conv_weight[0])

    step = half // 2
    u_own = rows_of(upstream, own_start, half)
    u_parts = [swap(rows_of(upstream, oth_start + k * step, step)) for k in range(2)]
    x_parts = [swap(rows_of(genome, oth_start, half)[:, k * cols : (k + 1) * cols]) for k in range(2)]
    x_own = rows_of(genome, own_start, half)
    u_oth_far = outward(u_own)
    act, slope_own = jax.vjp(jax.nn.gelu, x_own.astype(F32))
    a_own = act.astype(BF16)
    a_oth_far = outward(a_own)
    u_own_far = jnp.concatenate([inward(part) for part in u_parts], 0)
    u_oth = jnp.concatenate(u_parts, 0)

    dp_index, dp_count = lax.axis_index("dp"), lax.axis_size("dp")
    core = Group("seq", lax.rem(index, tap), tap, lambda s: [(i, i - i % tap + (i % tap + s) % tap) for i in range(count)])
    other = Group("dp", dp_index, dp_count, lambda s: [(i, (i + s) % dp_count) for i in range(dp_count)])
    span = 2 * tap
    along = Group("seq", index // span, count // span, lambda s: [(i, (i + s * span) % count) for i in range(count)])

    own_act = jax.nn.gelu(genome.astype(F32)).astype(BF16)
    mid = outer_sum(own_act, upstream).reshape(2, cols, chans)
    mid = other.scatter_sum(core.scatter_sum(mid))

    def outer_parts(k):
        a_k = a_own[:, k * cols : (k + 1) * cols]
        x_k, slope = jax.vjp(jax.nn.gelu, x_parts[k].astype(F32))
        b_k = x_k.astype(BF16)
        far = outer_sum(a_k, u_oth) + outer_sum(b_k, u_oth_far)
        near = outer_sum(b_k, u_own) + outer_sum(a_k, u_own_far)
        return b_k, slope, jnp.stack([far, near])

    def finish(parts, taps):
        total = along.scatter_sum(parts)
        side_sum = total[-2:]
        side_sum = jnp.where(is_even, side_sum, side_sum[::-1])
        total = jnp.concatenate([total[:-2], side_sum], 0)
        total = total + swap(total)
        return core.gather(other.gather(along.gather(total.astype(BF16))))

    a_parts, gg_back, sums = [], [], []
    for k in range(2):
        b_k, slope, outer = outer_parts(k)
        a_parts.append(b_k)
        span_k = slice(k * cols, (k + 1) * cols)
        grad_act = (
            mixing_back(u_own, w_near[span_k])
            + mixing_back(u_oth, w_mid[span_k])
            + mixing_back(u_oth_far, w_far[span_k])
        )
        gg = (u_oth[:, span_k].astype(F32) + slope(grad_act)[0]).astype(BF16)
        gg_back.append(swap(gg))
        outer = other.scatter_sum(core.scatter_sum(outer))
        sums.append(finish(jnp.concatenate([mid, outer], 0) if k == 0 else outer, None))
    a_own_far = jnp.concatenate([inward(part) for part in a_parts], 1)
    a_oth = jnp.concatenate(a_parts, 1)
    x_oth = jnp.concatenate(x_parts, 1)

    out_back = []
    for k in range(2):
        r = slice(k * step, (k + 1) * step)
        conv = mixing(a_own[r], w_far) + mixing(a_oth[r], w_mid) + mixing(a_oth_far[r], w_near)
        out_back.append(swap((x_oth[r].astype(F32) + conv).astype(BF16)))

    grad_act = mixing_back(u_oth, w_far) + mixing_back(u_own, w_mid) + mixing_back(u_own_far, w_near)
    gg_own = (u_own.astype(F32) + slope_own(grad_act)[0]).astype(BF16)
    conv = mixing(a_oth, w_near) + mixing(a_own, w_mid) + mixing(a_own_far, w_far)
    out_own = (x_own.astype(F32) + conv).astype(BF16)

    def placed(own, back):
        return jnp.where(is_even, jnp.concatenate([own, back], 0), jnp.concatenate([back, own], 0))[None]

    output = placed(out_own, jnp.concatenate(out_back, 0))
    grad_genome = placed(gg_own, jnp.concatenate(gg_back, 1))
    first, second = sums
    grad_weight = jnp.stack(
        [
            jnp.concatenate([first[2], second[0]], 0),
            jnp.concatenate([first[0], first[1]], 0),
            jnp.concatenate([first[3], second[1]], 0),
        ]
    ).astype(F32)
    return (output, grad_genome, grad_weight)


def solution(mesh):
    return jax.shard_map(
        per_device,
        mesh=mesh,
        in_specs=(P("dp", "seq", None), P(), P("dp", "seq", None)),
        out_specs=(P("dp", "seq", None), P("dp", "seq", None), P()),
        check_vma=False,
    )
```

time: 313 us -> 219 us (0.70)
  waiting for transfers between devices: 236 us -> 83.4 us
  starting transfers between devices: 12.9 us -> 66.1 us
  between operations: 14.1 us -> 1.46 us
  other arithmetic: 5.11 us -> 15.2 us
  local copies, waits for them, and re-layouts: 7.49 us -> 15.3 us
    psum x1 -> x0, waiting for transfers between devices: 92.3 us -> none  [per_device(): grad_weight = lax.psum(partial_gradient, ('seq', 'dp'))]
    ppermute x4 -> x38, waiting for transfers between devices: 144 us -> 83.4 us  [the longest x10 48.7 us: swap(): return lax.ppermute(value, 'seq', swap_pairs)]
    ppermute x4 -> x38, starting transfers between devices: 12.9 us -> 66.1 us  [the longest x10 22.3 us: gather(): part = lax.ppermute(value, self.axis, self.pairs(shift))]
    dynamic_slice x0 -> x8, local copies, waits for them, and re-layouts: none -> 5.84 us  [rows_of(): return lax.dynamic_slice_in_dim(value, start, size, dim)]
    select_n x0 -> x5, other arithmetic: none -> 4.91 us  [the longest x2 3.62 us: placed(): jnp.where(is_even, jnp.concatenate([own, back], 0), jnp.concatenate([back...]
    dot_general x0 -> x1, local copies, waits for them, and re-layouts: none -> 4.06 us  [outer_sum(): return jnp.einsum('bc,bd->cd', left, right, preferred_element_type=F32)]
    unnamed x17 -> x29, local copies, waits for them, and re-layouts: 7.49 us -> 3.71 us
    dot_general x9 -> x27, matrix products: 34.1 us -> 36.2 us  [the longest x9 13.8 us: mixing_back(): return jnp.einsum('bd,cd->bc', left, right, preferred_element_type=F32)]
  transfers between devices with their start and end apart: 5 -> 38, of which waited for: 3 -> 12; matrix products, arithmetic and copies ran while one was open for 12% -> 28% of each run, Pallas kernels for 0% -> 0%
where the time goes in v1:
time: 219 us; the launch traced here: 218 us
  waiting for transfers between devices  83.4 us (38%)
  starting transfers between devices  66.1 us (30%)
  matrix products  36.2 us (17%)
  local copies, waits for them, and re-layouts  15.3 us (7%)
  other arithmetic  15.2 us (7%)
    ppermute x10, waiting for transfers between devices, swap(): return lax.ppermute(value, 'seq', swap_pairs)  48.7 us
    ppermute x10, starting transfers between devices, gather(): part = lax.ppermute(value, self.axis, self.pairs(shift))  22.3 us
    ppermute x4, waiting for transfers between devices, inward(): return lax.ppermute(value, 'seq', inner_pairs)  20.6 us
    ppermute x10, starting transfers between devices, swap(): return lax.ppermute(value, 'seq', swap_pairs)  15.4 us
    ppermute x12, starting transfers between devices, scatter_sum(): lax.ppermute(rows_of(value, there * size, size, 1), self.axis, self.pairs...  15 us
    dot_general x9, matrix products, mixing_back(): return jnp.einsum('bd,cd->bc', left, right, preferred_element_type=F32)  13.8 us
    dot_general x9, matrix products, outer_sum(): return jnp.einsum('bc,bd->cd', left, right, preferred_element_type=F32)  12 us
    ppermute x4, starting transfers between devices, inward(): return lax.ppermute(value, 'seq', inner_pairs)  10.8 us
  transfers between devices with their start and end apart: 38, of which 12 were waited for; matrix products, arithmetic and copies ran while one was open for 28% of the time, Pallas kernels for 0%

profile of v1, /device:TPU:1, one launch (start us, length us, event | category | flops | bytes accessed | tf_op | source)
XLA Modules:
  0.0 217.8 jit_solution(14178942931660958862)
XLA Ops:
  0.7 2.5 %dynamic-slice_bitcast_fusion.2 = (bf16[512,512]{1,0:T(8,128)(2,1)}, bf16[512,512]{1,0:T(8,128)(2,1)}) fusion(bf16[1,2048,512]{2,1,0:T(8,128)(2,1)} %param.5, s32[]{:T(128)S(6)} %select_n.138, s32[]{:T(128)S(6)} %select_n.131), kind=kLoop, calls=%fused_computation.164 | loop fusion | bytes 2097160 | tf_op jit(solution)/shard_map/dynamic_slice | solution.py:11
  3.2 2.1 collective-permute-start.7
  8.9 2.7 %fusion.30 = bf16[512,2048]{0,1:T(8,128)(2,1)} fusion(bf16[1,2048,512]{2,1,0:T(8,128)(2,1)S(1)} %copy-done), kind=kLoop, calls=%fused_computation.39 | loop fusion | flops 10485760 | bytes 4194304 | tf_op jit(solution)/shard_map/bc,bd->cd/dot_general | solution.py:23
  11.7 4.1 %copy.7 = bf16[512,2048]{1,0:T(8,128)(2,1)} copy(bf16[512,2048]{0,1:T(8,128)(2,1)} %fusion.30) | data formatting | bytes 4194304 | tf_op jit(solution)/shard_map/bc,bd->cd/dot_general | solution.py:23
  15.7 3.8 %fusion.31 = f32[2,256,512]{2,1,0:T(8,128)} fusion(bf16[2,256,2048]{2,1,0:T(8,128)(2,1)} %bitcast.174, bf16[1,2048,512]{2,1,0:T(8,128)(2,1)S(1)} %copy-done.10), kind=kOutput, calls=%fused_computation.42 | convolution fusion | flops 1073741824 | bytes 5242880 | tf_op jit(solution)/shard_map/bc,bd->cd/dot_general | solution.py:23
  29.9 2.1 fusion.98
  31.9 2.2 %fusion.63 = f32[1024,512]{1,0:T(8,128)} fusion(bf16[1,2048,512]{2,1,0:T(8,128)(2,1)S(1)} %copy-done.1, s32[]{:T(128)S(6)} %select_n.130, bf16[3,512,512]{2,1,0:T(8,128)(2,1)S(1)} %copy-done.3), kind=kOutput, calls=%fused_computation.110 | convolution fusion | flops 542113792 | bytes 3670020 | tf_op jit(solution)/shard_map/bc,cd->bd/dot_general | solution.py:15
  37.0 6.8 %collective-permute-start.8 = (bf16[512,512]{1,0:T(8,128)(2,1)}, bf16[512,512]{1,0:T(8,128)(2,1)S(1)}, u32[]{:S(2)}, u32[]{:S(2)}) collective-permute-start(bf16[512,512]{1,0:T(8,128)(2,1)} %get-tuple-element.7), channel_id=1, source_target_pairs={{0,4},{2,6},{4,0},{6,2},{8,12},{10,14},{12,8},{14,10},{16,20},{18,... | collective-permute-start | bytes 1572872 | tf_op jit(solution)/shard_map/ppermute | solution.py:69
  49.2 7.0 %collective-permute-done.8 = bf16[512,512]{1,0:T(8,128)(2,1)S(1)} collective-permute-done((bf16[512,512]{1,0:T(8,128)(2,1)}, bf16[512,512]{1,0:T(8,128)(2,1)S(1)}, u32[]{:S(2)}, u32[]{:S(2)}) %collective-permute-start.8) | collective-permute-done | bytes 524320 | tf_op jit(solution)/shard_map/ppermute | solution.py:69
  56.2 2.2 %collective-permute-start.2 = (bf16[1024,256]{1,0:T(8,128)(2,1)S(1)}, bf16[1024,256]{1,0:T(8,128)(2,1)S(1)}, u32[]{:S(2)}, u32[]{:S(2)}) collective-permute-start(bf16[1024,256]{1,0:T(8,128)(2,1)S(1)} %fusion.53), channel_id=1, source_target_pairs={{12,4},{14,6},{0,8},{2,10},{20,12},{22,14},{8,16},{10,18},{28,20},... | collective-permute-start | bytes 1572872 | tf_op jit(solution)/shard_map/ppermute | solution.py:75
  60.2 7.1 %collective-permute-done.1 = bf16[1024,256]{1,0:T(8,128)(2,1)S(1)} collective-permute-done((bf16[1024,256]{1,0:T(8,128)(2,1)S(1)}, bf16[1024,256]{1,0:T(8,128)(2,1)S(1)}, u32[]{:S(2)}, u32[]{:S(2)}) %collective-permute-start.1) | collective-permute-done | bytes 524320 | tf_op jit(solution)/shard_map/ppermute | solution.py:69
  70.6 2.2 %collective-permute-start.9 = (bf16[512,512]{1,0:T(8,128)(2,1)}, bf16[512,512]{1,0:T(8,128)(2,1)S(1)}, u32[]{:S(2)}, u32[]{:S(2)}) collective-permute-start(bf16[512,512]{1,0:T(8,128)(2,1)} %collective-permute-done.7), channel_id=1, source_target_pairs={{12,4},{14,6},{0,8},{2,10},{20,12},{22,14},{8,16},{10,18},{28,20},... | collective-permute-start | bytes 1572872 | tf_op jit(solution)/shard_map/ppermute | solution.py:75
  76.4 2.1 collective-permute-start.3
  78.6 5.0 %collective-permute-done.9 = bf16[512,512]{1,0:T(8,128)(2,1)S(1)} collective-permute-done((bf16[512,512]{1,0:T(8,128)(2,1)}, bf16[512,512]{1,0:T(8,128)(2,1)S(1)}, u32[]{:S(2)}, u32[]{:S(2)}) %collective-permute-start.9) | collective-permute-done | bytes 524320 | tf_op jit(solution)/shard_map/ppermute | solution.py:75
  83.6 4.2 %collective-permute-start.10 = (bf16[512,512]{1,0:T(8,128)(2,1)S(1)}, bf16[512,512]{1,0:T(8,128)(2,1)S(1)}, u32[]{:S(2)}, u32[]{:S(2)}) collective-permute-start(bf16[512,512]{1,0:T(8,128)(2,1)S(1)} %collective-permute-done.8), channel_id=1, source_target_pairs={{12,4},{14,6},{0,8},{2,10},{20,12},{22,14},{8,16},{10,18},{28,20},... | collective-permute-start | bytes 1572872 | tf_op jit(solution)/shard_map/ppermute | solution.py:75
  87.9 2.0 fusion.143
  90.4 15.6 %collective-permute-done.10 = bf16[512,512]{1,0:T(8,128)(2,1)S(1)} collective-permute-done((bf16[512,512]{1,0:T(8,128)(2,1)S(1)}, bf16[512,512]{1,0:T(8,128)(2,1)S(1)}, u32[]{:S(2)}, u32[]{:S(2)}) %collective-permute-start.10) | collective-permute-done | bytes 524320 | tf_op jit(solution)/shard_map/ppermute | solution.py:75
  111.2 2.5 %fusion.49 = bf16[1024,256]{1,0:T(8,128)(2,1)S(1)} fusion(bf16[1024,256]{1,0:T(8,128)(2,1)} %collective-permute-done, bf16[1024,512]{1,0:T(8,128)(2,1)S(1)} %constant_dynamic-update-slice_fusion.2, f32[1024,256]{1,0:T(8,128)S(1)} %convolution_add_fusion.7, bf16[1024,512]{1,0:T(8,128)(2,1)} %collective-permute-done.11, ...), kind=kOutput, calls=%fused_computation.96 | convolution fusion | flops 274726912 | bytes 3932160 | tf_op jit(solution)/shard_map/bd,cd->bc/dot_general | solution.py:19
  113.8 2.2 fusion.36
  116.0 3.1 %collective-permute-start.12 = (bf16[1024,256]{1,0:T(8,128)(2,1)S(1)}, bf16[1024,256]{1,0:T(8,128)(2,1)S(1)}, u32[]{:S(2)}, u32[]{:S(2)}) collective-permute-start(bf16[1024,256]{1,0:T(8,128)(2,1)S(1)} %fusion.49), channel_id=1, source_target_pairs={{0,4},{2,6},{4,0},{6,2},{8,12},{10,14},{12,8},{14,10},{16,20},{18,... | collective-permute-start | bytes 1572872 | tf_op jit(solution)/shard_map/ppermute | solution.py:69
  120.6 2.4 %fusion.45 = bf16[1024,256]{1,0:T(8,128)(2,1)S(1)} fusion(bf16[1024,256]{1,0:T(8,128)(2,1)S(1)} %collective-permute-done.1, bf16[1024,512]{1,0:T(8,128)(2,1)S(1)} %constant_dynamic-update-slice_fusion.2, f32[1024,256]{1,0:T(8,128)S(1)} %convolution_add_fusion.5, bf16[1024,512]{1,0:T(8,128)(2,1)} %collective-permute-done.11, ...), kind=kOutput, calls=%fused_computation.92 | convolution fusion | flops 274726912 | bytes 3932160 | tf_op jit(solution)/shard_map/bd,cd->bc/dot_general | solution.py:19
  128.7 24.6 %collective-permute-done.5 = bf16[512,512]{1,0:T(8,128)(2,1)S(1)} collective-permute-done((bf16[512,512]{1,0:T(8,128)(2,1)S(1)}, bf16[512,512]{1,0:T(8,128)(2,1)S(1)}, u32[]{:S(2)}, u32[]{:S(2)}) %collective-permute-start.5) | collective-permute-done | bytes 524320 | tf_op jit(solution)/shard_map/ppermute | solution.py:69
  154.5 10.0 %collective-permute-done.6 = bf16[512,512]{1,0:T(8,128)(2,1)S(1)} collective-permute-done((bf16[512,512]{1,0:T(8,128)(2,1)S(1)}, bf16[512,512]{1,0:T(8,128)(2,1)S(1)}, u32[]{:S(2)}, u32[]{:S(2)}) %collective-permute-start.6) | collective-permute-done | bytes 524320 | tf_op jit(solution)/shard_map/ppermute | solution.py:69
  166.3 2.0 maximum_select_fusion.1
  175.4 3.0 %collective-permute-start.18 = (f32[4,16,512]{2,1,0:T(8,128)S(1)}, f32[4,16,512]{2,1,0:T(8,128)S(1)}, u32[]{:S(2)}, u32[]{:S(2)}) collective-permute-start(f32[4,16,512]{2,1,0:T(8,128)S(1)} %get-tuple-element.19), channel_id=1, source_target_pairs={{0,8},{2,10},{4,12},{6,14},{8,16},{10,18},{12,20},{14,22},{16,24},... | collective-permute-start | bytes 393224 | tf_op jit(solution)/shard_map/ppermute | solution.py:35
  183.9 2.8 %collective-permute-done.19 = f32[4,16,512]{2,1,0:T(8,128)S(1)} collective-permute-done((f32[4,16,512]{2,1,0:T(8,128)S(1)}, f32[4,16,512]{2,1,0:T(8,128)S(1)}, u32[]{:S(2)}, u32[]{:S(2)}) %collective-permute-start.19) | collective-permute-done | bytes 131104 | tf_op jit(solution)/shard_map/ppermute | solution.py:35
  187.2 4.9 %collective-permute-done.34 = bf16[2,16,512]{2,1,0:T(8,128)(2,1)S(1)} collective-permute-done((bf16[2,16,512]{2,1,0:T(8,128)(2,1)S(1)}, bf16[2,16,512]{2,1,0:T(8,128)(2,1)S(1)}, u32[]{:S(2)}, u32[]{:S(2)}) %collective-permute-start.34) | collective-permute-done | bytes 32800 | tf_op jit(solution)/shard_map/ppermute | solution.py:44
  192.2 3.9 %collective-permute-start.22 = (bf16[4,16,512]{2,1,0:T(8,128)(2,1)S(1)}, bf16[4,16,512]{2,1,0:T(8,128)(2,1)S(1)}, u32[]{:S(2)}, u32[]{:S(2)}) collective-permute-start(bf16[4,16,512]{2,1,0:T(8,128)(2,1)S(1)} %get-tuple-element.4), channel_id=1, source_target_pairs={{0,8},{2,10},{4,12},{6,14},{8,16},{10,18},{12,20},{14,22},{16,24},... | collective-permute-start | bytes 196616 | tf_op jit(solution)/shard_map/ppermute | solution.py:44
  197.4 2.1 collective-permute-start.24
  199.5 2.6 %collective-permute-done.23 = bf16[4,16,512]{2,1,0:T(8,128)(2,1)S(1)} collective-permute-done((bf16[4,16,512]{2,1,0:T(8,128)(2,1)S(1)}, bf16[4,16,512]{2,1,0:T(8,128)(2,1)S(1)}, u32[]{:S(2)}, u32[]{:S(2)}) %collective-permute-start.23) | collective-permute-done | bytes 65568 | tf_op jit(solution)/shard_map/ppermute | solution.py:44
  202.4 5.9 %collective-permute-start.37 = (bf16[2,128,512]{2,1,0:T(8,128)(2,1)S(1)}, bf16[2,128,512]{2,1,0:T(8,128)(2,1)S(1)}, u32[]{:S(2)}, u32[]{:S(2)}) collective-permute-start(bf16[2,128,512]{2,1,0:T(8,128)(2,1)S(1)} %constant_dynamic-update-slice_fusion.8), channel_id=1, source_target_pairs={{0,2},{2,0},{4,6},{6,4},{8,10},{10,8},{12,14},{14,12},{16,18},{18,... | collective-permute-start | bytes 786440 | tf_op jit(solution)/shard_map/ppermute | solution.py:44
  208.4 5.7 %collective-permute-start.26 = (bf16[4,128,512]{2,1,0:T(8,128)(2,1)S(1)}, bf16[4,128,512]{2,1,0:T(8,128)(2,1)S(1)}, u32[]{:S(2)}, u32[]{:S(2)}) collective-permute-start(bf16[4,128,512]{2,1,0:T(8,128)(2,1)S(1)} %constant_dynamic-update-slice_fusion.16), channel_id=1, source_target_pairs={{0,2},{2,0},{4,6},{6,4},{8,10},{10,8},{12,14},{14,12},{16,18},{18,... | collective-permute-start | bytes 1572872 | tf_op jit(solution)/shard_map/ppermute | solution.py:44
  (163 shorter events, 64.7 us)
Async XLA Ops:
  3.2 42.0 %collective-permute-start.7 = (bf16[512,512]{1,0:T(8,128)(2,1)}, bf16[512,512]{1,0:T(8,128)(2,1)}, u32[]{:S(2)}, u32[]{:S(2)}) collective-permute-start(bf16[512,512]{1,0:T(8,128)(2,1)} %get-tuple-element.8), channel_id=1, source_target_pairs={{0,4},{2,6},{4,0},{6,2},{8,12},{10,14},{12,8},{14,10},{16,20},{18,... | collective-permute-start | bytes 1572872 | tf_op jit(solution)/shard_map/ppermute | solution.py:69
  6.3 40.2 %collective-permute-start = (bf16[1024,256]{1,0:T(8,128)(2,1)}, bf16[1024,256]{1,0:T(8,128)(2,1)}, u32[]{:S(2)}, u32[]{:S(2)}) collective-permute-start(bf16[1024,256]{1,0:T(8,128)(2,1)} %get-tuple-element.16), channel_id=1, source_target_pairs={{0,4},{2,6},{4,0},{6,2},{8,12},{10,14},{12,8},{14,10},{16,20},{18,... | collective-permute-start | bytes 1572872 | tf_op jit(solution)/shard_map/ppermute | solution.py:69
  7.6 80.2 %collective-permute-start.11 = (bf16[1024,512]{1,0:T(8,128)(2,1)S(1)}, bf16[1024,512]{1,0:T(8,128)(2,1)}, u32[]{:S(2)}, u32[]{:S(2)}) collective-permute-start(bf16[1024,512]{1,0:T(8,128)(2,1)S(1)} %dynamic-slice_bitcast_fusion), channel_id=1, source_target_pairs={{4,12},{6,14},{8,0},{10,2},{12,20},{14,22},{16,8},{18,10},{20,28},... | collective-permute-start | bytes 3145736 | tf_op jit(solution)/shard_map/ppermute | solution.py:72
  21.5 15.5 %collective-permute-start.14 = (f32[2,128,512]{2,1,0:T(8,128)}, f32[2,128,512]{2,1,0:T(8,128)}, u32[]{:S(2)}, u32[]{:S(2)}) collective-permute-start(f32[2,128,512]{2,1,0:T(8,128)} %constant_dynamic-slice_fusion.6), channel_id=1, source_target_pairs={{0,2},{2,0},{4,6},{6,4},{8,10},{10,8},{12,14},{14,12},{16,18},{18,... | collective-permute-start | bytes 1572872 | tf_op jit(solution)/shard_map/ppermute | solution.py:35
  24.4 91.6 %collective-permute-start.4 = (bf16[1024,512]{1,0:T(8,128)(2,1)S(1)}, bf16[1024,512]{1,0:T(8,128)(2,1)}, u32[]{:S(2)}, u32[]{:S(2)}) collective-permute-start(bf16[1024,512]{1,0:T(8,128)(2,1)S(1)} %fusion.21), channel_id=1, source_target_pairs={{4,12},{6,14},{8,0},{10,2},{12,20},{14,22},{16,8},{18,10},{20,28},... | collective-permute-start | bytes 3145736 | tf_op jit(solution)/shard_map/ppermute | solution.py:72
  37.0 19.2 %collective-permute-start.8 = (bf16[512,512]{1,0:T(8,128)(2,1)}, bf16[512,512]{1,0:T(8,128)(2,1)S(1)}, u32[]{:S(2)}, u32[]{:S(2)}) collective-permute-start(bf16[512,512]{1,0:T(8,128)(2,1)} %get-tuple-element.7), channel_id=1, source_target_pairs={{0,4},{2,6},{4,0},{6,2},{8,12},{10,14},{12,8},{14,10},{16,20},{18,... | collective-permute-start | bytes 1572872 | tf_op jit(solution)/shard_map/ppermute | solution.py:69
  45.2 22.2 %collective-permute-start.1 = (bf16[1024,256]{1,0:T(8,128)(2,1)S(1)}, bf16[1024,256]{1,0:T(8,128)(2,1)S(1)}, u32[]{:S(2)}, u32[]{:S(2)}) collective-permute-start(bf16[1024,256]{1,0:T(8,128)(2,1)S(1)} %copy-done.12), channel_id=1, source_target_pairs={{0,4},{2,6},{4,0},{6,2},{8,12},{10,14},{12,8},{14,10},{16,20},{18,... | collective-permute-start | bytes 1572872 | tf_op jit(solution)/shard_map/ppermute | solution.py:69
  46.5 29.8 %collective-permute-start.15 = (f32[2,64,512]{2,1,0:T(8,128)S(1)}, f32[2,64,512]{2,1,0:T(8,128)S(1)}, u32[]{:S(2)}, u32[]{:S(2)}) collective-permute-start(f32[2,64,512]{2,1,0:T(8,128)S(1)} %constant_dynamic-slice_fusion.5), channel_id=1, source_target_pairs={{0,1},{1,0},{2,3},{3,2},{4,5},{5,4},{6,7},{7,6},{8,9},{9,8},{10,11... | collective-permute-start | bytes 786440 | tf_op jit(solution)/shard_map/ppermute | solution.py:35
  56.2 66.8 %collective-permute-start.2 = (bf16[1024,256]{1,0:T(8,128)(2,1)S(1)}, bf16[1024,256]{1,0:T(8,128)(2,1)S(1)}, u32[]{:S(2)}, u32[]{:S(2)}) collective-permute-start(bf16[1024,256]{1,0:T(8,128)(2,1)S(1)} %fusion.53), channel_id=1, source_target_pairs={{12,4},{14,6},{0,8},{2,10},{20,12},{22,14},{8,16},{10,18},{28,20},... | collective-permute-start | bytes 1572872 | tf_op jit(solution)/shard_map/ppermute | solution.py:75
  70.6 13.0 %collective-permute-start.9 = (bf16[512,512]{1,0:T(8,128)(2,1)}, bf16[512,512]{1,0:T(8,128)(2,1)S(1)}, u32[]{:S(2)}, u32[]{:S(2)}) collective-permute-start(bf16[512,512]{1,0:T(8,128)(2,1)} %collective-permute-done.7), channel_id=1, source_target_pairs={{12,4},{14,6},{0,8},{2,10},{20,12},{22,14},{8,16},{10,18},{28,20},... | collective-permute-start | bytes 1572872 | tf_op jit(solution)/shard_map/ppermute | solution.py:75
  76.4 46.8 %collective-permute-start.3 = (bf16[1024,256]{1,0:T(8,128)(2,1)S(1)}, bf16[1024,256]{1,0:T(8,128)(2,1)S(1)}, u32[]{:S(2)}, u32[]{:S(2)}) collective-permute-start(bf16[1024,256]{1,0:T(8,128)(2,1)S(1)} %fusion.59), channel_id=1, source_target_pairs={{12,4},{14,6},{0,8},{2,10},{20,12},{22,14},{8,16},{10,18},{28,20},... | collective-permute-start | bytes 1572872 | tf_op jit(solution)/shard_map/ppermute | solution.py:75
  83.6 22.4 %collective-permute-start.10 = (bf16[512,512]{1,0:T(8,128)(2,1)S(1)}, bf16[512,512]{1,0:T(8,128)(2,1)S(1)}, u32[]{:S(2)}, u32[]{:S(2)}) collective-permute-start(bf16[512,512]{1,0:T(8,128)(2,1)S(1)} %collective-permute-done.8), channel_id=1, source_target_pairs={{12,4},{14,6},{0,8},{2,10},{20,12},{22,14},{8,16},{10,18},{28,20},... | collective-permute-start | bytes 1572872 | tf_op jit(solution)/shard_map/ppermute | solution.py:75
  106.5 20.5 %collective-permute-start.16 = (f32[2,128,512]{2,1,0:T(8,128)S(1)}, f32[2,128,512]{2,1,0:T(8,128)S(1)}, u32[]{:S(2)}, u32[]{:S(2)}) collective-permute-start(f32[2,128,512]{2,1,0:T(8,128)S(1)} %fusion.76), channel_id=1, source_target_pairs={{0,2},{2,0},{4,6},{6,4},{8,10},{10,8},{12,14},{14,12},{16,18},{18,... | collective-permute-start | bytes 1572872 | tf_op jit(solution)/shard_map/ppermute | solution.py:35
  111.2 16.2 %collective-permute-start.27 = (f32[2,128,512]{2,1,0:T(8,128)S(1)}, f32[2,128,512]{2,1,0:T(8,128)S(1)}, u32[]{:S(2)}, u32[]{:S(2)}) collective-permute-start(f32[2,128,512]{2,1,0:T(8,128)S(1)} %fusion.73), channel_id=1, source_target_pairs={{0,2},{2,0},{4,6},{6,4},{8,10},{10,8},{12,14},{14,12},{16,18},{18,... | collective-permute-start | bytes 1572872 | tf_op jit(solution)/shard_map/ppermute | solution.py:35
  116.0 50.2 %collective-permute-start.12 = (bf16[1024,256]{1,0:T(8,128)(2,1)S(1)}, bf16[1024,256]{1,0:T(8,128)(2,1)S(1)}, u32[]{:S(2)}, u32[]{:S(2)}) collective-permute-start(bf16[1024,256]{1,0:T(8,128)(2,1)S(1)} %fusion.49), channel_id=1, source_target_pairs={{0,4},{2,6},{4,0},{6,2},{8,12},{10,14},{12,8},{14,10},{16,20},{18,... | collective-permute-start | bytes 1572872 | tf_op jit(solution)/shard_map/ppermute | solution.py:69
  123.1 43.1 %collective-permute-start.13 = (bf16[1024,256]{1,0:T(8,128)(2,1)S(1)}, bf16[1024,256]{1,0:T(8,128)(2,1)S(1)}, u32[]{:S(2)}, u32[]{:S(2)}) collective-permute-start(bf16[1024,256]{1,0:T(8,128)(2,1)S(1)} %fusion.45), channel_id=1, source_target_pairs={{0,4},{2,6},{4,0},{6,2},{8,12},{10,14},{12,8},{14,10},{16,20},{18,... | collective-permute-start | bytes 1572872 | tf_op jit(solution)/shard_map/ppermute | solution.py:69
  123.1 30.2 %collective-permute-start.5 = (bf16[512,512]{1,0:T(8,128)(2,1)S(1)}, bf16[512,512]{1,0:T(8,128)(2,1)S(1)}, u32[]{:S(2)}, u32[]{:S(2)}) collective-permute-start(bf16[512,512]{1,0:T(8,128)(2,1)S(1)} %add_convert_fusion.1), channel_id=1, source_target_pairs={{0,4},{2,6},{4,0},{6,2},{8,12},{10,14},{12,8},{14,10},{16,20},{18,... | collective-permute-start | bytes 1572872 | tf_op jit(solution)/shard_map/ppermute | solution.py:69
  127.0 37.5 %collective-permute-start.6 = (bf16[512,512]{1,0:T(8,128)(2,1)S(1)}, bf16[512,512]{1,0:T(8,128)(2,1)S(1)}, u32[]{:S(2)}, u32[]{:S(2)}) collective-permute-start(bf16[512,512]{1,0:T(8,128)(2,1)S(1)} %add_convert_fusion), channel_id=1, source_target_pairs={{0,4},{2,6},{4,0},{6,2},{8,12},{10,14},{12,8},{14,10},{16,20},{18,... | collective-permute-start | bytes 1572872 | tf_op jit(solution)/shard_map/ppermute | solution.py:69
  127.3 44.3 %collective-permute-start.17 = (f32[2,64,512]{2,1,0:T(8,128)S(1)}, f32[2,64,512]{2,1,0:T(8,128)S(1)}, u32[]{:S(2)}, u32[]{:S(2)}) collective-permute-start(f32[2,64,512]{2,1,0:T(8,128)S(1)} %constant_dynamic-slice_fusion.4), channel_id=1, source_target_pairs={{0,1},{1,0},{2,3},{3,2},{4,5},{5,4},{6,7},{7,6},{8,9},{9,8},{10,11... | collective-permute-start | bytes 786440 | tf_op jit(solution)/shard_map/ppermute | solution.py:35
  153.3 14.9 %collective-permute-start.28 = (f32[2,64,512]{2,1,0:T(8,128)S(1)}, f32[2,64,512]{2,1,0:T(8,128)S(1)}, u32[]{:S(2)}, u32[]{:S(2)}) collective-permute-start(f32[2,64,512]{2,1,0:T(8,128)S(1)} %constant_dynamic-slice_fusion.3), channel_id=1, source_target_pairs={{0,1},{1,0},{2,3},{3,2},{4,5},{5,4},{6,7},{7,6},{8,9},{9,8},{10,11... | collective-permute-start | bytes 786440 | tf_op jit(solution)/shard_map/ppermute | solution.py:35
  174.2 6.4 %collective-permute-start.32 = (f32[2,16,512]{2,1,0:T(8,128)S(1)}, f32[2,16,512]{2,1,0:T(8,128)S(1)}, u32[]{:S(2)}, u32[]{:S(2)}) collective-permute-start(f32[2,16,512]{2,1,0:T(8,128)S(1)} %reverse_select_fusion), channel_id=1, source_target_pairs={{0,4},{2,6},{4,0},{6,2},{8,12},{10,14},{12,8},{14,10},{16,20},{18,... | collective-permute-start | bytes 196616 | tf_op jit(solution)/shard_map/ppermute | solution.py:69
  175.4 6.9 %collective-permute-start.18 = (f32[4,16,512]{2,1,0:T(8,128)S(1)}, f32[4,16,512]{2,1,0:T(8,128)S(1)}, u32[]{:S(2)}, u32[]{:S(2)}) collective-permute-start(f32[4,16,512]{2,1,0:T(8,128)S(1)} %get-tuple-element.19), channel_id=1, source_target_pairs={{0,8},{2,10},{4,12},{6,14},{8,16},{10,18},{12,20},{14,22},{16,24},... | collective-permute-start | bytes 393224 | tf_op jit(solution)/shard_map/ppermute | solution.py:35
  178.4 8.3 %collective-permute-start.19 = (f32[4,16,512]{2,1,0:T(8,128)S(1)}, f32[4,16,512]{2,1,0:T(8,128)S(1)}, u32[]{:S(2)}, u32[]{:S(2)}) collective-permute-start(f32[4,16,512]{2,1,0:T(8,128)S(1)} %get-tuple-element.20), channel_id=1, source_target_pairs={{0,16},{2,18},{4,20},{6,22},{8,24},{10,26},{12,28},{14,30},{16,0},... | collective-permute-start | bytes 393224 | tf_op jit(solution)/shard_map/ppermute | solution.py:35
  178.7 8.0 %collective-permute-start.20 = (f32[4,16,512]{2,1,0:T(8,128)S(1)}, f32[4,16,512]{2,1,0:T(8,128)S(1)}, u32[]{:S(2)}, u32[]{:S(2)}) collective-permute-start(f32[4,16,512]{2,1,0:T(8,128)S(1)} %get-tuple-element.21), channel_id=1, source_target_pairs={{0,24},{2,26},{4,28},{6,30},{8,0},{10,2},{12,4},{14,6},{16,8},{18,... | collective-permute-start | bytes 393224 | tf_op jit(solution)/shard_map/ppermute | solution.py:35
  180.6 6.6 %collective-permute-start.33 = (bf16[2,16,512]{2,1,0:T(8,128)(2,1)S(1)}, bf16[2,16,512]{2,1,0:T(8,128)(2,1)S(1)}, u32[]{:S(2)}, u32[]{:S(2)}) collective-permute-start(bf16[2,16,512]{2,1,0:T(8,128)(2,1)S(1)} %get-tuple-element.6), channel_id=1, source_target_pairs={{0,8},{2,10},{4,12},{6,14},{8,16},{10,18},{12,20},{14,22},{16,24},... | collective-permute-start | bytes 98312 | tf_op jit(solution)/shard_map/ppermute | solution.py:44
  180.6 11.5 %collective-permute-start.34 = (bf16[2,16,512]{2,1,0:T(8,128)(2,1)S(1)}, bf16[2,16,512]{2,1,0:T(8,128)(2,1)S(1)}, u32[]{:S(2)}, u32[]{:S(2)}) collective-permute-start(bf16[2,16,512]{2,1,0:T(8,128)(2,1)S(1)} %get-tuple-element.6), channel_id=1, source_target_pairs={{0,16},{2,18},{4,20},{6,22},{8,24},{10,26},{12,28},{14,30},{16,0},... | collective-permute-start | bytes 98312 | tf_op jit(solution)/shard_map/ppermute | solution.py:44
  182.3 13.8 %collective-permute-start.35 = (bf16[2,16,512]{2,1,0:T(8,128)(2,1)S(1)}, bf16[2,16,512]{2,1,0:T(8,128)(2,1)S(1)}, u32[]{:S(2)}, u32[]{:S(2)}) collective-permute-start(bf16[2,16,512]{2,1,0:T(8,128)(2,1)S(1)} %get-tuple-element.6), channel_id=1, source_target_pairs={{0,24},{2,26},{4,28},{6,30},{8,0},{10,2},{12,4},{14,6},{16,8},{18,... | collective-permute-start | bytes 98312 | tf_op jit(solution)/shard_map/ppermute | solution.py:44
  192.2 7.3 %collective-permute-start.22 = (bf16[4,16,512]{2,1,0:T(8,128)(2,1)S(1)}, bf16[4,16,512]{2,1,0:T(8,128)(2,1)S(1)}, u32[]{:S(2)}, u32[]{:S(2)}) collective-permute-start(bf16[4,16,512]{2,1,0:T(8,128)(2,1)S(1)} %get-tuple-element.4), channel_id=1, source_target_pairs={{0,8},{2,10},{4,12},{6,14},{8,16},{10,18},{12,20},{14,22},{16,24},... | collective-permute-start | bytes 196616 | tf_op jit(solution)/shard_map/ppermute | solution.py:44
  196.1 6.2 %collective-permute-start.36 = (bf16[2,64,512]{2,1,0:T(8,128)(2,1)S(1)}, bf16[2,64,512]{2,1,0:T(8,128)(2,1)S(1)}, u32[]{:S(2)}, u32[]{:S(2)}) collective-permute-start(bf16[2,64,512]{2,1,0:T(8,128)(2,1)S(1)} %constant_dynamic-update-slice_fusion.10), channel_id=1, source_target_pairs={{0,1},{1,0},{2,3},{3,2},{4,5},{5,4},{6,7},{7,6},{8,9},{9,8},{10,11... | collective-permute-start | bytes 393224 | tf_op jit(solution)/shard_map/ppermute | solution.py:44
  202.2 6.2 %collective-permute-start.25 = (bf16[4,64,512]{2,1,0:T(8,128)(2,1)S(1)}, bf16[4,64,512]{2,1,0:T(8,128)(2,1)S(1)}, u32[]{:S(2)}, u32[]{:S(2)}) collective-permute-start(bf16[4,64,512]{2,1,0:T(8,128)(2,1)S(1)} %constant_dynamic-update-slice_fusion.18), channel_id=1, source_target_pairs={{0,1},{1,0},{2,3},{3,2},{4,5},{5,4},{6,7},{7,6},{8,9},{9,8},{10,11... | collective-permute-start | bytes 786440 | tf_op jit(solution)/shard_map/ppermute | solution.py:44
  202.4 11.8 %collective-permute-start.37 = (bf16[2,128,512]{2,1,0:T(8,128)(2,1)S(1)}, bf16[2,128,512]{2,1,0:T(8,128)(2,1)S(1)}, u32[]{:S(2)}, u32[]{:S(2)}) collective-permute-start(bf16[2,128,512]{2,1,0:T(8,128)(2,1)S(1)} %constant_dynamic-update-slice_fusion.8), channel_id=1, source_target_pairs={{0,2},{2,0},{4,6},{6,4},{8,10},{10,8},{12,14},{14,12},{16,18},{18,... | collective-permute-start | bytes 786440 | tf_op jit(solution)/shard_map/ppermute | solution.py:44
  208.4 7.2 %collective-permute-start.26 = (bf16[4,128,512]{2,1,0:T(8,128)(2,1)S(1)}, bf16[4,128,512]{2,1,0:T(8,128)(2,1)S(1)}, u32[]{:S(2)}, u32[]{:S(2)}) collective-permute-start(bf16[4,128,512]{2,1,0:T(8,128)(2,1)S(1)} %constant_dynamic-update-slice_fusion.16), channel_id=1, source_target_pairs={{0,2},{2,0},{4,6},{6,4},{8,10},{10,8},{12,14},{14,12},{16,18},{18,... | collective-permute-start | bytes 1572872 | tf_op jit(solution)/shard_map/ppermute | solution.py:44
  (19 other events, 99.6 us)

commit v2 on v0

v2 whole, which is shorter than its diff:
```python
import functools

import jax
import jax.numpy as jnp
from jax import lax
from jax.experimental import pallas as pl
from jax.experimental.pallas import tpu as pltpu
from jax.sharding import PartitionSpec as P

DILATION_BINS = 4096
BF16, F32 = jnp.bfloat16, jnp.float32
VMEM_BYTES = 40 * 1024 * 1024
SIDE, CORE, DP, ALONG = range(4)
HBM = pl.BlockSpec(memory_space=pltpu.HBM)
WHOLE = pl.BlockSpec(memory_space=pltpu.VMEM)


def shape_of(shape, dtype):
    return jax.ShapeDtypeStruct(shape, dtype)


TOKEN = jax.ShapeDtypeStruct((8, 128), F32)


class Device:
    def __init__(self, meta):
        self.meta, self.token = meta, None


def call(
    body, device, operands, in_specs, outs, out_specs, grid=(), scratch=(), aliases=None, name=None, after=()
):
    first = device.token is None
    n_in, single = len(operands), not isinstance(outs, list)
    outs, out_specs = ([outs], [out_specs]) if single else (outs, out_specs)
    n_out = len(outs)
    tokens = [*after] if first else [device.token, *after]

    def chained(meta, *refs):
        rest = refs[n_in + len(tokens) :]
        body(meta, *refs[:n_in], *rest[:n_out], *rest[n_out + 1 :])

    results = pl.pallas_call(
        chained,
        grid_spec=pltpu.PrefetchScalarGridSpec(
            num_scalar_prefetch=1, grid=grid, in_specs=[*in_specs, *[HBM] * len(tokens)], out_specs=[*out_specs, HBM],
            scratch_shapes=list(scratch),
        ),
        out_shape=[*outs, TOKEN],
        input_output_aliases=aliases or {},
        compiler_params=pltpu.CompilerParams(vmem_limit_bytes=VMEM_BYTES),
        cost_estimate=pl.CostEstimate(flops=1, bytes_accessed=200_000, transcendentals=0),
        name=name,
    )(device.meta, *operands, *tokens)
    device.token = results[-1]
    return results[0] if single else results[:-1]


def gelu_parts(x):
    k = 0.7978845608028654
    square = x * x
    t = jnp.tanh(k * (x * (1.0 + 0.044715 * square)))
    return t, square, k


def gelu(x):
    t, _, _ = gelu_parts(x)
    return x * (0.5 * (1.0 + t))


def gelu_and_slope(x):
    t, square, k = gelu_parts(x)
    cdf = 0.5 * (1.0 + t)
    slope = cdf + 0.5 * x * (1.0 - t * t) * (k + (3 * 0.044715 * k) * square)
    return x * cdf, slope


def mm(left, right):
    return lax.dot_general(left, right, (((1,), (0,)), ((), ())), preferred_element_type=F32)


def mm_back(left, right):
    return lax.dot_general(left, right, (((1,), (1,)), ((), ())), preferred_element_type=F32)


def mm_outer(left, right):
    return lax.dot_general(left, right, (((0,), (0,)), ((), ())), preferred_element_type=F32)


def cut_body(plan, n_in, meta, *refs):
    ins, outs, sems = refs[:n_in], refs[n_in:-1], refs[-1]
    copies = []
    for n, (which, own, col, rows, cols) in enumerate(plan):
        start = (meta[SIDE] if own else 1 - meta[SIDE]) * rows
        window = ins[which].at[pl.ds(pl.multiple_of(start, rows), rows), pl.ds(col, cols)]
        copies.append(pltpu.make_async_copy(window, outs[n], sems.at[n]))
    for copy in copies:
        copy.start()
    for copy in copies:
        copy.wait()


def cut(device, operands, plan, name):
    outs = [shape_of((rows, cols), BF16) for _, _, _, rows, cols in plan]
    return call(
        functools.partial(cut_body, plan, len(operands)), device, operands, [HBM] * len(operands), outs,
        [HBM] * len(plan), scratch=[pltpu.SemaphoreType.DMA((len(plan),))], name=name,
    )


def split_into(total, position, count, keep, sends):
    size = total.shape[1] // count
    for shift, ref in enumerate((keep, *sends)):
        there = lax.rem(position + shift, count)
        ref[...] = total[:, pl.ds(pl.multiple_of(there * size, size), size), :]


def mid_body(steps, count, meta, x, u, *refs):
    *slices, total = refs
    i = pl.program_id(0)

    @pl.when(i == 0)
    def _():
        total[...] = jnp.zeros_like(total)

    cols = total.shape[2]
    product = mm_outer(gelu(x[...].astype(F32)).astype(BF16), u[...])
    for part in range(2):
        total[part] += product[:, part * cols : (part + 1) * cols]
    send_slices(i == steps - 1, count, meta, total, slices)


def send_slices(last, count, meta, total, slices):
    @pl.when(last)
    def _():
        for part in range(2):
            split_into(total.at[part : part + 1], meta[CORE], count, slices[part], [slices[2 + part]])


def reduce_body(sizes, n_out, place, swap_sides, meta, *refs):
    n_in = sum(sizes)
    ins, outs, total = refs[:n_in], refs[n_in:-1], refs[-1]
    first = lead = 0
    for size in sizes:
        value = ins[first][...]
        for ref in ins[first + 1 : first + size]:
            value = value + ref[...]
        first += size
        parts = value.shape[0]
        if not swap_sides:
            total[lead : lead + parts] = value
        else:
            plain = parts - 2
            if plain:
                total[lead : lead + plain] = value[:plain]
            for part in range(2):
                total[lead + plain + part] = jnp.where(meta[SIDE] == 0, value[plain + part], value[plain + 1 - part])
        lead += parts
    if n_out > 1:
        split_into(total, meta[place], n_out, outs[0], outs[1:])
    else:
        outs[0][...] = total[...].astype(outs[0].dtype)


def reduce(device, groups, n_out=1, place=None, swap_sides=False, dtype=F32, name=None, after=()):
    _, rows, cols = groups[0][0].shape
    k = sum(group[0].shape[0] for group in groups)
    values = [value for group in groups for value in group]
    outs = [shape_of((k, rows // n_out, cols), dtype)] * n_out
    body = functools.partial(reduce_body, [len(group) for group in groups], n_out, place, swap_sides)
    return call(
        body, device, values, [WHOLE] * len(values), outs, [WHOLE] * n_out,
        scratch=[pltpu.VMEM((k, rows, cols), F32)], name=name, after=after,
    )


def gather_body(count, place, meta, *refs):
    ins, out = refs[:count], refs[count]
    size = ins[0].shape[1]
    for shift, ref in enumerate(ins):
        source = lax.rem(meta[place] + count - shift, count)
        out[:, pl.ds(pl.multiple_of(source * size, size), size), :] = ref[...]


def gather(device, values, place, name=None):
    count = len(values)
    k, rows, cols = values[0].shape
    return call(
        functools.partial(gather_body, count, place), device, values, [WHOLE] * count,
        shape_of((k, rows * count, cols), BF16), WHOLE, name=name,
    )


def write_taps_body(count, targets, meta, *refs):
    ins = refs[:count]
    out, wide, sems = refs[count:]
    size = ins[0].shape[1]
    for shift, ref in enumerate(ins):
        source = lax.rem(meta[CORE] + count - shift, count)
        wide[:, pl.ds(pl.multiple_of(source * size, size), size), :] = ref[...].astype(F32)
    copies = []
    for n, (tap, col) in enumerate(targets):
        window = out.at[tap, :, pl.ds(col, wide.shape[2])]
        copies.append(pltpu.make_async_copy(wide.at[n], window, sems.at[n]))
    for copy in copies:
        copy.start()
    for copy in copies:
        copy.wait()


def write_taps(device, values, targets, shape, name):
    count = len(values)
    k, rows, cols = values[0].shape
    return call(
        functools.partial(write_taps_body, count, targets), device, values, [WHOLE] * count,
        shape_of(shape, F32), HBM, scratch=[pltpu.VMEM((k, rows * count, cols), F32), pltpu.SemaphoreType.DMA((k,))],
        name=name,
    )


def act_body(meta, x, *acts):
    act = gelu(x[...].astype(F32)).astype(BF16)
    cols = acts[0].shape[1]
    for n, ref in enumerate(acts):
        ref[...] = act[:, n * cols : (n + 1) * cols]


def mm_parts(lefts, weight):
    cols = lefts[0].shape[1]
    return sum(mm(left[...], weight[0, n * cols : (n + 1) * cols]) for n, left in enumerate(lefts))


def oth_out_body(meta, x0, x1, oth0, oth1, far0, far1, own0, own1, w_near, w_mid, w_far, out):
    cols = x0.shape[1]
    conv = mm_parts((oth0, oth1), w_mid) + mm_parts((far0, far1), w_near) + mm_parts((own0, own1), w_far)
    out[:, :cols] = (x0[...].astype(F32) + conv[:, :cols]).astype(BF16)
    out[:, cols:] = (x1[...].astype(F32) + conv[:, cols:]).astype(BF16)


def own_out_body(meta, x, own0, own1, oth0, oth1, far0, far1, w_near, w_mid, w_far, out):
    conv = mm_parts((own0, own1), w_mid) + mm_parts((oth0, oth1), w_near) + mm_parts((far0, far1), w_far)
    out[...] = (x[...].astype(F32) + conv).astype(BF16)


def outer_body(steps, count, meta, own0, own1, oth0, oth1, far0, far1, u_own, u_oth, u_far, *refs):
    *slices, total = refs
    i = pl.program_id(0)

    @pl.when(i == 0)
    def _():
        total[...] = jnp.zeros_like(total)

    cols = own0.shape[1]
    for n, (own, oth, far) in enumerate(((own0, oth0, far0), (own1, oth1, far1))):
        rows = slice(n * cols, (n + 1) * cols)
        total[0, rows] += mm_outer(own[...], u_oth[...]) + mm_outer(oth[...], u_far[...])
        total[1, rows] += mm_outer(far[...], u_oth[...]) + mm_outer(oth[...], u_own[...])
    send_slices(i == steps - 1, count, meta, total, slices)


def mm_back_parts(lefts, weight):
    cols = lefts[0].shape[1]
    return sum(mm_back(left[...], weight[0, :, n * cols : (n + 1) * cols]) for n, left in enumerate(lefts))


def oth_grad_body(meta, x0, x1, u_own, oth0, oth1, far0, far1, w_near, w_mid, w_far, grad0, grad1):
    cols = oth0.shape[1]
    grad_act = mm_back(u_own[...], w_near[0]) + mm_back_parts((oth0, oth1), w_mid) + mm_back_parts((far0, far1), w_far)
    for n, (x, u, grad) in enumerate(((x0, oth0, grad0), (x1, oth1, grad1))):
        _, slope = gelu_and_slope(x[...].astype(F32))
        grad[...] = (u[...].astype(F32) + slope * grad_act[:, n * cols : (n + 1) * cols]).astype(BF16)


def own_grad_body(meta, x, u_own, oth0, oth1, far0, far1, w_near, w_mid, w_far, grad):
    _, slope = gelu_and_slope(x[...].astype(F32))
    u = u_own[...]
    grad_act = mm_back(u, w_mid[0]) + mm_back_parts((oth0, oth1), w_far) + mm_back_parts((far0, far1), w_near)
    grad[...] = (u.astype(F32) + slope * grad_act).astype(BF16)


def place_body(row, col, meta, part, buffer, out, sem):
    rows, cols = part.shape
    start = pl.multiple_of((1 - meta[SIDE]) * (buffer.shape[0] // 2), rows) + row
    copy = pltpu.make_async_copy(part, out.at[pl.ds(pl.multiple_of(start, 16), rows), pl.ds(col, cols)], sem)
    copy.start()
    copy.wait()


def place(device, part, buffer, row, col, name):
    return call(
        functools.partial(place_body, row, col), device, (part, buffer), [HBM, HBM],
        shape_of(buffer.shape, buffer.dtype), HBM, scratch=[pltpu.SemaphoreType.DMA], aliases={2: 0}, name=name,
    )


def per_device(genome, conv_weight, upstream):
    genome, upstream = genome[0], upstream[0]
    bins, chans = genome.shape
    half, cols = bins // 2, chans // 2
    block = half // 4
    steps = half // block
    count = lax.axis_size("seq")
    index = lax.axis_index("seq")
    tap = DILATION_BINS // bins
    span = 2 * tap
    dp_count, along_count = lax.axis_size("dp"), count // span
    side, along = lax.rem(index // tap, 2), index // span
    if along_count % 2 == 0:
        along = along ^ side
    meta = jnp.stack(
        [side, lax.rem(index, tap), lax.axis_index("dp"), along]
    ).astype(jnp.int32)

    def is_even(i):
        return (i // tap) % 2 == 0

    swap_pairs = [(i, i + tap if is_even(i) else i - tap) for i in range(count)]
    outer_pairs = [(i, i - span if is_even(i) else i + span) for i in range(count)]
    outer_pairs = [(i, j) for i, j in outer_pairs if 0 <= j < count]
    inner_pairs = [(j, i) for i, j in outer_pairs]

    def swap(value):
        return lax.ppermute(value, "seq", swap_pairs)

    def outward(value):
        return lax.ppermute(value, "seq", outer_pairs)

    def inward(value):
        return lax.ppermute(value, "seq", inner_pairs)

    def to_core(value, shift=1):
        return lax.ppermute(value, "seq", [(i, i - i % tap + (i % tap + shift) % tap) for i in range(count)])

    def to_dp(value, shift=1):
        return lax.ppermute(value, "dp", [(i, (i + shift) % dp_count) for i in range(dp_count)])

    flip = 1 if along_count % 2 == 0 else 0

    def place_along(i):
        return (i // span) ^ (flip * ((i // tap) % 2))

    def device_at(i, side, position):
        return (position ^ (flip * side)) * span + side * tap + i % tap

    def to_along(value, shift):
        pairs = [(i, device_at(i, (i // tap) % 2, (place_along(i) + shift) % along_count)) for i in range(count)]
        return lax.ppermute(value, "seq", pairs)

    def to_side(value):
        pairs = [(i, device_at(i, 1 - (i // tap) % 2, place_along(i))) for i in range(count)]
        return lax.ppermute(value, "seq", pairs)

    rows_spec = pl.BlockSpec((block, chans), lambda i, s: (i, 0))
    part_spec = pl.BlockSpec((block, cols), lambda i, s: (i, 0))
    own_spec = pl.BlockSpec((block, chans), lambda i, s: (s[SIDE] * steps + i, 0))

    w_near = pl.BlockSpec((1, chans, chans), lambda i, s: (2 - 2 * s[SIDE], 0, 0))
    w_mid = pl.BlockSpec((1, chans, chans), lambda i, s: (1, 0, 0))
    w_far = pl.BlockSpec((1, chans, chans), lambda i, s: (2 * s[SIDE], 0, 0))

    weights = (conv_weight,) * 3
    slice_specs = [pl.BlockSpec((1, chans // tap, cols), lambda i, s: (0, 0, 0))] * 4
    slices = [shape_of((1, chans // tap, cols), F32)] * 4
    total_shape = pltpu.VMEM((2, chans, cols), F32)

    device = Device(meta)

    (x_send0,) = cut(device, (genome,), [(0, False, 0, half, cols)], "cut_first")
    x_oth0 = swap(x_send0)
    a_own = call(
        act_body, device, (genome,), [own_spec], [shape_of((half, cols), BF16)] * 2, [part_spec] * 2,
        grid=(steps,), name="own_act",
    )
    a_oth_far = [outward(part) for part in a_own]
    plan = [(0, False, cols), (1, False, 0), (1, False, cols), (1, True, 0), (1, True, cols)]
    x_send1, u_send0, u_send1, u_own0, u_own1 = cut(
        device, (genome, upstream), [(which, own, col, half, cols) for which, own, col in plan], "cut_rest"
    )
    x_oth1, u_oth = swap(x_send1), [swap(u_send0), swap(u_send1)]
    u_oth_far = [outward(u_own0), outward(u_own1)]
    mid = call(
        functools.partial(mid_body, 2 * steps, tap), device, (genome, upstream), [rows_spec] * 2, slices, slice_specs,
        grid=(2 * steps,), scratch=[total_shape], name="mid_tap",
    )

    staged = (chans // tap // dp_count) % (16 * along_count) == 0

    def core_stage(parts, name, after=()):
        groups = [[keep, to_core(send)] for keep, send in zip(parts[:2], parts[2:])]
        keep, send = reduce(device, groups, dp_count, DP, name=name + "_core", after=after)
        return [keep, to_dp(send)]

    def dp_stage(groups, name, after=()):
        if not staged:
            return reduce(device, groups, name=name + "_dp", after=after)
        parts = reduce(device, groups, along_count, ALONG, name=name + "_dp", after=after)
        return [parts[0]] + [to_along(part, shift) for shift, part in enumerate(parts[1:], 1)]

    def along_stage(groups, name, after=()):
        (total,) = reduce(device, groups, swap_sides=True, name=name + "_along", after=after)
        if not staged:
            together = [[i + span * j for j in range(along_count)] for i in range(span)]
            total = lax.psum(total, "seq", axis_index_groups=together)
        return [total, to_side(total)]

    def side_stage(parts, name):
        (total,) = reduce(device, [parts], dtype=BF16, name=name + "_side")
        return [total] + [to_along(total, s) for s in range(1, along_count) if staged]

    def gather_along(parts, name):
        total = gather(device, parts, ALONG, name + "_all_along") if staged else parts[0]
        return [total] + [to_dp(total, s) for s in range(1, dp_count)]

    def gather_dp(parts, name):
        total = gather(device, parts, DP, name + "_all_dp")
        return [total] + [to_core(total, s) for s in range(1, tap)]

    def outer_taps(k, after=()):
        u_own_spec = pl.BlockSpec((block, cols), lambda i, s: (s[SIDE] * steps + i, k))
        return call(
            functools.partial(outer_body, steps, tap), device,
            (*a_own, *a_oth, *a_oth_far, upstream, u_oth[k], u_oth_far[k]),
            [*[part_spec] * 6, u_own_spec, part_spec, part_spec], slices, slice_specs,
            grid=(steps,), scratch=[total_shape], name=f"outer_taps{k}", after=after,
        )

    def oth_act(x, name, after=()):
        return call(
            act_body, device, (x,), [part_spec], shape_of((half, cols), BF16), part_spec, grid=(steps,), name=name,
            after=after,
        )

    a_oth0 = oth_act(x_oth0, "oth_act0")
    a_own_far0 = inward(a_oth0)
    mid = core_stage(mid, "mid", after=(a_oth_far[0],))
    a_oth1 = oth_act(x_oth1, "oth_act1", after=(a_oth_far[1],))
    a_own_far1 = inward(a_oth1)
    a_oth = [a_oth0, a_oth1]
    out = call(
        oth_out_body, device, (x_oth0, x_oth1, *a_oth, *a_oth_far, *a_own, *weights),
        [*[part_spec] * 8, w_near, w_mid, w_far],
        shape_of((half, chans), BF16), rows_spec, grid=(steps,), name="oth_out", after=(a_own_far0,),
    )
    out = swap(out)
    sent0 = outer_taps(0, after=(a_own_far1,))
    u_own_far0 = inward(u_oth[0])
    parts0 = core_stage(sent0, "outer0", after=(u_oth[1], u_oth_far[1], u_own_far0))
    sent1 = outer_taps(1)
    grad0, grad1 = call(
        oth_grad_body, device, (x_oth0, x_oth1, upstream, *u_oth, *u_oth_far, *weights),
        [part_spec, part_spec, own_spec, *[part_spec] * 4, w_near, w_mid, w_far],
        [shape_of((half, cols), BF16)] * 2, [part_spec] * 2, grid=(steps,), name="oth_grad",
    )
    grad0, grad1 = swap(grad0), swap(grad1)
    parts1 = core_stage(sent1, "outer1")
    u_own_far1 = inward(u_oth[1])
    parts0 = dp_stage([mid, parts0], "outer0")
    output = call(
        own_out_body, device, (genome, *a_own, *a_oth, a_own_far0, a_own_far1, *weights),
        [own_spec, *[part_spec] * 6, w_near, w_mid, w_far],
        shape_of((bins, chans), BF16), own_spec, grid=(steps,), name="own_out",
    )
    parts1 = dp_stage([parts1], "outer1")
    grad_genome = call(
        own_grad_body, device, (genome, upstream, *u_oth, u_own_far0, u_own_far1, *weights),
        [own_spec, own_spec, *[part_spec] * 4, w_near, w_mid, w_far],
        shape_of((bins, chans), BF16), own_spec, grid=(steps,), name="own_grad",
    )
    output = place(device, out, output, 0, 0, "place_out")
    parts = along_stage([parts0, parts1], "outer")
    parts = side_stage(parts, "outer")
    grad_genome = place(device, grad0, grad_genome, 0, 0, "place_grad0")
    parts = gather_along(parts, "outer")
    grad_genome = place(device, grad1, grad_genome, 0, cols, "place_grad1")
    parts = gather_dp(parts, "outer")
    targets = [(1, 0), (1, cols), (0, 0), (2, 0), (0, cols), (2, cols)]
    grad_weight = write_taps(device, parts, targets, conv_weight.shape, "write_taps")
    return (output[None], grad_genome[None], grad_weight)


def solution(mesh):
    return jax.shard_map(
        per_device,
        mesh=mesh,
        in_specs=(P("dp", "seq", None), P(), P("dp", "seq", None)),
        out_specs=(P("dp", "seq", None), P("dp", "seq", None), P()),
        check_vma=False,
    )
```

time: 313 us -> 138 us (0.44)
  waiting for transfers between devices: 236 us -> 32.7 us
  starting transfers between devices: 12.9 us -> 60.7 us
  Pallas kernels: 0 us -> 41.5 us
  matrix products: 34.1 us -> 0 us
  between operations: 14.1 us -> 1.02 us
  local copies, waits for them, and re-layouts: 7.49 us -> 1.61 us
  other arithmetic: 5.11 us -> 0.08 us
    ppermute x4 -> x36, waiting for transfers between devices: 144 us -> 32.7 us  [the longest x4 10.7 us: to_dp(): lax.ppermute(value, 'dp', [(i, (i + shift) % dp_count) for i in range(dp_...]
    psum x1 -> x0, waiting for transfers between devices: 92.3 us -> none  [per_device(): grad_weight = lax.psum(partial_gradient, ('seq', 'dp'))]
    ppermute x4 -> x36, starting transfers between devices: 12.9 us -> 60.7 us  [the longest x7 18.9 us: to_core(): lax.ppermute(value, 'seq', [(i, i - i % tap + (i % tap + shift) % tap) fo...]
    pallas_call x0 -> x25, Pallas kernels: none -> 41.5 us  [call(): pl.pallas_call(chained, grid_spec=pltpu.PrefetchScalarGridSpec(num_scalar...]
    dot_general x9 -> x0, matrix products: 34.1 us -> none  [the longest x3 14.9 us: mixing_back(): jnp.einsum('gbd,cd->gbc', left, right, preferred_element_type=jnp.float32)]
    unnamed x17 -> x8, local copies, waits for them, and re-layouts: 7.49 us -> 1.61 us
    convert_element_type x1 -> x0, other arithmetic: 3.14 us -> none  [per_device(): act = act_full.astype(jnp.bfloat16)]
  transfers between devices with their start and end apart: 5 -> 36, of which waited for: 3 -> 14; matrix products, arithmetic and copies ran while one was open for 12% -> 0% of each run, Pallas kernels for 0% -> 28%
where the time goes in v2:
time: 138 us
  starting transfers between devices  60.7 us (44%)
  Pallas kernels  41.5 us (30%)
  waiting for transfers between devices  32.7 us (24%)
  local copies, waits for them, and re-layouts  1.61 us (1%)
    pallas_call x25, Pallas kernels, call(): pl.pallas_call(chained, grid_spec=pltpu.PrefetchScalarGridSpec(num_scalar...  41.5 us
    ppermute x7, starting transfers between devices, to_core(): lax.ppermute(value, 'seq', [(i, i - i % tap + (i % tap + shift) % tap) fo...  18.9 us
    ppermute x4, starting transfers between devices, inward(): return lax.ppermute(value, 'seq', inner_pairs)  14.6 us
    ppermute x4, waiting for transfers between devices, to_dp(): lax.ppermute(value, 'dp', [(i, (i + shift) % dp_count) for i in range(dp_...  10.7 us
    ppermute x9, starting transfers between devices, to_along(): return lax.ppermute(value, 'seq', pairs)  9.76 us
    ppermute x7, starting transfers between devices, swap(): return lax.ppermute(value, 'seq', swap_pairs)  7.04 us
    ppermute x7, waiting for transfers between devices, swap(): return lax.ppermute(value, 'seq', swap_pairs)  6.2 us
    ppermute x4, starting transfers between devices, outward(): return lax.ppermute(value, 'seq', outer_pairs)  5.14 us
  transfers between devices with their start and end apart: 36, of which 14 were waited for; matrix products, arithmetic and copies ran while one was open for 0% of the time, Pallas kernels for 28%

profile of v2, /device:TPU:1, one launch (start us, length us, event | category | flops | bytes accessed | tf_op | source)
XLA Modules:
  0.0 137.5 jit_solution(12185082505990150190)
XLA Ops:
  0.7 1.6 %copy-done.1 = bf16[1,2048,512]{2,1,0:T(8,128)(2,1)S(1)} copy-done((bf16[1,2048,512]{2,1,0:T(8,128)(2,1)S(1)}, bf16[1,2048,512]{2,1,0:T(8,128)(2,1)}, u32[]{:S(2)}) %copy-start.1) | copy-done | bytes 2097176
  2.9 2.1 %collective-permute-start = (bf16[1024,256]{1,0:T(8,128)(2,1)S(1)}, bf16[1024,256]{1,0:T(8,128)(2,1)S(1)}, u32[]{:S(2)}, u32[]{:S(2)}) collective-permute-start(bf16[1024,256]{1,0:T(8,128)(2,1)S(1)} %get-tuple-element.76), channel_id=1, source_target_pairs={{0,4},{2,6},{4,0},{6,2},{8,12},{10,14},{12,8},{14,10},{16,20},{18,... | collective-permute-start | bytes 1572872 | tf_op jit(solution)/shard_map/ppermute | solution.py:323
  8.5 2.2 %collective-permute-start.1 = (bf16[1024,256]{1,0:T(8,128)(2,1)S(1)}, bf16[1024,256]{1,0:T(8,128)(2,1)S(1)}, u32[]{:S(2)}, u32[]{:S(2)}) collective-permute-start(bf16[1024,256]{1,0:T(8,128)(2,1)S(1)} %get-tuple-element.79), channel_id=1, source_target_pairs={{0,4},{2,6},{4,0},{6,2},{8,12},{10,14},{12,8},{14,10},{16,20},{18,... | collective-permute-start | bytes 1572872 | tf_op jit(solution)/shard_map/ppermute | solution.py:323
  12.0 4.1 %mid_tap.1 = (f32[1,256,256]{2,1,0:T(8,128)S(1)}, f32[1,256,256]{2,1,0:T(8,128)S(1)}, f32[1,256,256]{2,1,0:T(8,128)S(1)}, f32[1,256,256]{2,1,0:T(8,128)S(1)}, f32[8,128]{1,0:T(8,128)S(1)}) custom-call(s32[4]{0:T(128)S(1)} %pad_add_fusion.meta, bf16[2048,512]{1,0:T(8,128)(2,1)S(1)} %bitcast.11, bf16[2048,512]{1,0:T(8,128)(2,1)S(1)} %bitcast.15, ...), custom_call_target="tpu_custom_call" | custom-call | flops 1 | bytes 200000 | tf_op jit(solution)/shard_map/mid_tap/pallas_call | solution.py:43
  16.1 1.6 %collective-permute-start.2 = (f32[1,256,256]{2,1,0:T(8,128)S(1)}, f32[1,256,256]{2,1,0:T(8,128)S(1)}, u32[]{:S(2)}, u32[]{:S(2)}) collective-permute-start(f32[1,256,256]{2,1,0:T(8,128)S(1)} %get-tuple-element.84), channel_id=1, source_target_pairs={{0,2},{2,0},{4,6},{6,4},{8,10},{10,8},{12,14},{14,12},{16,18},{18,... | collective-permute-start | bytes 786440 | tf_op jit(solution)/shard_map/ppermute | solution.py:332
  19.8 1.8 %collective-permute-start.10 = (bf16[1024,256]{1,0:T(8,128)(2,1)S(1)}, bf16[1024,256]{1,0:T(8,128)(2,1)S(1)}, u32[]{:S(2)}, u32[]{:S(2)}) collective-permute-start(bf16[1024,256]{1,0:T(8,128)(2,1)S(1)} %get-tuple-element.96), channel_id=1, source_target_pairs={{0,4},{2,6},{4,0},{6,2},{8,12},{10,14},{12,8},{14,10},{16,20},{18,... | collective-permute-start | bytes 1572872 | tf_op jit(solution)/shard_map/ppermute | solution.py:323
  21.6 3.2 %collective-permute-start.6 = (bf16[1024,256]{1,0:T(8,128)(2,1)S(1)}, bf16[1024,256]{1,0:T(8,128)(2,1)S(1)}, u32[]{:S(2)}, u32[]{:S(2)}) collective-permute-start(bf16[1024,256]{1,0:T(8,128)(2,1)S(1)} %get-tuple-element.82.refs_2_.refs_3_), channel_id=1, source_target_pairs={{12,4},{14,6},{0,8},{2,10},{20,12},{22,14},{8,16},{10,18},{28,20},... | collective-permute-start | bytes 1572872 | tf_op jit(solution)/shard_map/ppermute | solution.py:329
  27.9 4.1 %collective-permute-done.5.refs_2_.refs_5_ = bf16[1024,256]{1,0:T(8,128)(2,1)S(1)} collective-permute-done((bf16[1024,256]{1,0:T(8,128)(2,1)S(1)}, bf16[1024,256]{1,0:T(8,128)(2,1)S(1)}, u32[]{:S(2)}, u32[]{:S(2)}) %collective-permute-start.5) | collective-permute-done | bytes 524320 | tf_op jit(solution)/shard_map/ppermute | solution.py:326
  33.0 3.2 %collective-permute-start.8 = (bf16[1024,256]{1,0:T(8,128)(2,1)S(1)}, bf16[1024,256]{1,0:T(8,128)(2,1)S(1)}, u32[]{:S(2)}, u32[]{:S(2)}) collective-permute-start(bf16[1024,256]{1,0:T(8,128)(2,1)S(1)} %get-tuple-element.91.refs_3_.refs_4_), channel_id=1, source_target_pairs={{12,4},{14,6},{0,8},{2,10},{20,12},{22,14},{8,16},{10,18},{28,20},... | collective-permute-start | bytes 1572872 | tf_op jit(solution)/shard_map/ppermute | solution.py:329
  36.4 2.8 %collective-permute-done.10.refs_7_.refs_3_.refs_2_ = bf16[1024,256]{1,0:T(8,128)(2,1)S(1)} collective-permute-done((bf16[1024,256]{1,0:T(8,128)(2,1)S(1)}, bf16[1024,256]{1,0:T(8,128)(2,1)S(1)}, u32[]{:S(2)}, u32[]{:S(2)}) %collective-permute-start.10) | collective-permute-done | bytes 524320 | tf_op jit(solution)/shard_map/ppermute | solution.py:323
  40.5 4.0 %collective-permute-start.16 = (bf16[1024,256]{1,0:T(8,128)(2,1)S(1)}, bf16[1024,256]{1,0:T(8,128)(2,1)S(1)}, u32[]{:S(2)}, u32[]{:S(2)}) collective-permute-start(bf16[1024,256]{1,0:T(8,128)(2,1)S(1)} %collective-permute-done.10.refs_7_.refs_3_.refs_2_), channel_id=1, source_target_pairs={{12,4},{14,6},{0,8},{2,10},{20,12},{22,14},{8,16},{10,18},{28,20},... | collective-permute-start | bytes 1572872 | tf_op jit(solution)/shard_map/ppermute | solution.py:329
  44.5 2.9 %oth_out.1 = (bf16[1024,512]{1,0:T(8,128)(2,1)S(1)}, f32[8,128]{1,0:T(8,128)S(1)}) custom-call(s32[4]{0:T(128)S(1)} %pad_add_fusion.meta, bf16[1024,256]{1,0:T(8,128)(2,1)S(1)} %collective-permute-done.refs_0_, bf16[1024,256]{1,0:T(8,128)(2,1)S(1)} %collective-permute-done.1.refs_0_.refs_1_, bf16[1024,256]{1,0:T(8,128)(2,1)S(1)} %get-tuple-element.82.refs_2_.refs_3_, ...), custom_call_target="tpu_custom_call" | custom-call | flops 1 | bytes 200000 | tf_op jit(solution)/shard_map/oth_out/pallas_call | solution.py:43
  47.8 2.8 %outer_taps0.1 = (f32[1,256,256]{2,1,0:T(8,128)S(1)}, f32[1,256,256]{2,1,0:T(8,128)S(1)}, f32[1,256,256]{2,1,0:T(8,128)S(1)}, f32[1,256,256]{2,1,0:T(8,128)S(1)}, f32[8,128]{1,0:T(8,128)S(1)}) custom-call(s32[4]{0:T(128)S(1)} %pad_add_fusion.meta, bf16[1024,256]{1,0:T(8,128)(2,1)S(1)} %get-tuple-element.88.refs_6_.refs_0_.refs_1_, ...), custom_call_target="tpu_custom_call" | custom-call | flops 1 | bytes 200000 | tf_op jit(solution)/shard_map/outer_taps0/pallas_call | solution.py:43
  50.7 3.5 %collective-permute-start.12 = (f32[1,256,256]{2,1,0:T(8,128)S(1)}, f32[1,256,256]{2,1,0:T(8,128)S(1)}, u32[]{:S(2)}, u32[]{:S(2)}) collective-permute-start(f32[1,256,256]{2,1,0:T(8,128)S(1)} %get-tuple-element.100), channel_id=1, source_target_pairs={{0,2},{2,0},{4,6},{6,4},{8,10},{10,8},{12,14},{14,12},{16,18},{18,... | collective-permute-start | bytes 786440 | tf_op jit(solution)/shard_map/ppermute | solution.py:332
  54.3 2.0 %collective-permute-done.16.refs_7_.refs_4_ = bf16[1024,256]{1,0:T(8,128)(2,1)S(1)} collective-permute-done((bf16[1024,256]{1,0:T(8,128)(2,1)S(1)}, bf16[1024,256]{1,0:T(8,128)(2,1)S(1)}, u32[]{:S(2)}, u32[]{:S(2)}) %collective-permute-start.16) | collective-permute-done | bytes 524320 | tf_op jit(solution)/shard_map/ppermute | solution.py:329
  56.9 2.8 %outer_taps1.1 = (f32[1,256,256]{2,1,0:T(8,128)S(1)}, f32[1,256,256]{2,1,0:T(8,128)S(1)}, f32[1,256,256]{2,1,0:T(8,128)S(1)}, f32[1,256,256]{2,1,0:T(8,128)S(1)}, f32[8,128]{1,0:T(8,128)S(1)}) custom-call(s32[4]{0:T(128)S(1)} %pad_add_fusion.meta, bf16[1024,256]{1,0:T(8,128)(2,1)S(1)} %get-tuple-element.88.refs_6_.refs_0_.refs_1_, ...), custom_call_target="tpu_custom_call" | custom-call | flops 1 | bytes 200000 | tf_op jit(solution)/shard_map/outer_taps1/pallas_call | solution.py:43
  59.8 3.4 %collective-permute-start.18 = (f32[1,256,256]{2,1,0:T(8,128)S(1)}, f32[1,256,256]{2,1,0:T(8,128)S(1)}, u32[]{:S(2)}, u32[]{:S(2)}) collective-permute-start(f32[1,256,256]{2,1,0:T(8,128)S(1)} %get-tuple-element.110), channel_id=1, source_target_pairs={{0,2},{2,0},{4,6},{6,4},{8,10},{10,8},{12,14},{14,12},{16,18},{18,... | collective-permute-start | bytes 786440 | tf_op jit(solution)/shard_map/ppermute | solution.py:332
  63.2 4.1 %collective-permute-start.20 = (bf16[1024,256]{1,0:T(8,128)(2,1)S(1)}, bf16[1024,256]{1,0:T(8,128)(2,1)S(1)}, u32[]{:S(2)}, u32[]{:S(2)}) collective-permute-start(bf16[1024,256]{1,0:T(8,128)(2,1)S(1)} %collective-permute-done.14.refs_5_.refs_7_.refs_4_.refs_3_), channel_id=1, source_target_pairs={{12,4},{14,6},{0,8},{2,10},{20,12},{22,14},{8,16},{10,18},{28,20},... | collective-permute-start | bytes 1572872 | tf_op jit(solution)/shard_map/ppermute | solution.py:329
  69.1 3.8 %oth_grad.1 = (bf16[1024,256]{1,0:T(8,128)(2,1)S(1)}, bf16[1024,256]{1,0:T(8,128)(2,1)S(1)}, f32[8,128]{1,0:T(8,128)S(1)}) custom-call(s32[4]{0:T(128)S(1)} %pad_add_fusion.meta, bf16[1024,256]{1,0:T(8,128)(2,1)S(1)} %collective-permute-done.refs_0_, bf16[1024,256]{1,0:T(8,128)(2,1)S(1)} %collective-permute-done.1.refs_0_.refs_1_, ...), custom_call_target="tpu_custom_call" | custom-call | flops 1 | bytes 200000 | tf_op jit(solution)/shard_map/oth_grad/pallas_call | solution.py:43
  75.4 5.6 %collective-permute-done.17.refs_3_ = f32[2,128,256]{2,1,0:T(8,128)S(1)} collective-permute-done((f32[2,128,256]{2,1,0:T(8,128)S(1)}, f32[2,128,256]{2,1,0:T(8,128)S(1)}, u32[]{:S(2)}, u32[]{:S(2)}) %collective-permute-start.17) | collective-permute-done | bytes 262176 | tf_op jit(solution)/shard_map/ppermute | solution.py:335
  83.9 2.7 %collective-permute-done.21.refs_1_ = f32[2,128,256]{2,1,0:T(8,128)S(1)} collective-permute-done((f32[2,128,256]{2,1,0:T(8,128)S(1)}, f32[2,128,256]{2,1,0:T(8,128)S(1)}, u32[]{:S(2)}, u32[]{:S(2)}) %collective-permute-start.21) | collective-permute-done | bytes 262176 | tf_op jit(solution)/shard_map/ppermute | solution.py:335
  87.3 3.7 %own_out.1 = (bf16[2048,512]{1,0:T(8,128)(2,1)}, f32[8,128]{1,0:T(8,128)S(1)}) custom-call(s32[4]{0:T(128)S(1)} %pad_add_fusion.meta, bf16[2048,512]{1,0:T(8,128)(2,1)S(1)} %bitcast.12, bf16[1024,256]{1,0:T(8,128)(2,1)S(1)} %get-tuple-element.88.refs_6_.refs_0_.refs_1_, bf16[1024,256]{1,0:T(8,128)(2,1)S(1)} %get-tuple-element.90.refs_7_.refs_1_.refs_2_, ...), custom_call_target="tpu_custom_call" | custom-call | flops 1 | bytes 200000 | tf_op jit(solution)/shard_map/own_out/pallas_call | solution.py:43
  92.4 2.1 %collective-permute-done.25.refs_2_ = f32[4,32,256]{2,1,0:T(8,128)S(1)} collective-permute-done((f32[4,32,256]{2,1,0:T(8,128)S(1)}, f32[4,32,256]{2,1,0:T(8,128)S(1)}, u32[]{:S(2)}, u32[]{:S(2)}) %collective-permute-start.25) | collective-permute-done | bytes 131104 | tf_op jit(solution)/shard_map/ppermute | solution.py:347
  94.6 2.1 %collective-permute-start.29 = (f32[2,32,256]{2,1,0:T(8,128)S(1)}, f32[2,32,256]{2,1,0:T(8,128)S(1)}, u32[]{:S(2)}, u32[]{:S(2)}) collective-permute-start(f32[2,32,256]{2,1,0:T(8,128)S(1)} %get-tuple-element.134), channel_id=1, source_target_pairs={{0,24},{2,26},{4,12},{6,14},{8,0},{10,2},{12,20},{14,22},{16,8},{1... | collective-permute-start | bytes 196616 | tf_op jit(solution)/shard_map/ppermute | solution.py:347
  96.7 4.6 %own_grad.1 = (bf16[2048,512]{1,0:T(8,128)(2,1)}, f32[8,128]{1,0:T(8,128)S(1)}) custom-call(s32[4]{0:T(128)S(1)} %pad_add_fusion.meta, bf16[2048,512]{1,0:T(8,128)(2,1)S(1)} %bitcast.13, bf16[2048,512]{1,0:T(8,128)(2,1)S(1)} %bitcast.19, bf16[1024,256]{1,0:T(8,128)(2,1)S(1)} %collective-permute-done.10.refs_7_.refs_3_.refs_2_, ...), custom_call_target="tpu_custom_call" | custom-call | flops 1 | bytes 200000 | tf_op jit(solution)/shard_map/own_grad/pallas_call | solution.py:43
  105.0 4.1 %collective-permute-done.30.refs_1_ = f32[6,32,256]{2,1,0:T(8,128)S(1)} collective-permute-done((f32[6,32,256]{2,1,0:T(8,128)S(1)}, f32[6,32,256]{2,1,0:T(8,128)S(1)}, u32[]{:S(2)}, u32[]{:S(2)}) %collective-permute-start.30) | collective-permute-done | bytes 196640 | tf_op jit(solution)/shard_map/ppermute | solution.py:351
  111.3 2.1 %collective-permute-start.33 = (bf16[6,32,256]{2,1,0:T(8,128)(2,1)S(1)}, bf16[6,32,256]{2,1,0:T(8,128)(2,1)S(1)}, u32[]{:S(2)}, u32[]{:S(2)}) collective-permute-start(bf16[6,32,256]{2,1,0:T(8,128)(2,1)S(1)} %get-tuple-element.140.refs_0_), channel_id=1, source_target_pairs={{0,24},{2,26},{4,12},{6,14},{8,0},{10,2},{12,20},{14,22},{16,8},{1... | collective-permute-start | bytes 294920 | tf_op jit(solution)/shard_map/ppermute | solution.py:347
  118.3 2.2 %collective-permute-done.22.refs_0_ = bf16[1024,256]{1,0:T(8,128)(2,1)S(1)} collective-permute-done((bf16[1024,256]{1,0:T(8,128)(2,1)S(1)}, bf16[1024,256]{1,0:T(8,128)(2,1)S(1)}, u32[]{:S(2)}, u32[]{:S(2)}) %collective-permute-start.22) | collective-permute-done | bytes 524320 | tf_op jit(solution)/shard_map/ppermute | solution.py:323
  121.8 1.8 %collective-permute-done.34.refs_1_ = bf16[6,128,256]{2,1,0:T(8,128)(2,1)S(1)} collective-permute-done((bf16[6,128,256]{2,1,0:T(8,128)(2,1)S(1)}, bf16[6,128,256]{2,1,0:T(8,128)(2,1)S(1)}, u32[]{:S(2)}, u32[]{:S(2)}) %collective-permute-start.34) | collective-permute-done | bytes 393248 | tf_op jit(solution)/shard_map/ppermute | solution.py:335
  124.3 8.9 %collective-permute-start.35 = (bf16[6,256,256]{2,1,0:T(8,128)(2,1)S(1)}, bf16[6,256,256]{2,1,0:T(8,128)(2,1)S(1)}, u32[]{:S(2)}, u32[]{:S(2)}) collective-permute-start(bf16[6,256,256]{2,1,0:T(8,128)(2,1)S(1)} %get-tuple-element.146.refs_0_), channel_id=1, source_target_pairs={{0,2},{2,0},{4,6},{6,4},{8,10},{10,8},{12,14},{14,12},{16,18},{18,... | collective-permute-start | bytes 2359304 | tf_op jit(solution)/shard_map/ppermute | solution.py:332
  133.2 1.9 %collective-permute-done.35.refs_1_ = bf16[6,256,256]{2,1,0:T(8,128)(2,1)S(1)} collective-permute-done((bf16[6,256,256]{2,1,0:T(8,128)(2,1)S(1)}, bf16[6,256,256]{2,1,0:T(8,128)(2,1)S(1)}, u32[]{:S(2)}, u32[]{:S(2)}) %collective-permute-start.35) | collective-permute-done | bytes 786464 | tf_op jit(solution)/shard_map/ppermute | solution.py:332
  135.1 2.5 %write_taps.1 = (f32[3,512,512]{2,1,0:T(8,128)}, f32[8,128]{1,0:T(8,128)}) custom-call(s32[4]{0:T(128)S(1)} %pad_add_fusion.meta, bf16[6,256,256]{2,1,0:T(8,128)(2,1)S(1)} %get-tuple-element.146.refs_0_, bf16[6,256,256]{2,1,0:T(8,128)(2,1)S(1)} %collective-permute-done.35.refs_1_, f32[8,128]{1,0:T(8,128)S(1)} %get-tuple-element.147.refs_2_), custom_call_target="tpu_custom_call" | custom-call | flops 1 | bytes 200000 | tf_op jit(solution)/shard_map/write_taps/pallas_call | solution.py:43
  (74 shorter events, 35.9 us)
Async XLA Ops:
  2.9 14.8 %collective-permute-start = (bf16[1024,256]{1,0:T(8,128)(2,1)S(1)}, bf16[1024,256]{1,0:T(8,128)(2,1)S(1)}, u32[]{:S(2)}, u32[]{:S(2)}) collective-permute-start(bf16[1024,256]{1,0:T(8,128)(2,1)S(1)} %get-tuple-element.76), channel_id=1, source_target_pairs={{0,4},{2,6},{4,0},{6,2},{8,12},{10,14},{12,8},{14,10},{16,20},{18,... | collective-permute-start | bytes 1572872 | tf_op jit(solution)/shard_map/ppermute | solution.py:323
  6.4 18.4 %collective-permute-start.4 = (bf16[1024,256]{1,0:T(8,128)(2,1)S(1)}, bf16[1024,256]{1,0:T(8,128)(2,1)S(1)}, u32[]{:S(2)}, u32[]{:S(2)}) collective-permute-start(bf16[1024,256]{1,0:T(8,128)(2,1)S(1)} %get-tuple-element.88.refs_6_.refs_0_.refs_1_), channel_id=1, source_target_pairs={{4,12},{6,14},{8,0},{10,2},{12,20},{14,22},{16,8},{18,10},{20,28},... | collective-permute-start | bytes 1572872 | tf_op jit(solution)/shard_map/ppermute | solution.py:326
  8.5 19.4 %collective-permute-start.1 = (bf16[1024,256]{1,0:T(8,128)(2,1)S(1)}, bf16[1024,256]{1,0:T(8,128)(2,1)S(1)}, u32[]{:S(2)}, u32[]{:S(2)}) collective-permute-start(bf16[1024,256]{1,0:T(8,128)(2,1)S(1)} %get-tuple-element.79), channel_id=1, source_target_pairs={{0,4},{2,6},{4,0},{6,2},{8,12},{10,14},{12,8},{14,10},{16,20},{18,... | collective-permute-start | bytes 1572872 | tf_op jit(solution)/shard_map/ppermute | solution.py:323
  10.8 21.3 %collective-permute-start.5 = (bf16[1024,256]{1,0:T(8,128)(2,1)S(1)}, bf16[1024,256]{1,0:T(8,128)(2,1)S(1)}, u32[]{:S(2)}, u32[]{:S(2)}) collective-permute-start(bf16[1024,256]{1,0:T(8,128)(2,1)S(1)} %get-tuple-element.90.refs_7_.refs_1_.refs_2_), channel_id=1, source_target_pairs={{4,12},{6,14},{8,0},{10,2},{12,20},{14,22},{16,8},{18,10},{20,28},... | collective-permute-start | bytes 1572872 | tf_op jit(solution)/shard_map/ppermute | solution.py:326
  19.8 19.4 %collective-permute-start.10 = (bf16[1024,256]{1,0:T(8,128)(2,1)S(1)}, bf16[1024,256]{1,0:T(8,128)(2,1)S(1)}, u32[]{:S(2)}, u32[]{:S(2)}) collective-permute-start(bf16[1024,256]{1,0:T(8,128)(2,1)S(1)} %get-tuple-element.96), channel_id=1, source_target_pairs={{0,4},{2,6},{4,0},{6,2},{8,12},{10,14},{12,8},{14,10},{16,20},{18,... | collective-permute-start | bytes 1572872 | tf_op jit(solution)/shard_map/ppermute | solution.py:323
  21.6 18.8 %collective-permute-start.6 = (bf16[1024,256]{1,0:T(8,128)(2,1)S(1)}, bf16[1024,256]{1,0:T(8,128)(2,1)S(1)}, u32[]{:S(2)}, u32[]{:S(2)}) collective-permute-start(bf16[1024,256]{1,0:T(8,128)(2,1)S(1)} %get-tuple-element.82.refs_2_.refs_3_), channel_id=1, source_target_pairs={{12,4},{14,6},{0,8},{2,10},{20,12},{22,14},{8,16},{10,18},{28,20},... | collective-permute-start | bytes 1572872 | tf_op jit(solution)/shard_map/ppermute | solution.py:329
  24.9 22.5 %collective-permute-start.11 = (bf16[1024,256]{1,0:T(8,128)(2,1)S(1)}, bf16[1024,256]{1,0:T(8,128)(2,1)S(1)}, u32[]{:S(2)}, u32[]{:S(2)}) collective-permute-start(bf16[1024,256]{1,0:T(8,128)(2,1)S(1)} %get-tuple-element.97), channel_id=1, source_target_pairs={{4,12},{6,14},{8,0},{10,2},{12,20},{14,22},{16,8},{18,10},{20,28},... | collective-permute-start | bytes 1572872 | tf_op jit(solution)/shard_map/ppermute | solution.py:326
  33.0 14.8 %collective-permute-start.8 = (bf16[1024,256]{1,0:T(8,128)(2,1)S(1)}, bf16[1024,256]{1,0:T(8,128)(2,1)S(1)}, u32[]{:S(2)}, u32[]{:S(2)}) collective-permute-start(bf16[1024,256]{1,0:T(8,128)(2,1)S(1)} %get-tuple-element.91.refs_3_.refs_4_), channel_id=1, source_target_pairs={{12,4},{14,6},{0,8},{2,10},{20,12},{22,14},{8,16},{10,18},{28,20},... | collective-permute-start | bytes 1572872 | tf_op jit(solution)/shard_map/ppermute | solution.py:329
  36.3 17.9 %collective-permute-start.14 = (bf16[1024,256]{1,0:T(8,128)(2,1)S(1)}, bf16[1024,256]{1,0:T(8,128)(2,1)S(1)}, u32[]{:S(2)}, u32[]{:S(2)}) collective-permute-start(bf16[1024,256]{1,0:T(8,128)(2,1)S(1)} %get-tuple-element.104), channel_id=1, source_target_pairs={{0,4},{2,6},{4,0},{6,2},{8,12},{10,14},{12,8},{14,10},{16,20},{18,... | collective-permute-start | bytes 1572872 | tf_op jit(solution)/shard_map/ppermute | solution.py:323
  39.2 15.1 %collective-permute-start.15 = (bf16[1024,256]{1,0:T(8,128)(2,1)S(1)}, bf16[1024,256]{1,0:T(8,128)(2,1)S(1)}, u32[]{:S(2)}, u32[]{:S(2)}) collective-permute-start(bf16[1024,256]{1,0:T(8,128)(2,1)S(1)} %get-tuple-element.105), channel_id=1, source_target_pairs={{4,12},{6,14},{8,0},{10,2},{12,20},{14,22},{16,8},{18,10},{20,28},... | collective-permute-start | bytes 1572872 | tf_op jit(solution)/shard_map/ppermute | solution.py:326
  40.5 15.8 %collective-permute-start.16 = (bf16[1024,256]{1,0:T(8,128)(2,1)S(1)}, bf16[1024,256]{1,0:T(8,128)(2,1)S(1)}, u32[]{:S(2)}, u32[]{:S(2)}) collective-permute-start(bf16[1024,256]{1,0:T(8,128)(2,1)S(1)} %collective-permute-done.10.refs_7_.refs_3_.refs_2_), channel_id=1, source_target_pairs={{12,4},{14,6},{0,8},{2,10},{20,12},{22,14},{8,16},{10,18},{28,20},... | collective-permute-start | bytes 1572872 | tf_op jit(solution)/shard_map/ppermute | solution.py:329
  47.4 47.2 %collective-permute-start.7 = (bf16[1024,512]{1,0:T(8,128)(2,1)S(1)}, bf16[1024,512]{1,0:T(8,128)(2,1)S(1)}, u32[]{:S(2)}, u32[]{:S(2)}) collective-permute-start(bf16[1024,512]{1,0:T(8,128)(2,1)S(1)} %get-tuple-element.93), channel_id=1, source_target_pairs={{0,4},{2,6},{4,0},{6,2},{8,12},{10,14},{12,8},{14,10},{16,20},{18,... | collective-permute-start | bytes 3145736 | tf_op jit(solution)/shard_map/ppermute | solution.py:323
  50.7 5.6 %collective-permute-start.12 = (f32[1,256,256]{2,1,0:T(8,128)S(1)}, f32[1,256,256]{2,1,0:T(8,128)S(1)}, u32[]{:S(2)}, u32[]{:S(2)}) collective-permute-start(f32[1,256,256]{2,1,0:T(8,128)S(1)} %get-tuple-element.100), channel_id=1, source_target_pairs={{0,2},{2,0},{4,6},{6,4},{8,10},{10,8},{12,14},{14,12},{16,18},{18,... | collective-permute-start | bytes 786440 | tf_op jit(solution)/shard_map/ppermute | solution.py:332
  59.8 9.1 %collective-permute-start.18 = (f32[1,256,256]{2,1,0:T(8,128)S(1)}, f32[1,256,256]{2,1,0:T(8,128)S(1)}, u32[]{:S(2)}, u32[]{:S(2)}) collective-permute-start(f32[1,256,256]{2,1,0:T(8,128)S(1)} %get-tuple-element.110), channel_id=1, source_target_pairs={{0,2},{2,0},{4,6},{6,4},{8,10},{10,8},{12,14},{14,12},{16,18},{18,... | collective-permute-start | bytes 786440 | tf_op jit(solution)/shard_map/ppermute | solution.py:332
  63.2 19.8 %collective-permute-start.20 = (bf16[1024,256]{1,0:T(8,128)(2,1)S(1)}, bf16[1024,256]{1,0:T(8,128)(2,1)S(1)}, u32[]{:S(2)}, u32[]{:S(2)}) collective-permute-start(bf16[1024,256]{1,0:T(8,128)(2,1)S(1)} %collective-permute-done.14.refs_5_.refs_7_.refs_4_.refs_3_), channel_id=1, source_target_pairs={{12,4},{14,6},{0,8},{2,10},{20,12},{22,14},{8,16},{10,18},{28,20},... | collective-permute-start | bytes 1572872 | tf_op jit(solution)/shard_map/ppermute | solution.py:329
  67.3 5.7 %collective-permute-start.19 = (f32[1,256,256]{2,1,0:T(8,128)S(1)}, f32[1,256,256]{2,1,0:T(8,128)S(1)}, u32[]{:S(2)}, u32[]{:S(2)}) collective-permute-start(f32[1,256,256]{2,1,0:T(8,128)S(1)} %get-tuple-element.112), channel_id=1, source_target_pairs={{0,2},{2,0},{4,6},{6,4},{8,10},{10,8},{12,14},{14,12},{16,18},{18,... | collective-permute-start | bytes 786440 | tf_op jit(solution)/shard_map/ppermute | solution.py:332
  67.7 7.7 %collective-permute-start.9 = (f32[2,128,256]{2,1,0:T(8,128)S(1)}, f32[2,128,256]{2,1,0:T(8,128)S(1)}, u32[]{:S(2)}, u32[]{:S(2)}) collective-permute-start(f32[2,128,256]{2,1,0:T(8,128)S(1)} %get-tuple-element.95), channel_id=1, source_target_pairs={{0,1},{1,0},{2,3},{3,2},{4,5},{5,4},{6,7},{7,6},{8,9},{9,8},{10,11... | collective-permute-start | bytes 786440 | tf_op jit(solution)/shard_map/ppermute | solution.py:335
  68.9 12.1 %collective-permute-start.17 = (f32[2,128,256]{2,1,0:T(8,128)S(1)}, f32[2,128,256]{2,1,0:T(8,128)S(1)}, u32[]{:S(2)}, u32[]{:S(2)}) collective-permute-start(f32[2,128,256]{2,1,0:T(8,128)S(1)} %get-tuple-element.107), channel_id=1, source_target_pairs={{0,1},{1,0},{2,3},{3,2},{4,5},{5,4},{6,7},{7,6},{8,9},{9,8},{10,11... | collective-permute-start | bytes 786440 | tf_op jit(solution)/shard_map/ppermute | solution.py:335
  73.6 13.0 %collective-permute-start.21 = (f32[2,128,256]{2,1,0:T(8,128)S(1)}, f32[2,128,256]{2,1,0:T(8,128)S(1)}, u32[]{:S(2)}, u32[]{:S(2)}) collective-permute-start(f32[2,128,256]{2,1,0:T(8,128)S(1)} %get-tuple-element.119), channel_id=1, source_target_pairs={{0,1},{1,0},{2,3},{3,2},{4,5},{5,4},{6,7},{7,6},{8,9},{9,8},{10,11... | collective-permute-start | bytes 786440 | tf_op jit(solution)/shard_map/ppermute | solution.py:335
  75.4 38.1 %collective-permute-start.23 = (bf16[1024,256]{1,0:T(8,128)(2,1)S(1)}, bf16[1024,256]{1,0:T(8,128)(2,1)S(1)}, u32[]{:S(2)}, u32[]{:S(2)}) collective-permute-start(bf16[1024,256]{1,0:T(8,128)(2,1)S(1)} %get-tuple-element.125), channel_id=1, source_target_pairs={{0,4},{2,6},{4,0},{6,2},{8,12},{10,14},{12,8},{14,10},{16,20},{18,... | collective-permute-start | bytes 1572872 | tf_op jit(solution)/shard_map/ppermute | solution.py:323
  81.6 10.0 %collective-permute-start.24 = (f32[4,32,256]{2,1,0:T(8,128)S(1)}, f32[4,32,256]{2,1,0:T(8,128)S(1)}, u32[]{:S(2)}, u32[]{:S(2)}) collective-permute-start(f32[4,32,256]{2,1,0:T(8,128)S(1)} %get-tuple-element.128), channel_id=1, source_target_pairs={{0,8},{2,10},{4,28},{6,30},{8,16},{10,18},{12,4},{14,6},{16,24},{1... | collective-permute-start | bytes 393224 | tf_op jit(solution)/shard_map/ppermute | solution.py:347
  83.0 11.6 %collective-permute-start.25 = (f32[4,32,256]{2,1,0:T(8,128)S(1)}, f32[4,32,256]{2,1,0:T(8,128)S(1)}, u32[]{:S(2)}, u32[]{:S(2)}) collective-permute-start(f32[4,32,256]{2,1,0:T(8,128)S(1)} %get-tuple-element.129), channel_id=1, source_target_pairs={{0,16},{2,18},{4,20},{6,22},{8,24},{10,26},{12,28},{14,30},{16,0},... | collective-permute-start | bytes 393224 | tf_op jit(solution)/shard_map/ppermute | solution.py:347
  86.6 16.2 %collective-permute-start.26 = (f32[4,32,256]{2,1,0:T(8,128)S(1)}, f32[4,32,256]{2,1,0:T(8,128)S(1)}, u32[]{:S(2)}, u32[]{:S(2)}) collective-permute-start(f32[4,32,256]{2,1,0:T(8,128)S(1)} %get-tuple-element.130), channel_id=1, source_target_pairs={{0,24},{2,26},{4,12},{6,14},{8,0},{10,2},{12,20},{14,22},{16,8},{1... | collective-permute-start | bytes 393224 | tf_op jit(solution)/shard_map/ppermute | solution.py:347
  91.6 11.2 %collective-permute-start.27 = (f32[2,32,256]{2,1,0:T(8,128)S(1)}, f32[2,32,256]{2,1,0:T(8,128)S(1)}, u32[]{:S(2)}, u32[]{:S(2)}) collective-permute-start(f32[2,32,256]{2,1,0:T(8,128)S(1)} %get-tuple-element.132), channel_id=1, source_target_pairs={{0,8},{2,10},{4,28},{6,30},{8,16},{10,18},{12,4},{14,6},{16,24},{1... | collective-permute-start | bytes 196616 | tf_op jit(solution)/shard_map/ppermute | solution.py:347
  94.6 8.3 %collective-permute-start.28 = (f32[2,32,256]{2,1,0:T(8,128)S(1)}, f32[2,32,256]{2,1,0:T(8,128)S(1)}, u32[]{:S(2)}, u32[]{:S(2)}) collective-permute-start(f32[2,32,256]{2,1,0:T(8,128)S(1)} %get-tuple-element.133), channel_id=1, source_target_pairs={{0,16},{2,18},{4,20},{6,22},{8,24},{10,26},{12,28},{14,30},{16,0},... | collective-permute-start | bytes 196616 | tf_op jit(solution)/shard_map/ppermute | solution.py:347
  94.6 8.3 %collective-permute-start.29 = (f32[2,32,256]{2,1,0:T(8,128)S(1)}, f32[2,32,256]{2,1,0:T(8,128)S(1)}, u32[]{:S(2)}, u32[]{:S(2)}) collective-permute-start(f32[2,32,256]{2,1,0:T(8,128)S(1)} %get-tuple-element.134), channel_id=1, source_target_pairs={{0,24},{2,26},{4,12},{6,14},{8,0},{10,2},{12,20},{14,22},{16,8},{1... | collective-permute-start | bytes 196616 | tf_op jit(solution)/shard_map/ppermute | solution.py:347
  103.4 5.6 %collective-permute-start.30 = (f32[6,32,256]{2,1,0:T(8,128)S(1)}, f32[6,32,256]{2,1,0:T(8,128)S(1)}, u32[]{:S(2)}, u32[]{:S(2)}) collective-permute-start(f32[6,32,256]{2,1,0:T(8,128)S(1)} %get-tuple-element.136.refs_0_), channel_id=1, source_target_pairs={{0,12},{2,14},{4,8},{6,10},{8,4},{10,6},{12,0},{14,2},{16,28},{18,... | collective-permute-start | bytes 589832 | tf_op jit(solution)/shard_map/ppermute | solution.py:351
  104.6 15.9 %collective-permute-start.22 = (bf16[1024,256]{1,0:T(8,128)(2,1)S(1)}, bf16[1024,256]{1,0:T(8,128)(2,1)S(1)}, u32[]{:S(2)}, u32[]{:S(2)}) collective-permute-start(bf16[1024,256]{1,0:T(8,128)(2,1)S(1)} %get-tuple-element.124), channel_id=1, source_target_pairs={{0,4},{2,6},{4,0},{6,2},{8,12},{10,14},{12,8},{14,10},{16,20},{18,... | collective-permute-start | bytes 1572872 | tf_op jit(solution)/shard_map/ppermute | solution.py:323
  109.6 5.5 %collective-permute-start.31 = (bf16[6,32,256]{2,1,0:T(8,128)(2,1)S(1)}, bf16[6,32,256]{2,1,0:T(8,128)(2,1)S(1)}, u32[]{:S(2)}, u32[]{:S(2)}) collective-permute-start(bf16[6,32,256]{2,1,0:T(8,128)(2,1)S(1)} %get-tuple-element.140.refs_0_), channel_id=1, source_target_pairs={{0,8},{2,10},{4,28},{6,30},{8,16},{10,18},{12,4},{14,6},{16,24},{1... | collective-permute-start | bytes 294920 | tf_op jit(solution)/shard_map/ppermute | solution.py:347
  109.9 6.5 %collective-permute-start.32 = (bf16[6,32,256]{2,1,0:T(8,128)(2,1)S(1)}, bf16[6,32,256]{2,1,0:T(8,128)(2,1)S(1)}, u32[]{:S(2)}, u32[]{:S(2)}) collective-permute-start(bf16[6,32,256]{2,1,0:T(8,128)(2,1)S(1)} %get-tuple-element.140.refs_0_), channel_id=1, source_target_pairs={{0,16},{2,18},{4,20},{6,22},{8,24},{10,26},{12,28},{14,30},{16,0},... | collective-permute-start | bytes 294920 | tf_op jit(solution)/shard_map/ppermute | solution.py:347
  117.0 6.7 %collective-permute-start.34 = (bf16[6,128,256]{2,1,0:T(8,128)(2,1)S(1)}, bf16[6,128,256]{2,1,0:T(8,128)(2,1)S(1)}, u32[]{:S(2)}, u32[]{:S(2)}) collective-permute-start(bf16[6,128,256]{2,1,0:T(8,128)(2,1)S(1)} %get-tuple-element.144.refs_0_), channel_id=1, source_target_pairs={{0,1},{1,0},{2,3},{3,2},{4,5},{5,4},{6,7},{7,6},{8,9},{9,8},{10,11... | collective-permute-start | bytes 1179656 | tf_op jit(solution)/shard_map/ppermute | solution.py:335
  124.3 10.8 %collective-permute-start.35 = (bf16[6,256,256]{2,1,0:T(8,128)(2,1)S(1)}, bf16[6,256,256]{2,1,0:T(8,128)(2,1)S(1)}, u32[]{:S(2)}, u32[]{:S(2)}) collective-permute-start(bf16[6,256,256]{2,1,0:T(8,128)(2,1)S(1)} %get-tuple-element.146.refs_0_), channel_id=1, source_target_pairs={{0,2},{2,0},{4,6},{6,4},{8,10},{10,8},{12,14},{14,12},{16,18},{18,... | collective-permute-start | bytes 2359304 | tf_op jit(solution)/shard_map/ppermute | solution.py:332
  (8 other events, 64.5 us)

commit v3 on v2

v3 whole, which is shorter than its diff:
```python
import functools

import jax
import jax.numpy as jnp
from jax import lax
from jax.experimental import pallas as pl
from jax.experimental.pallas import tpu as pltpu
from jax.sharding import PartitionSpec as P

DILATION_BINS = 4096
BF16, F32 = jnp.bfloat16, jnp.float32
VMEM_BYTES = 40 * 1024 * 1024
SIDE, CORE, DP, ALONG, ALONG_BITS = range(5)
HBM = pl.BlockSpec(memory_space=pltpu.HBM)
WHOLE = pl.BlockSpec(memory_space=pltpu.VMEM)


def shape_of(shape, dtype):
    return jax.ShapeDtypeStruct(shape, dtype)


TOKEN = jax.ShapeDtypeStruct((8, 128), F32)


class Device:
    def __init__(self, meta):
        self.meta, self.token = meta, None


def call(
    body, device, operands, in_specs, outs, out_specs, grid=(), scratch=(), aliases=None, name=None, after=()
):
    first = device.token is None
    n_in, single = len(operands), not isinstance(outs, list)
    outs, out_specs = ([outs], [out_specs]) if single else (outs, out_specs)
    n_out = len(outs)
    tokens = [*after] if first else [device.token, *after]

    def chained(meta, *refs):
        rest = refs[n_in + len(tokens) :]
        body(meta, *refs[:n_in], *rest[:n_out], *rest[n_out + 1 :])

    results = pl.pallas_call(
        chained,
        grid_spec=pltpu.PrefetchScalarGridSpec(
            num_scalar_prefetch=1, grid=grid, in_specs=[*in_specs, *[HBM] * len(tokens)], out_specs=[*out_specs, HBM],
            scratch_shapes=list(scratch),
        ),
        out_shape=[*outs, TOKEN],
        input_output_aliases=aliases or {},
        compiler_params=pltpu.CompilerParams(vmem_limit_bytes=VMEM_BYTES),
        cost_estimate=pl.CostEstimate(flops=1, bytes_accessed=200_000, transcendentals=0),
        name=name,
    )(device.meta, *operands, *tokens)
    device.token = results[-1]
    return results[0] if single else results[:-1]


def gelu_parts(x):
    k = 0.7978845608028654
    square = x * x
    t = jnp.tanh(k * (x * (1.0 + 0.044715 * square)))
    return t, square, k


def gelu(x):
    t, _, _ = gelu_parts(x)
    return x * (0.5 * (1.0 + t))


def gelu_and_slope(x):
    t, square, k = gelu_parts(x)
    cdf = 0.5 * (1.0 + t)
    slope = cdf + 0.5 * x * (1.0 - t * t) * (k + (3 * 0.044715 * k) * square)
    return x * cdf, slope


def mm(left, right):
    return lax.dot_general(left, right, (((1,), (0,)), ((), ())), preferred_element_type=F32)


def mm_back(left, right):
    return lax.dot_general(left, right, (((1,), (1,)), ((), ())), preferred_element_type=F32)


def mm_outer(left, right):
    return lax.dot_general(left, right, (((0,), (0,)), ((), ())), preferred_element_type=F32)


def cut_body(plan, n_in, meta, *refs):
    ins, outs, sems = refs[:n_in], refs[n_in:-1], refs[-1]
    copies = []
    for n, (which, own, col, rows, cols) in enumerate(plan):
        start = (meta[SIDE] if own else 1 - meta[SIDE]) * rows
        window = ins[which].at[pl.ds(pl.multiple_of(start, rows), rows), pl.ds(col, cols)]
        copies.append(pltpu.make_async_copy(window, outs[n], sems.at[n]))
    for copy in copies:
        copy.start()
    for copy in copies:
        copy.wait()


def cut(device, operands, plan, name):
    outs = [shape_of((rows, cols), BF16) for _, _, _, rows, cols in plan]
    return call(
        functools.partial(cut_body, plan, len(operands)), device, operands, [HBM] * len(operands), outs,
        [HBM] * len(plan), scratch=[pltpu.SemaphoreType.DMA((len(plan),))], name=name,
    )


def split_into(total, position, count, keep, sends):
    size = total.shape[1] // count
    for shift, ref in enumerate((keep, *sends)):
        there = lax.rem(position + shift, count)
        ref[...] = total[:, pl.ds(pl.multiple_of(there * size, size), size), :].astype(ref.dtype)


def mid_body(x, u, total):
    @pl.when(pl.program_id(0) == 0)
    def _():
        total[...] = jnp.zeros_like(total)

    cols = total.shape[2]
    product = mm_outer(gelu(x[...].astype(F32)).astype(BF16), u[...])
    for part in range(2):
        total[part] += product[:, part * cols : (part + 1) * cols]


def reduce_body(sizes, n_out, place, swap_from, meta, *refs):
    ins, outs, total = refs[: sum(sizes)], refs[sum(sizes) : -1], refs[-1]
    first = lead = 0
    for size in sizes:
        value = ins[first][...].astype(F32)
        for ref in ins[first + 1 : first + size]:
            value = value + ref[...].astype(F32)
        total[lead : lead + value.shape[0]] = value
        first, lead = first + size, lead + value.shape[0]
    for part in range(swap_from, lead, 2):
        pair = total[part : part + 2]
        for n in range(2):
            total[part + n] = jnp.where(meta[SIDE] == 0, pair[n], pair[1 - n])
    if n_out > 1:
        split_into(total, meta[place], n_out, outs[0], outs[1:])
    else:
        outs[0][...] = total[...].astype(outs[0].dtype)


def reduce(device, groups, n_out=1, place=None, swap_from=None, dtype=F32, name=None, after=()):
    _, rows, cols = groups[0][0].shape
    k = sum(group[0].shape[0] for group in groups)
    values = [value for group in groups for value in group]
    dtypes = [dtype] if n_out == 1 else [F32] + [dtype] * (n_out - 1)
    outs = [shape_of((k, rows // n_out, cols), each) for each in dtypes]
    sizes = [len(group) for group in groups]
    body = functools.partial(reduce_body, sizes, n_out, place, k if swap_from is None else swap_from)
    return call(
        body, device, values, [WHOLE] * len(values), outs, [WHOLE] * n_out,
        scratch=[pltpu.VMEM((k, rows, cols), F32)], name=name, after=after,
    )


def gather_body(count, place, meta, *refs):
    ins, out = refs[:count], refs[count]
    size = ins[0].shape[1]
    for shift, ref in enumerate(ins):
        source = lax.rem(meta[place] + count - shift, count)
        out[:, pl.ds(pl.multiple_of(source * size, size), size), :] = ref[...]


def gather(device, values, place, name=None):
    count = len(values)
    k, rows, cols = values[0].shape
    return call(
        functools.partial(gather_body, count, place), device, values, [WHOLE] * count,
        shape_of((k, rows * count, cols), BF16), WHOLE, name=name,
    )


def write_taps_body(count, targets, aliased, meta, *refs):
    ins = refs[:count]
    out, wide, sems = refs[count + aliased :]
    size = ins[0].shape[1]
    for shift, ref in enumerate(ins):
        source = lax.rem(meta[CORE] + count - shift, count)
        wide[:, pl.ds(pl.multiple_of(source * size, size), size), :] = ref[...].astype(F32)
    copies = []
    for n, (tap, col) in enumerate(targets):
        window = out.at[tap, :, pl.ds(col, wide.shape[2])]
        copies.append(pltpu.make_async_copy(wide.at[n], window, sems.at[n]))
    for copy in copies:
        copy.start()
    for copy in copies:
        copy.wait()


def write_taps(device, values, targets, shape, buffer, name):
    count = len(values)
    k, rows, cols = values[0].shape
    extra = [] if buffer is None else [buffer]
    return call(
        functools.partial(write_taps_body, count, targets, len(extra)), device, (*values, *extra),
        [WHOLE] * count + [HBM] * len(extra), shape_of(shape, F32), HBM,
        scratch=[pltpu.VMEM((k, rows * count, cols), F32), pltpu.SemaphoreType.DMA((k,))],
        aliases={1 + count: 0} if extra else None, name=name,
    )


def act_body(meta, x, *acts):
    act = gelu(x[...].astype(F32)).astype(BF16)
    cols = acts[0].shape[1]
    for n, ref in enumerate(acts):
        ref[...] = act[:, n * cols : (n + 1) * cols]


def mm_parts(lefts, weight):
    cols = lefts[0].shape[1]
    return sum(mm(left[...], weight[0, n * cols : (n + 1) * cols]) for n, left in enumerate(lefts))


def mm_back_parts(lefts, weight):
    cols = lefts[0].shape[1]
    return sum(mm_back(left[...], weight[0, :, n * cols : (n + 1) * cols]) for n, left in enumerate(lefts))


def oth_out_body(meta, x0, x1, oth0, oth1, far0, far1, own0, own1, w_near, w_mid, w_far, out):
    cols = x0.shape[1]
    conv = mm_parts((oth0, oth1), w_mid) + mm_parts((far0, far1), w_near) + mm_parts((own0, own1), w_far)
    out[:, :cols] = (x0[...].astype(F32) + conv[:, :cols]).astype(BF16)
    out[:, cols:] = (x1[...].astype(F32) + conv[:, cols:]).astype(BF16)


def own_out_body(meta, x, own0, own1, oth0, oth1, far0, far1, w_near, w_mid, w_far, out):
    conv = mm_parts((own0, own1), w_mid) + mm_parts((oth0, oth1), w_near) + mm_parts((far0, far1), w_far)
    out[...] = (x[...].astype(F32) + conv).astype(BF16)


def outer_body(
    steps, count, n_extra, meta, own0, own1, oth0, oth1, far0, far1, own_far0, own_far1, u_own, u_oth, *refs
):
    extra, (keep, send, total) = refs[:n_extra], refs[n_extra:]
    i = pl.program_id(0)

    @pl.when(i == 0)
    def _():
        total[...] = jnp.zeros_like(total)

    cols = own0.shape[1]
    for n, (own, oth, far, own_far) in enumerate(((own0, oth0, far0, own_far0), (own1, oth1, far1, own_far1))):
        rows = slice(n * cols, (n + 1) * cols)
        total[0, rows] += mm_outer(own[...], u_oth[...]) + mm_outer(own_far[...], u_own[...])
        total[1, rows] += mm_outer(far[...], u_oth[...]) + mm_outer(oth[...], u_own[...])

    @pl.when(i == steps - 1)
    def _():
        lead = 0
        for part in (*extra, total):
            window = pl.ds(lead, part.shape[0])
            split_into(part, meta[CORE], count, keep.at[window], [send.at[window]])
            lead += part.shape[0]


def oth_grad_body(meta, x0, x1, u_own, oth0, oth1, far, w_near, w_mid, w_far, grad):
    cols = oth0.shape[1]
    grad_act = mm_back(u_own[...], w_near[0]) + mm_back_parts((oth0, oth1), w_mid) + mm_back(far[...], w_far[0])
    for n, (x, u) in enumerate(((x0, oth0), (x1, oth1))):
        part = slice(n * cols, (n + 1) * cols)
        _, slope = gelu_and_slope(x[...].astype(F32))
        grad[:, part] = (u[...].astype(F32) + slope * grad_act[:, part]).astype(BF16)


def own_grad_body(meta, x, u_own, oth0, oth1, far0, far1, w_near, w_mid, w_far, grad):
    _, slope = gelu_and_slope(x[...].astype(F32))
    u = u_own[...]
    grad_act = mm_back(u, w_mid[0]) + mm_back_parts((oth0, oth1), w_far) + mm_back_parts((far0, far1), w_near)
    grad[...] = (u.astype(F32) + slope * grad_act).astype(BF16)


def place_body(row, col, meta, part, buffer, out, sem):
    rows, cols = part.shape
    start = pl.multiple_of((1 - meta[SIDE]) * (buffer.shape[0] // 2), rows) + row
    copy = pltpu.make_async_copy(part, out.at[pl.ds(pl.multiple_of(start, 16), rows), pl.ds(col, cols)], sem)
    copy.start()
    copy.wait()


def place(device, part, buffer, row, col, name):
    return call(
        functools.partial(place_body, row, col), device, (part, buffer), [HBM, HBM],
        shape_of(buffer.shape, buffer.dtype), HBM, scratch=[pltpu.SemaphoreType.DMA], aliases={2: 0}, name=name,
    )


def per_device(genome, conv_weight, upstream):
    genome, upstream = genome[0], upstream[0]
    bins, chans = genome.shape
    half, cols = bins // 2, chans // 2
    block = half // 4
    steps = half // block
    count = lax.axis_size("seq")
    index = lax.axis_index("seq")
    tap = DILATION_BINS // bins
    span = 2 * tap
    dp_count, along_count = lax.axis_size("dp"), count // span
    side, along = lax.rem(index // tap, 2), index // span
    if along_count % 2 == 0:
        along = along ^ side
    def is_even(i):
        return (i // tap) % 2 == 0

    swap_pairs = [(i, i + tap if is_even(i) else i - tap) for i in range(count)]
    outer_pairs = [(i, i - span if is_even(i) else i + span) for i in range(count)]
    outer_pairs = [(i, j) for i, j in outer_pairs if 0 <= j < count]
    inner_pairs = [(j, i) for i, j in outer_pairs]

    def swap(value):
        return lax.ppermute(value, "seq", swap_pairs)

    def outward(value):
        return lax.ppermute(value, "seq", outer_pairs)

    def inward(value):
        return lax.ppermute(value, "seq", inner_pairs)

    def to_core(value, shift=1):
        return lax.ppermute(value, "seq", [(i, i - i % tap + (i % tap + shift) % tap) for i in range(count)])

    def to_dp(value, shift=1):
        return lax.ppermute(value, "dp", [(i, (i + shift) % dp_count) for i in range(dp_count)])

    flip = 1 if along_count % 2 == 0 else 0
    bits = (along_count - 1).bit_length()
    halving = along_count == 1 << bits

    def reversed_bits(value):
        return sum(((value >> n) & 1) << (bits - 1 - n) for n in range(bits)) if halving else value

    def place_along(i):
        return reversed_bits((i // span) ^ (flip * ((i // tap) % 2)))

    def device_at(i, side, position):
        return (reversed_bits(position) ^ (flip * side)) * span + side * tap + i % tap

    def to_along(value, move):
        pairs = [(i, device_at(i, (i // tap) % 2, move(place_along(i)))) for i in range(count)]
        return lax.ppermute(value, "seq", pairs)

    def to_side(value):
        pairs = [(i, device_at(i, 1 - (i // tap) % 2, place_along(i))) for i in range(count)]
        return lax.ppermute(value, "seq", pairs)

    rows_spec = pl.BlockSpec((block, chans), lambda i, s: (i, 0))
    own_spec = pl.BlockSpec((block, chans), lambda i, s: (s[SIDE] * steps + i, 0))
    w_near = pl.BlockSpec((1, chans, chans), lambda i, s: (2 - 2 * s[SIDE], 0, 0))
    w_mid = pl.BlockSpec((1, chans, chans), lambda i, s: (1, 0, 0))
    w_far = pl.BlockSpec((1, chans, chans), lambda i, s: (2 * s[SIDE], 0, 0))
    half_shape, whole_shape = shape_of((half, chans), BF16), shape_of((bins, chans), BF16)
    along = reversed_bits(along)
    along_bits = [(along >> n) & 1 for n in reversed(range(bits))]
    meta = jnp.stack([side, lax.rem(index, tap), lax.axis_index("dp"), along, *along_bits]).astype(jnp.int32)
    device = Device(meta)

    part_spec = pl.BlockSpec((block, cols), lambda i, s: (i, 0))
    weights, weight_specs = (conv_weight,) * 3, [w_near, w_mid, w_far]

    staged = halving and (chans // tap // dp_count) % (16 * along_count) == 0

    def core_stage(parts, name, after=()):
        keep, send = parts
        keep, send = reduce(device, [[keep, to_core(send)]], dp_count, DP, dtype=BF16, name=name + "_core", after=after)
        return [keep, to_dp(send)]

    def along_stage(groups, step, after=()):
        if not staged:
            return reduce(device, groups, name=f"along{step}", after=after)
        keep, send = reduce(device, groups, 2, ALONG_BITS + step, dtype=BF16, name=f"along{step}", after=after)
        return [keep, to_along(send, lambda position: position ^ (1 << (bits - 1 - step)))]

    def side_stage(groups, after=()):
        (total,) = reduce(device, groups, swap_from=2, name="last", after=after)
        if not staged:
            together = [[i + span * j for j in range(along_count)] for i in range(span)]
            total = lax.psum(total, "seq", axis_index_groups=together)
        return [total, to_side(total)]

    def round_and_spread(parts, after=()):
        (total,) = reduce(device, [parts], dtype=BF16, name="side", after=after)
        moves = [lambda position, s=s: (position + s) % along_count for s in range(1, along_count)]
        return [total] + [to_along(total, move) for move in moves if staged]

    def gather_along(parts):
        total = gather(device, parts, ALONG, "all_along") if staged else parts[0]
        return [total] + [to_dp(total, s) for s in range(1, dp_count)]

    def gather_dp(parts):
        total = gather(device, parts, DP, "all_dp")
        return [total] + [to_core(total, s) for s in range(1, tap)]

    def outer_taps(k, extra=(), dtype=F32):
        u_own_spec = pl.BlockSpec((block, cols), lambda i, s: (i, k))
        piece = (2 + sum(part.shape[0] for part in extra), chans // tap, cols)
        return call(
            functools.partial(outer_body, steps, tap, len(extra)), device,
            (*a_own, *a_oth, *a_oth_far, *a_own_far, u_own, u_oth[k], *extra),
            [*[part_spec] * 8, u_own_spec, part_spec, *[WHOLE] * len(extra)], [shape_of(piece, F32), shape_of(piece, dtype)],
            [pl.BlockSpec(piece, lambda i, s: (0, 0, 0))] * 2, grid=(steps,),
            scratch=[pltpu.VMEM((2, chans, cols), F32)], name=f"outer_taps{k}",
        )

    def oth_act(x, name):
        return call(
            act_body, device, (x,), [part_spec], shape_of((half, cols), BF16), part_spec, grid=(steps,), name=name
        )

    (x_send0,) = cut(device, (genome,), [(0, False, 0, half, cols)], "cut_first")
    x_oth0 = swap(x_send0)
    a_own = call(
        act_body, device, (genome,), [own_spec], [shape_of((half, cols), BF16)] * 2, [part_spec] * 2, grid=(steps,),
        name="own_act",
    )
    a_oth_far = [outward(part) for part in a_own]
    x_send1, u_send0, u_send1, u_own = cut(
        device, (genome, upstream),
        [(0, False, cols, half, cols), (1, False, 0, half, cols), (1, False, cols, half, cols), (1, True, 0, half, chans)],
        "cut_rest",
    )
    x_oth1, u_oth = swap(x_send1), [swap(u_send0), swap(u_send1)]
    u_oth_far = outward(u_own)

    mid = call(
        lambda meta, *refs: mid_body(*refs), device, (genome, upstream), [rows_spec] * 2,
        shape_of((2, chans, cols), F32), pl.BlockSpec((2, chans, cols), lambda i, s: (0, 0, 0)), grid=(2 * steps,),
        name="mid_tap",
    )
    a_oth0 = oth_act(x_oth0, "oth_act0")
    a_own_far0 = inward(a_oth0)
    a_oth1 = oth_act(x_oth1, "oth_act1")
    a_own_far1 = inward(a_oth1)
    a_oth, a_own_far = [a_oth0, a_oth1], [a_own_far0, a_own_far1]
    out = call(
        oth_out_body, device, (x_oth0, x_oth1, *a_oth, *a_oth_far, *a_own, *weights),
        [*[part_spec] * 8, *weight_specs], half_shape, rows_spec, grid=(steps,), name="oth_out", after=(a_own_far[0],),
    )
    out = swap(out)
    outer0 = outer_taps(0, [mid], BF16)
    u_own_far0 = inward(u_oth[0])
    outer1 = outer_taps(1)
    u_own_far1 = inward(u_oth[1])
    outer0 = core_stage(outer0, "outer0", after=(u_own_far0,))
    outer1 = core_stage(outer1, "outer1")
    grad = call(
        oth_grad_body, device, (x_oth0, x_oth1, u_own, *u_oth, u_oth_far, *weights),
        [part_spec, part_spec, rows_spec, part_spec, part_spec, rows_spec, *weight_specs], half_shape, rows_spec,
        grid=(steps,), name="oth_grad",
    )
    grad = swap(grad)
    output = call(
        own_out_body, device, (genome, *a_own, *a_oth, *a_own_far, *weights),
        [own_spec, *[part_spec] * 6, *weight_specs], whole_shape, own_spec, grid=(steps,), name="own_out",
    )
    parts = along_stage([outer0, outer1], 0)
    grad_genome = call(
        own_grad_body, device, (genome, u_own, *u_oth, u_own_far0, u_own_far1, *weights),
        [own_spec, rows_spec, *[part_spec] * 4, *weight_specs], whole_shape, own_spec, grid=(steps,), name="own_grad",
    )
    parts = along_stage([parts], 1)
    output = place(device, out, output, 0, 0, "place_out")
    parts = side_stage([parts])
    parts = round_and_spread(parts)
    parts = gather_along(parts)
    grad_genome = place(device, grad, grad_genome, 0, 0, "place_grad")
    parts = gather_dp(parts)
    targets = [(1, 0), (1, cols), (0, 0), (2, 0), (0, cols), (2, cols)]
    grad_weight = write_taps(device, parts, targets, conv_weight.shape, None, "write_taps")
    return (output[None], grad_genome[None], grad_weight)


def solution(mesh):
    return jax.shard_map(
        per_device,
        mesh=mesh,
        in_specs=(P("dp", "seq", None), P(), P("dp", "seq", None)),
        out_specs=(P("dp", "seq", None), P("dp", "seq", None), P()),
        check_vma=False,
    )
```

time: 138 us -> 119 us (0.86)
  starting transfers between devices: 60.7 us -> 47.5 us
  waiting for transfers between devices: 32.7 us -> 28.7 us
  Pallas kernels: 41.5 us -> 39.8 us
    ppermute x4 -> x3, waiting for transfers between devices: 10.7 us -> 0.06 us  [to_dp(): lax.ppermute(value, 'dp', [(i, (i + shift) % dp_count) for i in range(dp_...]
    ppermute x7 -> x6, waiting for transfers between devices: 6.2 us -> 13.3 us  [swap(): return lax.ppermute(value, 'seq', swap_pairs)]
    ppermute x7 -> x3, starting transfers between devices: 18.9 us -> 13.1 us  [to_core(): lax.ppermute(value, 'seq', [(i, i - i % tap + (i % tap + shift) % tap) fo...]
    ppermute x4 -> x3, waiting for transfers between devices: 4.09 us -> 0.77 us  [outward(): return lax.ppermute(value, 'seq', outer_pairs)]
    ppermute x9 -> x5, starting transfers between devices: 9.76 us -> 6.54 us  [to_along(): return lax.ppermute(value, 'seq', pairs)]
    ppermute x9 -> x5, waiting for transfers between devices: 3.72 us -> 6.63 us  [to_along(): return lax.ppermute(value, 'seq', pairs)]
    ppermute x1, waiting for transfers between devices: 4.05 us -> 6.1 us  [to_side(): return lax.ppermute(value, 'seq', pairs)]
    ppermute x4, waiting for transfers between devices: 1.99 us -> 0.01 us  [inward(): return lax.ppermute(value, 'seq', inner_pairs)]
  transfers between devices with their start and end apart: 36 -> 25, of which waited for: 14 -> 10; matrix products, arithmetic and copies ran while one was open for 0% -> 0% of each run, Pallas kernels for 28% -> 30%
where the time goes in v3:
time: 119 us
  starting transfers between devices  47.5 us (40%)
  Pallas kernels  39.8 us (33%)
  waiting for transfers between devices  28.7 us (24%)
  local copies, waits for them, and re-layouts  1.69 us (1%)
    pallas_call x23, Pallas kernels, call(): pl.pallas_call(chained, grid_spec=pltpu.PrefetchScalarGridSpec(num_scalar...  39.8 us
    ppermute x6, waiting for transfers between devices, swap(): return lax.ppermute(value, 'seq', swap_pairs)  13.3 us
    ppermute x4, starting transfers between devices, inward(): return lax.ppermute(value, 'seq', inner_pairs)  13.2 us
    ppermute x3, starting transfers between devices, to_core(): lax.ppermute(value, 'seq', [(i, i - i % tap + (i % tap + shift) % tap) fo...  13.1 us
    ppermute x6, starting transfers between devices, swap(): return lax.ppermute(value, 'seq', swap_pairs)  7.88 us
    ppermute x5, waiting for transfers between devices, to_along(): return lax.ppermute(value, 'seq', pairs)  6.63 us
    ppermute x5, starting transfers between devices, to_along(): return lax.ppermute(value, 'seq', pairs)  6.54 us
    ppermute x1, waiting for transfers between devices, to_side(): return lax.ppermute(value, 'seq', pairs)  6.1 us
  transfers between devices with their start and end apart: 25, of which 10 were waited for; matrix products, arithmetic and copies ran while one was open for 0% of the time, Pallas kernels for 30%

profile of v3, /device:TPU:1, one launch (start us, length us, event | category | flops | bytes accessed | tf_op | source)
XLA Modules:
  0.0 118.7 jit_solution(13745447247991772057)
XLA Ops:
  0.7 1.6 %copy-done.1 = bf16[1,2048,512]{2,1,0:T(8,128)(2,1)S(1)} copy-done((bf16[1,2048,512]{2,1,0:T(8,128)(2,1)S(1)}, bf16[1,2048,512]{2,1,0:T(8,128)(2,1)}, u32[]{:S(2)}) %copy-start.1) | copy-done | bytes 2097176
  2.9 2.1 %collective-permute-start = (bf16[1024,256]{1,0:T(8,128)(2,1)S(1)}, bf16[1024,256]{1,0:T(8,128)(2,1)S(1)}, u32[]{:S(2)}, u32[]{:S(2)}) collective-permute-start(bf16[1024,256]{1,0:T(8,128)(2,1)S(1)} %get-tuple-element.58), channel_id=1, source_target_pairs={{0,4},{2,6},{4,0},{6,2},{8,12},{10,14},{12,8},{14,10},{16,20},{18,... | collective-permute-start | bytes 1572872 | tf_op jit(solution)/shard_map/ppermute | solution.py:316
  5.1 1.4 %own_act.1 = (bf16[1024,256]{1,0:T(8,128)(2,1)S(1)}, bf16[1024,256]{1,0:T(8,128)(2,1)S(1)}, f32[8,128]{1,0:T(8,128)S(1)}) custom-call(s32[6]{0:T(128)S(1)} %stack.27.meta, bf16[2048,512]{1,0:T(8,128)(2,1)S(1)} %bitcast.11, f32[8,128]{1,0:T(8,128)S(1)} %get-tuple-element.59.refs_1_), custom_call_target="tpu_custom_call" | custom-call | flops 1 | bytes 200000 | tf_op jit(solution)/shard_map/own_act/pallas_call | solution.py:43
  8.6 1.3 %collective-permute-start.3 = (bf16[1024,256]{1,0:T(8,128)(2,1)S(1)}, bf16[1024,256]{1,0:T(8,128)(2,1)S(1)}, u32[]{:S(2)}, u32[]{:S(2)}) collective-permute-start(bf16[1024,256]{1,0:T(8,128)(2,1)S(1)} %get-tuple-element.68.refs_7_.refs_1_.refs_2_), channel_id=1, source_target_pairs={{4,12},{6,14},{8,0},{10,2},{12,20},{14,22},{16,8},{18,10},{20,28},... | collective-permute-start | bytes 1572872 | tf_op jit(solution)/shard_map/ppermute | solution.py:319
  9.9 5.4 %collective-permute-start.7 = (bf16[1024,256]{1,0:T(8,128)(2,1)S(1)}, bf16[1024,256]{1,0:T(8,128)(2,1)S(1)}, u32[]{:S(2)}, u32[]{:S(2)}) collective-permute-start(bf16[1024,256]{1,0:T(8,128)(2,1)S(1)} %get-tuple-element.72), channel_id=1, source_target_pairs={{0,4},{2,6},{4,0},{6,2},{8,12},{10,14},{12,8},{14,10},{16,20},{18,... | collective-permute-start | bytes 1572872 | tf_op jit(solution)/shard_map/ppermute | solution.py:316
  15.3 4.0 %mid_tap.1 = (f32[2,512,256]{2,1,0:T(8,128)S(1)}, f32[8,128]{1,0:T(8,128)S(1)}) custom-call(s32[6]{0:T(128)S(1)} %stack.27.meta, bf16[2048,512]{1,0:T(8,128)(2,1)S(1)} %bitcast.13, bf16[2048,512]{1,0:T(8,128)(2,1)S(1)} %bitcast.17, f32[8,128]{1,0:T(8,128)S(1)} %get-tuple-element.62.refs_2_), custom_call_target="tpu_custom_call" | custom-call | flops 1 | bytes 200000 | tf_op jit(solution)/shard_map/mid_tap/pallas_call | solution.py:43
  20.3 3.2 %collective-permute-start.4 = (bf16[1024,256]{1,0:T(8,128)(2,1)S(1)}, bf16[1024,256]{1,0:T(8,128)(2,1)S(1)}, u32[]{:S(2)}, u32[]{:S(2)}) collective-permute-start(bf16[1024,256]{1,0:T(8,128)(2,1)S(1)} %get-tuple-element.64.refs_2_.refs_3_), channel_id=1, source_target_pairs={{12,4},{14,6},{0,8},{2,10},{20,12},{22,14},{8,16},{10,18},{28,20},... | collective-permute-start | bytes 1572872 | tf_op jit(solution)/shard_map/ppermute | solution.py:322
  23.5 4.5 %collective-permute-done.1.refs_0_.refs_1_ = bf16[1024,256]{1,0:T(8,128)(2,1)S(1)} collective-permute-done((bf16[1024,256]{1,0:T(8,128)(2,1)S(1)}, bf16[1024,256]{1,0:T(8,128)(2,1)S(1)}, u32[]{:S(2)}, u32[]{:S(2)}) %collective-permute-start.1) | collective-permute-done | bytes 524320 | tf_op jit(solution)/shard_map/ppermute | solution.py:316
  29.0 3.1 %collective-permute-start.6 = (bf16[1024,256]{1,0:T(8,128)(2,1)S(1)}, bf16[1024,256]{1,0:T(8,128)(2,1)S(1)}, u32[]{:S(2)}, u32[]{:S(2)}) collective-permute-start(bf16[1024,256]{1,0:T(8,128)(2,1)S(1)} %get-tuple-element.66.refs_3_.refs_4_), channel_id=1, source_target_pairs={{12,4},{14,6},{0,8},{2,10},{20,12},{22,14},{8,16},{10,18},{28,20},... | collective-permute-start | bytes 1572872 | tf_op jit(solution)/shard_map/ppermute | solution.py:322
  34.2 5.0 %collective-permute-done.7.refs_9_.refs_3_.refs_2_ = bf16[1024,256]{1,0:T(8,128)(2,1)S(1)} collective-permute-done((bf16[1024,256]{1,0:T(8,128)(2,1)S(1)}, bf16[1024,256]{1,0:T(8,128)(2,1)S(1)}, u32[]{:S(2)}, u32[]{:S(2)}) %collective-permute-start.7) | collective-permute-done | bytes 524320 | tf_op jit(solution)/shard_map/ppermute | solution.py:316
  39.2 3.1 %collective-permute-start.12 = (bf16[1024,256]{1,0:T(8,128)(2,1)S(1)}, bf16[1024,256]{1,0:T(8,128)(2,1)S(1)}, u32[]{:S(2)}, u32[]{:S(2)}) collective-permute-start(bf16[1024,256]{1,0:T(8,128)(2,1)S(1)} %collective-permute-done.7.refs_9_.refs_3_.refs_2_), channel_id=1, source_target_pairs={{12,4},{14,6},{0,8},{2,10},{20,12},{22,14},{8,16},{10,18},{28,20},... | collective-permute-start | bytes 1572872 | tf_op jit(solution)/shard_map/ppermute | solution.py:322
  42.3 2.9 %oth_out.1 = (bf16[1024,512]{1,0:T(8,128)(2,1)S(1)}, f32[8,128]{1,0:T(8,128)S(1)}) custom-call(s32[6]{0:T(128)S(1)} %stack.27.meta, bf16[1024,256]{1,0:T(8,128)(2,1)S(1)} %collective-permute-done.refs_0_, bf16[1024,256]{1,0:T(8,128)(2,1)S(1)} %collective-permute-done.1.refs_0_.refs_1_, bf16[1024,256]{1,0:T(8,128)(2,1)S(1)} %get-tuple-element.64.refs_2_.refs_3_, ...), custom_call_target="tpu_custom_call" | custom-call | flops 1 | bytes 200000 | tf_op jit(solution)/shard_map/oth_out/pallas_call | solution.py:43
  45.2 2.8 %outer_taps0.1 = (f32[4,256,256]{2,1,0:T(8,128)S(1)}, bf16[4,256,256]{2,1,0:T(8,128)(2,1)S(1)}, f32[8,128]{1,0:T(8,128)S(1)}) custom-call(s32[6]{0:T(128)S(1)} %stack.27.meta, bf16[1024,256]{1,0:T(8,128)(2,1)S(1)} %get-tuple-element.67.refs_6_.refs_0_.refs_1_, bf16[1024,256]{1,0:T(8,128)(2,1)S(1)} %get-tuple-element.68.refs_7_.refs_1_.refs_2_, ...), custom_call_target="tpu_custom_call" | custom-call | flops 1 | bytes 200000 | tf_op jit(solution)/shard_map/outer_taps0/pallas_call | solution.py:43
  48.1 4.2 %collective-permute-start.11 = (bf16[4,256,256]{2,1,0:T(8,128)(2,1)S(1)}, bf16[4,256,256]{2,1,0:T(8,128)(2,1)S(1)}, u32[]{:S(2)}, u32[]{:S(2)}) collective-permute-start(bf16[4,256,256]{2,1,0:T(8,128)(2,1)S(1)} %get-tuple-element.80), channel_id=1, source_target_pairs={{0,2},{2,0},{4,6},{6,4},{8,10},{10,8},{12,14},{14,12},{16,18},{18,... | collective-permute-start | bytes 1572872 | tf_op jit(solution)/shard_map/ppermute | solution.py:325
  52.5 2.8 %outer_taps1.1 = (f32[2,256,256]{2,1,0:T(8,128)S(1)}, f32[2,256,256]{2,1,0:T(8,128)S(1)}, f32[8,128]{1,0:T(8,128)S(1)}) custom-call(s32[6]{0:T(128)S(1)} %stack.27.meta, bf16[1024,256]{1,0:T(8,128)(2,1)S(1)} %get-tuple-element.67.refs_6_.refs_0_.refs_1_, bf16[1024,256]{1,0:T(8,128)(2,1)S(1)} %get-tuple-element.68.refs_7_.refs_1_.refs_2_, ...), custom_call_target="tpu_custom_call" | custom-call | flops 1 | bytes 200000 | tf_op jit(solution)/shard_map/outer_taps1/pallas_call | solution.py:43
  55.7 3.7 %collective-permute-start.16 = (bf16[1024,256]{1,0:T(8,128)(2,1)S(1)}, bf16[1024,256]{1,0:T(8,128)(2,1)S(1)}, u32[]{:S(2)}, u32[]{:S(2)}) collective-permute-start(bf16[1024,256]{1,0:T(8,128)(2,1)S(1)} %collective-permute-done.8.refs_9_.refs_4_.refs_3_), channel_id=1, source_target_pairs={{12,4},{14,6},{0,8},{2,10},{20,12},{22,14},{8,16},{10,18},{28,20},... | collective-permute-start | bytes 1572872 | tf_op jit(solution)/shard_map/ppermute | solution.py:322
  62.5 3.8 %oth_grad.1 = (bf16[1024,512]{1,0:T(8,128)(2,1)S(1)}, f32[8,128]{1,0:T(8,128)S(1)}) custom-call(s32[6]{0:T(128)S(1)} %stack.27.meta, bf16[1024,256]{1,0:T(8,128)(2,1)S(1)} %collective-permute-done.refs_0_, bf16[1024,256]{1,0:T(8,128)(2,1)S(1)} %collective-permute-done.1.refs_0_.refs_1_, bf16[1024,512]{1,0:T(8,128)(2,1)S(1)} %get-tuple-element.71.refs_8_.refs_2_.refs_1_, ...), custom_call_target="tpu_custom_call" | custom-call | flops 1 | bytes 200000 | tf_op jit(solution)/shard_map/oth_grad/pallas_call | solution.py:43
  66.4 3.7 %own_out.1 = (bf16[2048,512]{1,0:T(8,128)(2,1)}, f32[8,128]{1,0:T(8,128)S(1)}) custom-call(s32[6]{0:T(128)S(1)} %stack.27.meta, bf16[2048,512]{1,0:T(8,128)(2,1)S(1)} %bitcast.14, bf16[1024,256]{1,0:T(8,128)(2,1)S(1)} %get-tuple-element.67.refs_6_.refs_0_.refs_1_, bf16[1024,256]{1,0:T(8,128)(2,1)S(1)} %get-tuple-element.68.refs_7_.refs_1_.refs_2_, ...), custom_call_target="tpu_custom_call" | custom-call | flops 1 | bytes 200000 | tf_op jit(solution)/shard_map/own_out/pallas_call | solution.py:43
  70.8 1.7 %collective-permute-start.15 = (bf16[6,64,256]{2,1,0:T(8,128)(2,1)S(1)}, bf16[6,64,256]{2,1,0:T(8,128)(2,1)S(1)}, u32[]{:S(2)}, u32[]{:S(2)}) collective-permute-start(bf16[6,64,256]{2,1,0:T(8,128)(2,1)S(1)} %get-tuple-element.92), channel_id=1, source_target_pairs={{0,8},{2,10},{4,12},{6,14},{8,0},{10,2},{12,4},{14,6},{16,24},{18,... | collective-permute-start | bytes 589832 | tf_op jit(solution)/shard_map/ppermute | solution.py:345
  72.6 4.6 %own_grad.1 = (bf16[2048,512]{1,0:T(8,128)(2,1)}, f32[8,128]{1,0:T(8,128)S(1)}) custom-call(s32[6]{0:T(128)S(1)} %stack.27.meta, bf16[2048,512]{1,0:T(8,128)(2,1)S(1)} %bitcast.15, bf16[1024,512]{1,0:T(8,128)(2,1)S(1)} %get-tuple-element.71.refs_8_.refs_2_.refs_1_, bf16[1024,256]{1,0:T(8,128)(2,1)S(1)} %collective-permute-done.7.refs_9_.refs_3_.refs_2_, ...), custom_call_target="tpu_custom_call" | custom-call | flops 1 | bytes 200000 | tf_op jit(solution)/shard_map/own_grad/pallas_call | solution.py:43
  77.8 1.5 %collective-permute-start.18 = (bf16[6,32,256]{2,1,0:T(8,128)(2,1)S(1)}, bf16[6,32,256]{2,1,0:T(8,128)(2,1)S(1)}, u32[]{:S(2)}, u32[]{:S(2)}) collective-permute-start(bf16[6,32,256]{2,1,0:T(8,128)(2,1)S(1)} %get-tuple-element.100), channel_id=1, source_target_pairs={{0,16},{2,18},{4,20},{6,22},{8,24},{10,26},{12,28},{14,30},{16,0},... | collective-permute-start | bytes 294920 | tf_op jit(solution)/shard_map/ppermute | solution.py:345
  79.3 1.5 %place_out.1 = (bf16[2048,512]{1,0:T(8,128)(2,1)}, f32[8,128]{1,0:T(8,128)S(1)}) custom-call(s32[6]{0:T(128)S(1)} %stack.27.meta, bf16[1024,512]{1,0:T(8,128)(2,1)S(1)} %collective-permute-done.5.refs_0_, bf16[2048,512]{1,0:T(8,128)(2,1)} %get-tuple-element.85.refs_1_, f32[8,128]{1,0:T(8,128)S(1)} %get-tuple-element.95.refs_2_), custom_call_target="tpu_custom_call", output_to_operand_aliasing={{0}: (2, {})} | custom-call | flops 1 | bytes 200000 | tf_op jit(solution)/shard_map/place_out/pallas_call | solution.py:43
  80.8 2.5 %collective-permute-done.18.refs_1_ = bf16[6,32,256]{2,1,0:T(8,128)(2,1)S(1)} collective-permute-done((bf16[6,32,256]{2,1,0:T(8,128)(2,1)S(1)}, bf16[6,32,256]{2,1,0:T(8,128)(2,1)S(1)}, u32[]{:S(2)}, u32[]{:S(2)}) %collective-permute-start.18) | collective-permute-done | bytes 98336 | tf_op jit(solution)/shard_map/ppermute | solution.py:345
  83.9 6.1 %collective-permute-done.19.refs_1_ = f32[6,32,256]{2,1,0:T(8,128)S(1)} collective-permute-done((f32[6,32,256]{2,1,0:T(8,128)S(1)}, f32[6,32,256]{2,1,0:T(8,128)S(1)}, u32[]{:S(2)}, u32[]{:S(2)}) %collective-permute-start.19) | collective-permute-done | bytes 196640 | tf_op jit(solution)/shard_map/ppermute | solution.py:349
  90.6 2.0 %collective-permute-start.21 = (bf16[6,32,256]{2,1,0:T(8,128)(2,1)S(1)}, bf16[6,32,256]{2,1,0:T(8,128)(2,1)S(1)}, u32[]{:S(2)}, u32[]{:S(2)}) collective-permute-start(bf16[6,32,256]{2,1,0:T(8,128)(2,1)S(1)} %get-tuple-element.104.refs_0_), channel_id=1, source_target_pairs={{0,8},{2,10},{4,12},{6,14},{8,0},{10,2},{12,4},{14,6},{16,24},{18,... | collective-permute-start | bytes 294920 | tf_op jit(solution)/shard_map/ppermute | solution.py:345
  93.9 2.1 %collective-permute-done.20.refs_1_ = bf16[6,32,256]{2,1,0:T(8,128)(2,1)S(1)} collective-permute-done((bf16[6,32,256]{2,1,0:T(8,128)(2,1)S(1)}, bf16[6,32,256]{2,1,0:T(8,128)(2,1)S(1)}, u32[]{:S(2)}, u32[]{:S(2)}) %collective-permute-start.20) | collective-permute-done | bytes 98336 | tf_op jit(solution)/shard_map/ppermute | solution.py:345
  96.0 2.1 %collective-permute-done.21.refs_2_ = bf16[6,32,256]{2,1,0:T(8,128)(2,1)S(1)} collective-permute-done((bf16[6,32,256]{2,1,0:T(8,128)(2,1)S(1)}, bf16[6,32,256]{2,1,0:T(8,128)(2,1)S(1)}, u32[]{:S(2)}, u32[]{:S(2)}) %collective-permute-start.21) | collective-permute-done | bytes 98336 | tf_op jit(solution)/shard_map/ppermute | solution.py:345
  99.9 3.8 %collective-permute-done.17.refs_0_ = bf16[1024,512]{1,0:T(8,128)(2,1)S(1)} collective-permute-done((bf16[1024,512]{1,0:T(8,128)(2,1)S(1)}, bf16[1024,512]{1,0:T(8,128)(2,1)S(1)}, u32[]{:S(2)}, u32[]{:S(2)}) %collective-permute-start.17) | collective-permute-done | bytes 1048608 | tf_op jit(solution)/shard_map/ppermute | solution.py:316
  103.7 1.5 %place_grad.1 = (bf16[2048,512]{1,0:T(8,128)(2,1)}, f32[8,128]{1,0:T(8,128)S(1)}) custom-call(s32[6]{0:T(128)S(1)} %stack.27.meta, bf16[1024,512]{1,0:T(8,128)(2,1)S(1)} %collective-permute-done.17.refs_0_, bf16[2048,512]{1,0:T(8,128)(2,1)} %get-tuple-element.98.refs_1_, f32[8,128]{1,0:T(8,128)S(1)} %get-tuple-element.106.refs_2_), custom_call_target="tpu_custom_call", output_to_operand_aliasing={{0}: (2, {})} | custom-call | flops 1 | bytes 200000 | tf_op jit(solution)/shard_map/place_grad/pallas_call | solution.py:43
  105.9 8.4 %collective-permute-start.24 = (bf16[6,256,256]{2,1,0:T(8,128)(2,1)S(1)}, bf16[6,256,256]{2,1,0:T(8,128)(2,1)S(1)}, u32[]{:S(2)}, u32[]{:S(2)}) collective-permute-start(bf16[6,256,256]{2,1,0:T(8,128)(2,1)S(1)} %get-tuple-element.110.refs_0_), channel_id=1, source_target_pairs={{0,2},{2,0},{4,6},{6,4},{8,10},{10,8},{12,14},{14,12},{16,18},{18,... | collective-permute-start | bytes 2359304 | tf_op jit(solution)/shard_map/ppermute | solution.py:325
  114.3 1.9 %collective-permute-done.24.refs_1_ = bf16[6,256,256]{2,1,0:T(8,128)(2,1)S(1)} collective-permute-done((bf16[6,256,256]{2,1,0:T(8,128)(2,1)S(1)}, bf16[6,256,256]{2,1,0:T(8,128)(2,1)S(1)}, u32[]{:S(2)}, u32[]{:S(2)}) %collective-permute-start.24) | collective-permute-done | bytes 786464 | tf_op jit(solution)/shard_map/ppermute | solution.py:325
  116.3 2.5 %write_taps.1 = (f32[3,512,512]{2,1,0:T(8,128)}, f32[8,128]{1,0:T(8,128)}) custom-call(s32[6]{0:T(128)S(1)} %stack.27.meta, bf16[6,256,256]{2,1,0:T(8,128)(2,1)S(1)} %get-tuple-element.110.refs_0_, bf16[6,256,256]{2,1,0:T(8,128)(2,1)S(1)} %collective-permute-done.24.refs_1_, f32[8,128]{1,0:T(8,128)S(1)} %get-tuple-element.111.refs_2_), custom_call_target="tpu_custom_call" | custom-call | flops 1 | bytes 200000 | tf_op jit(solution)/shard_map/write_taps/pallas_call | solution.py:43
  (50 shorter events, 17.0 us)
Async XLA Ops:
  0.7 1.6 %copy-start.1 = (bf16[1,2048,512]{2,1,0:T(8,128)(2,1)S(1)}, bf16[1,2048,512]{2,1,0:T(8,128)(2,1)}, u32[]{:S(2)}) copy-start(bf16[1,2048,512]{2,1,0:T(8,128)(2,1)} %param.3) | copy-start | bytes 6291460
  2.3 4.1 %copy-start.3 = (bf16[1,2048,512]{2,1,0:T(8,128)(2,1)S(1)}, bf16[1,2048,512]{2,1,0:T(8,128)(2,1)}, u32[]{:S(2)}) copy-start(bf16[1,2048,512]{2,1,0:T(8,128)(2,1)} %param.5) | copy-start | bytes 6291460
  2.9 16.3 %collective-permute-start = (bf16[1024,256]{1,0:T(8,128)(2,1)S(1)}, bf16[1024,256]{1,0:T(8,128)(2,1)S(1)}, u32[]{:S(2)}, u32[]{:S(2)}) collective-permute-start(bf16[1024,256]{1,0:T(8,128)(2,1)S(1)} %get-tuple-element.58), channel_id=1, source_target_pairs={{0,4},{2,6},{4,0},{6,2},{8,12},{10,14},{12,8},{14,10},{16,20},{18,... | collective-permute-start | bytes 1572872 | tf_op jit(solution)/shard_map/ppermute | solution.py:316
  7.2 20.7 %collective-permute-start.1 = (bf16[1024,256]{1,0:T(8,128)(2,1)S(1)}, bf16[1024,256]{1,0:T(8,128)(2,1)S(1)}, u32[]{:S(2)}, u32[]{:S(2)}) collective-permute-start(bf16[1024,256]{1,0:T(8,128)(2,1)S(1)} %get-tuple-element.61), channel_id=1, source_target_pairs={{0,4},{2,6},{4,0},{6,2},{8,12},{10,14},{12,8},{14,10},{16,20},{18,... | collective-permute-start | bytes 1572872 | tf_op jit(solution)/shard_map/ppermute | solution.py:316
  7.3 24.8 %collective-permute-start.2 = (bf16[1024,256]{1,0:T(8,128)(2,1)S(1)}, bf16[1024,256]{1,0:T(8,128)(2,1)S(1)}, u32[]{:S(2)}, u32[]{:S(2)}) collective-permute-start(bf16[1024,256]{1,0:T(8,128)(2,1)S(1)} %get-tuple-element.67.refs_6_.refs_0_.refs_1_), channel_id=1, source_target_pairs={{4,12},{6,14},{8,0},{10,2},{12,20},{14,22},{16,8},{18,10},{20,28},... | collective-permute-start | bytes 1572872 | tf_op jit(solution)/shard_map/ppermute | solution.py:319
  8.6 24.3 %collective-permute-start.3 = (bf16[1024,256]{1,0:T(8,128)(2,1)S(1)}, bf16[1024,256]{1,0:T(8,128)(2,1)S(1)}, u32[]{:S(2)}, u32[]{:S(2)}) collective-permute-start(bf16[1024,256]{1,0:T(8,128)(2,1)S(1)} %get-tuple-element.68.refs_7_.refs_1_.refs_2_), channel_id=1, source_target_pairs={{4,12},{6,14},{8,0},{10,2},{12,20},{14,22},{16,8},{18,10},{20,28},... | collective-permute-start | bytes 1572872 | tf_op jit(solution)/shard_map/ppermute | solution.py:319
  9.9 29.3 %collective-permute-start.7 = (bf16[1024,256]{1,0:T(8,128)(2,1)S(1)}, bf16[1024,256]{1,0:T(8,128)(2,1)S(1)}, u32[]{:S(2)}, u32[]{:S(2)}) collective-permute-start(bf16[1024,256]{1,0:T(8,128)(2,1)S(1)} %get-tuple-element.72), channel_id=1, source_target_pairs={{0,4},{2,6},{4,0},{6,2},{8,12},{10,14},{12,8},{14,10},{16,20},{18,... | collective-permute-start | bytes 1572872 | tf_op jit(solution)/shard_map/ppermute | solution.py:316
  15.3 27.1 %copy-start = (bf16[3,512,512]{2,1,0:T(8,128)(2,1)S(1)}, bf16[3,512,512]{2,1,0:T(8,128)(2,1)}, u32[]{:S(2)}) copy-start(bf16[3,512,512]{2,1,0:T(8,128)(2,1)} %refs_8_.7) | copy-start | bytes 4718596
  20.3 22.1 %collective-permute-start.4 = (bf16[1024,256]{1,0:T(8,128)(2,1)S(1)}, bf16[1024,256]{1,0:T(8,128)(2,1)S(1)}, u32[]{:S(2)}, u32[]{:S(2)}) collective-permute-start(bf16[1024,256]{1,0:T(8,128)(2,1)S(1)} %get-tuple-element.64.refs_2_.refs_3_), channel_id=1, source_target_pairs={{12,4},{14,6},{0,8},{2,10},{20,12},{22,14},{8,16},{10,18},{28,20},... | collective-permute-start | bytes 1572872 | tf_op jit(solution)/shard_map/ppermute | solution.py:322
  29.0 16.3 %collective-permute-start.6 = (bf16[1024,256]{1,0:T(8,128)(2,1)S(1)}, bf16[1024,256]{1,0:T(8,128)(2,1)S(1)}, u32[]{:S(2)}, u32[]{:S(2)}) collective-permute-start(bf16[1024,256]{1,0:T(8,128)(2,1)S(1)} %get-tuple-element.66.refs_3_.refs_4_), channel_id=1, source_target_pairs={{12,4},{14,6},{0,8},{2,10},{20,12},{22,14},{8,16},{10,18},{28,20},... | collective-permute-start | bytes 1572872 | tf_op jit(solution)/shard_map/ppermute | solution.py:322
  32.1 20.4 %collective-permute-start.8 = (bf16[1024,256]{1,0:T(8,128)(2,1)S(1)}, bf16[1024,256]{1,0:T(8,128)(2,1)S(1)}, u32[]{:S(2)}, u32[]{:S(2)}) collective-permute-start(bf16[1024,256]{1,0:T(8,128)(2,1)S(1)} %get-tuple-element.73), channel_id=1, source_target_pairs={{0,4},{2,6},{4,0},{6,2},{8,12},{10,14},{12,8},{14,10},{16,20},{18,... | collective-permute-start | bytes 1572872 | tf_op jit(solution)/shard_map/ppermute | solution.py:316
  33.0 29.5 %collective-permute-start.9 = (bf16[1024,512]{1,0:T(8,128)(2,1)S(1)}, bf16[1024,512]{1,0:T(8,128)(2,1)S(1)}, u32[]{:S(2)}, u32[]{:S(2)}) collective-permute-start(bf16[1024,512]{1,0:T(8,128)(2,1)S(1)} %get-tuple-element.71.refs_8_.refs_2_.refs_1_), channel_id=1, source_target_pairs={{4,12},{6,14},{8,0},{10,2},{12,20},{14,22},{16,8},{18,10},{20,28},... | collective-permute-start | bytes 3145736 | tf_op jit(solution)/shard_map/ppermute | solution.py:319
  39.2 16.5 %collective-permute-start.12 = (bf16[1024,256]{1,0:T(8,128)(2,1)S(1)}, bf16[1024,256]{1,0:T(8,128)(2,1)S(1)}, u32[]{:S(2)}, u32[]{:S(2)}) collective-permute-start(bf16[1024,256]{1,0:T(8,128)(2,1)S(1)} %collective-permute-done.7.refs_9_.refs_3_.refs_2_), channel_id=1, source_target_pairs={{12,4},{14,6},{0,8},{2,10},{20,12},{22,14},{8,16},{10,18},{28,20},... | collective-permute-start | bytes 1572872 | tf_op jit(solution)/shard_map/ppermute | solution.py:322
  48.1 11.3 %collective-permute-start.11 = (bf16[4,256,256]{2,1,0:T(8,128)(2,1)S(1)}, bf16[4,256,256]{2,1,0:T(8,128)(2,1)S(1)}, u32[]{:S(2)}, u32[]{:S(2)}) collective-permute-start(bf16[4,256,256]{2,1,0:T(8,128)(2,1)S(1)} %get-tuple-element.80), channel_id=1, source_target_pairs={{0,2},{2,0},{4,6},{6,4},{8,10},{10,8},{12,14},{14,12},{16,18},{18,... | collective-permute-start | bytes 1572872 | tf_op jit(solution)/shard_map/ppermute | solution.py:325
  52.3 26.9 %collective-permute-start.5 = (bf16[1024,512]{1,0:T(8,128)(2,1)S(1)}, bf16[1024,512]{1,0:T(8,128)(2,1)S(1)}, u32[]{:S(2)}, u32[]{:S(2)}) collective-permute-start(bf16[1024,512]{1,0:T(8,128)(2,1)S(1)} %get-tuple-element.70), channel_id=1, source_target_pairs={{0,4},{2,6},{4,0},{6,2},{8,12},{10,14},{12,8},{14,10},{16,20},{18,... | collective-permute-start | bytes 3145736 | tf_op jit(solution)/shard_map/ppermute | solution.py:316
  55.3 6.2 %collective-permute-start.10 = (f32[2,256,256]{2,1,0:T(8,128)S(1)}, f32[2,256,256]{2,1,0:T(8,128)S(1)}, u32[]{:S(2)}, u32[]{:S(2)}) collective-permute-start(f32[2,256,256]{2,1,0:T(8,128)S(1)} %get-tuple-element.78), channel_id=1, source_target_pairs={{0,2},{2,0},{4,6},{6,4},{8,10},{10,8},{12,14},{14,12},{16,18},{18,... | collective-permute-start | bytes 1572872 | tf_op jit(solution)/shard_map/ppermute | solution.py:325
  55.7 16.9 %collective-permute-start.16 = (bf16[1024,256]{1,0:T(8,128)(2,1)S(1)}, bf16[1024,256]{1,0:T(8,128)(2,1)S(1)}, u32[]{:S(2)}, u32[]{:S(2)}) collective-permute-start(bf16[1024,256]{1,0:T(8,128)(2,1)S(1)} %collective-permute-done.8.refs_9_.refs_4_.refs_3_), channel_id=1, source_target_pairs={{12,4},{14,6},{0,8},{2,10},{20,12},{22,14},{8,16},{10,18},{28,20},... | collective-permute-start | bytes 1572872 | tf_op jit(solution)/shard_map/ppermute | solution.py:322
  60.2 9.9 %collective-permute-start.13 = (bf16[4,128,256]{2,1,0:T(8,128)(2,1)S(1)}, bf16[4,128,256]{2,1,0:T(8,128)(2,1)S(1)}, u32[]{:S(2)}, u32[]{:S(2)}) collective-permute-start(bf16[4,128,256]{2,1,0:T(8,128)(2,1)S(1)} %get-tuple-element.87), channel_id=1, source_target_pairs={{0,1},{1,0},{2,3},{3,2},{4,5},{5,4},{6,7},{7,6},{8,9},{9,8},{10,11... | collective-permute-start | bytes 786440 | tf_op jit(solution)/shard_map/ppermute | solution.py:328
  62.2 7.9 %collective-permute-start.14 = (bf16[2,128,256]{2,1,0:T(8,128)(2,1)S(1)}, bf16[2,128,256]{2,1,0:T(8,128)(2,1)S(1)}, u32[]{:S(2)}, u32[]{:S(2)}) collective-permute-start(bf16[2,128,256]{2,1,0:T(8,128)(2,1)S(1)} %get-tuple-element.89), channel_id=1, source_target_pairs={{0,1},{1,0},{2,3},{3,2},{4,5},{5,4},{6,7},{7,6},{8,9},{9,8},{10,11... | collective-permute-start | bytes 393224 | tf_op jit(solution)/shard_map/ppermute | solution.py:328
  62.5 3.9 %copy-start.2 = (bf16[1,2048,512]{2,1,0:T(8,128)(2,1)S(1)}, bf16[1,2048,512]{2,1,0:T(8,128)(2,1)}, u32[]{:S(2)}) copy-start(bf16[1,2048,512]{2,1,0:T(8,128)(2,1)} %param.3) | copy-start | bytes 6291460
  66.3 37.4 %collective-permute-start.17 = (bf16[1024,512]{1,0:T(8,128)(2,1)S(1)}, bf16[1024,512]{1,0:T(8,128)(2,1)S(1)}, u32[]{:S(2)}, u32[]{:S(2)}) collective-permute-start(bf16[1024,512]{1,0:T(8,128)(2,1)S(1)} %get-tuple-element.97), channel_id=1, source_target_pairs={{0,4},{2,6},{4,0},{6,2},{8,12},{10,14},{12,8},{14,10},{16,20},{18,... | collective-permute-start | bytes 3145736 | tf_op jit(solution)/shard_map/ppermute | solution.py:316
  70.8 6.3 %collective-permute-start.15 = (bf16[6,64,256]{2,1,0:T(8,128)(2,1)S(1)}, bf16[6,64,256]{2,1,0:T(8,128)(2,1)S(1)}, u32[]{:S(2)}, u32[]{:S(2)}) collective-permute-start(bf16[6,64,256]{2,1,0:T(8,128)(2,1)S(1)} %get-tuple-element.92), channel_id=1, source_target_pairs={{0,8},{2,10},{4,12},{6,14},{8,0},{10,2},{12,4},{14,6},{16,24},{18,... | collective-permute-start | bytes 589832 | tf_op jit(solution)/shard_map/ppermute | solution.py:345
  77.8 5.5 %collective-permute-start.18 = (bf16[6,32,256]{2,1,0:T(8,128)(2,1)S(1)}, bf16[6,32,256]{2,1,0:T(8,128)(2,1)S(1)}, u32[]{:S(2)}, u32[]{:S(2)}) collective-permute-start(bf16[6,32,256]{2,1,0:T(8,128)(2,1)S(1)} %get-tuple-element.100), channel_id=1, source_target_pairs={{0,16},{2,18},{4,20},{6,22},{8,24},{10,26},{12,28},{14,30},{16,0},... | collective-permute-start | bytes 294920 | tf_op jit(solution)/shard_map/ppermute | solution.py:345
  83.8 6.2 %collective-permute-start.19 = (f32[6,32,256]{2,1,0:T(8,128)S(1)}, f32[6,32,256]{2,1,0:T(8,128)S(1)}, u32[]{:S(2)}, u32[]{:S(2)}) collective-permute-start(f32[6,32,256]{2,1,0:T(8,128)S(1)} %get-tuple-element.102.refs_0_), channel_id=1, source_target_pairs={{0,12},{2,14},{4,8},{6,10},{8,4},{10,6},{12,0},{14,2},{16,28},{18,... | collective-permute-start | bytes 589832 | tf_op jit(solution)/shard_map/ppermute | solution.py:349
  90.6 5.4 %collective-permute-start.20 = (bf16[6,32,256]{2,1,0:T(8,128)(2,1)S(1)}, bf16[6,32,256]{2,1,0:T(8,128)(2,1)S(1)}, u32[]{:S(2)}, u32[]{:S(2)}) collective-permute-start(bf16[6,32,256]{2,1,0:T(8,128)(2,1)S(1)} %get-tuple-element.104.refs_0_), channel_id=1, source_target_pairs={{0,16},{2,18},{4,20},{6,22},{8,24},{10,26},{12,28},{14,30},{16,8},... | collective-permute-start | bytes 294920 | tf_op jit(solution)/shard_map/ppermute | solution.py:345
  90.6 7.4 %collective-permute-start.21 = (bf16[6,32,256]{2,1,0:T(8,128)(2,1)S(1)}, bf16[6,32,256]{2,1,0:T(8,128)(2,1)S(1)}, u32[]{:S(2)}, u32[]{:S(2)}) collective-permute-start(bf16[6,32,256]{2,1,0:T(8,128)(2,1)S(1)} %get-tuple-element.104.refs_0_), channel_id=1, source_target_pairs={{0,8},{2,10},{4,12},{6,14},{8,0},{10,2},{12,4},{14,6},{16,24},{18,... | collective-permute-start | bytes 294920 | tf_op jit(solution)/shard_map/ppermute | solution.py:345
  92.6 5.4 %collective-permute-start.22 = (bf16[6,32,256]{2,1,0:T(8,128)(2,1)S(1)}, bf16[6,32,256]{2,1,0:T(8,128)(2,1)S(1)}, u32[]{:S(2)}, u32[]{:S(2)}) collective-permute-start(bf16[6,32,256]{2,1,0:T(8,128)(2,1)S(1)} %get-tuple-element.104.refs_0_), channel_id=1, source_target_pairs={{0,24},{2,26},{4,28},{6,30},{8,16},{10,18},{12,20},{14,22},{16,0},... | collective-permute-start | bytes 294920 | tf_op jit(solution)/shard_map/ppermute | solution.py:345
  98.6 6.7 %collective-permute-start.23 = (bf16[6,128,256]{2,1,0:T(8,128)(2,1)S(1)}, bf16[6,128,256]{2,1,0:T(8,128)(2,1)S(1)}, u32[]{:S(2)}, u32[]{:S(2)}) collective-permute-start(bf16[6,128,256]{2,1,0:T(8,128)(2,1)S(1)} %get-tuple-element.108.refs_0_), channel_id=1, source_target_pairs={{0,1},{1,0},{2,3},{3,2},{4,5},{5,4},{6,7},{7,6},{8,9},{9,8},{10,11... | collective-permute-start | bytes 1179656 | tf_op jit(solution)/shard_map/ppermute | solution.py:328
  105.9 10.3 %collective-permute-start.24 = (bf16[6,256,256]{2,1,0:T(8,128)(2,1)S(1)}, bf16[6,256,256]{2,1,0:T(8,128)(2,1)S(1)}, u32[]{:S(2)}, u32[]{:S(2)}) collective-permute-start(bf16[6,256,256]{2,1,0:T(8,128)(2,1)S(1)} %get-tuple-element.110.refs_0_), channel_id=1, source_target_pairs={{0,2},{2,0},{4,6},{6,4},{8,10},{10,8},{12,14},{14,12},{16,18},{18,... | collective-permute-start | bytes 2359304 | tf_op jit(solution)/shard_map/ppermute | solution.py:325

commit v4 on v3

--- a/solution.py
+++ b/solution.py
@@ -10,6 +10,7 @@
 DILATION_BINS = 4096
 BF16, F32 = jnp.bfloat16, jnp.float32
 VMEM_BYTES = 40 * 1024 * 1024
+COSTS = {}
 SIDE, CORE, DP, ALONG, ALONG_BITS = range(5)
 HBM = pl.BlockSpec(memory_space=pltpu.HBM)
 WHOLE = pl.BlockSpec(memory_space=pltpu.VMEM)
@@ -49,7 +50,7 @@
         out_shape=[*outs, TOKEN],
         input_output_aliases=aliases or {},
         compiler_params=pltpu.CompilerParams(vmem_limit_bytes=VMEM_BYTES),
-        cost_estimate=pl.CostEstimate(flops=1, bytes_accessed=200_000, transcendentals=0),
+        cost_estimate=pl.CostEstimate(flops=1, bytes_accessed=COSTS.get(name, 200_000), transcendentals=0),
         name=name,
     )(device.meta, *operands, *tokens)
     device.token = results[-1]
@@ -167,41 +168,44 @@
         out[:, pl.ds(pl.multiple_of(source * size, size), size), :] = ref[...]
 
 
-def gather(device, values, place, name=None):
+def gather(device, values, place, name=None, after=()):
     count = len(values)
     k, rows, cols = values[0].shape
     return call(
         functools.partial(gather_body, count, place), device, values, [WHOLE] * count,
-        shape_of((k, rows * count, cols), BF16), WHOLE, name=name,
-    )
-
-
-def write_taps_body(count, targets, aliased, meta, *refs):
-    ins = refs[:count]
-    out, wide, sems = refs[count + aliased :]
-    size = ins[0].shape[1]
-    for shift, ref in enumerate(ins):
-        source = lax.rem(meta[CORE] + count - shift, count)
-        wide[:, pl.ds(pl.multiple_of(source * size, size), size), :] = ref[...].astype(F32)
+        shape_of((k, rows * count, cols), BF16), WHOLE, name=name, after=after,
+    )
+
+
+def write_taps_body(shifts, groups, targets, aliased, meta, *refs):
+    parts = refs[: len(shifts)]
+    out, wide, sems = refs[len(shifts) + aliased :]
+    rows, cols = parts[0].shape[1:]
+    cores, dps = groups
     copies = []
-    for n, (tap, col) in enumerate(targets):
-        window = out.at[tap, :, pl.ds(col, wide.shape[2])]
-        copies.append(pltpu.make_async_copy(wide.at[n], window, sems.at[n]))
-    for copy in copies:
-        copy.start()
+    for m, (part, (core_shift, dp_shift)) in enumerate(zip(parts, shifts)):
+        core = lax.rem(meta[CORE] + cores - core_shift, cores)
+        dp = lax.rem(meta[DP] + dps - dp_shift, dps)
+        first = pl.multiple_of((core * dps + dp) * rows, rows)
+        wide[m] = part[...].astype(F32)
+        for n, (tap, col) in enumerate(targets):
+            window = out.at[tap, pl.ds(first, rows), pl.ds(col, cols)]
+            copy = pltpu.make_async_copy(wide.at[m, n], window, sems.at[m, n])
+            copy.start()
+            copies.append(copy)
     for copy in copies:
         copy.wait()
 
 
-def write_taps(device, values, targets, shape, buffer, name):
-    count = len(values)
-    k, rows, cols = values[0].shape
+def write_taps(device, parts, shifts, groups, targets, shape, buffer, name, after=()):
     extra = [] if buffer is None else [buffer]
     return call(
-        functools.partial(write_taps_body, count, targets, len(extra)), device, (*values, *extra),
-        [WHOLE] * count + [HBM] * len(extra), shape_of(shape, F32), HBM,
-        scratch=[pltpu.VMEM((k, rows * count, cols), F32), pltpu.SemaphoreType.DMA((k,))],
-        aliases={1 + count: 0} if extra else None, name=name,
+        functools.partial(write_taps_body, shifts, groups, targets, len(extra)), device, (*parts, *extra),
+        [WHOLE] * len(parts) + [HBM] * len(extra), shape_of(shape, F32), HBM,
+        scratch=[
+            pltpu.VMEM((len(parts), *parts[0].shape), F32), pltpu.SemaphoreType.DMA((len(parts), len(targets)))
+        ],
+        aliases={1 + len(parts): 0} if extra else None, name=name, after=after,
     )
 
 
@@ -234,29 +238,49 @@
     out[...] = (x[...].astype(F32) + conv).astype(BF16)
 
 
-def outer_body(
-    steps, count, n_extra, meta, own0, own1, oth0, oth1, far0, far1, own_far0, own_far1, u_own, u_oth, *refs
-):
-    extra, (keep, send, total) = refs[:n_extra], refs[n_extra:]
+def outer_first_body(steps, count, meta, own0, own1, oth0, oth1, far0, far1, own_far0, own_far1, u_own, u_oth, mid, *refs):
+    keep, send, rest, total = refs
     i = pl.program_id(0)
 
     @pl.when(i == 0)
     def _():
         total[...] = jnp.zeros_like(total)
+        rest[...] = jnp.zeros_like(rest)
 
     cols = own0.shape[1]
     for n, (own, oth, far, own_far) in enumerate(((own0, oth0, far0, own_far0), (own1, oth1, far1, own_far1))):
         rows = slice(n * cols, (n + 1) * cols)
-        total[0, rows] += mm_outer(own[...], u_oth[...]) + mm_outer(own_far[...], u_own[...])
-        total[1, rows] += mm_outer(far[...], u_oth[...]) + mm_outer(oth[...], u_own[...])
+        u_first, u_second = u_own[:, :cols], u_own[:, cols:]
+        total[0, rows] += mm_outer(own[...], u_oth[...]) + mm_outer(own_far[...], u_first)
+        total[1, rows] += mm_outer(far[...], u_oth[...]) + mm_outer(oth[...], u_first)
+        rest[0, rows] += mm_outer(own_far[...], u_second)
+        rest[1, rows] += mm_outer(oth[...], u_second)
 
     @pl.when(i == steps - 1)
     def _():
         lead = 0
-        for part in (*extra, total):
+        for part in (mid, total):
             window = pl.ds(lead, part.shape[0])
             split_into(part, meta[CORE], count, keep.at[window], [send.at[window]])
             lead += part.shape[0]
+
+
+def outer_second_body(steps, count, meta, own0, own1, far0, far1, u_oth, rest, keep, send, total):
+    i = pl.program_id(0)
+
+    @pl.when(i == 0)
+    def _():
+        total[...] = rest[...]
+
+    cols = own0.shape[1]
+    for n, (own, far) in enumerate(((own0, far0), (own1, far1))):
+        rows = slice(n * cols, (n + 1) * cols)
+        total[0, rows] += mm_outer(own[...], u_oth[...])
+        total[1, rows] += mm_outer(far[...], u_oth[...])
+
+    @pl.when(i == steps - 1)
+    def _():
+        split_into(total, meta[CORE], count, keep, [send])
 
 
 def oth_grad_body(meta, x0, x1, u_own, oth0, oth1, far, w_near, w_mid, w_far, grad):
@@ -283,10 +307,10 @@
     copy.wait()
 
 
-def place(device, part, buffer, row, col, name):
+def place(device, part, buffer, row, col, name, after=()):
     return call(
         functools.partial(place_body, row, col), device, (part, buffer), [HBM, HBM],
-        shape_of(buffer.shape, buffer.dtype), HBM, scratch=[pltpu.SemaphoreType.DMA], aliases={2: 0}, name=name,
+        shape_of(buffer.shape, buffer.dtype), HBM, scratch=[pltpu.SemaphoreType.DMA], aliases={2: 0}, name=name, after=after,
     )
 
 
@@ -387,28 +411,29 @@
         moves = [lambda position, s=s: (position + s) % along_count for s in range(1, along_count)]
         return [total] + [to_along(total, move) for move in moves if staged]
 
-    def gather_along(parts):
-        total = gather(device, parts, ALONG, "all_along") if staged else parts[0]
-        return [total] + [to_dp(total, s) for s in range(1, dp_count)]
-
-    def gather_dp(parts):
-        total = gather(device, parts, DP, "all_dp")
+    def join(pieces, name, after=()):
+        total = gather(device, pieces, ALONG, name, after) if staged else pieces[0]
         return [total] + [to_core(total, s) for s in range(1, tap)]
 
-    def outer_taps(k, extra=(), dtype=F32):
-        u_own_spec = pl.BlockSpec((block, cols), lambda i, s: (i, k))
-        piece = (2 + sum(part.shape[0] for part in extra), chans // tap, cols)
+    targets = [(1, 0), (1, cols), (0, 0), (2, 0), (0, cols), (2, cols)]
+
+    def write(joined, dp_shift, buffer, after=()):
+        shifts = [(core_shift, dp_shift) for core_shift in range(tap)]
+        return write_taps(
+            device, joined, shifts, (tap, dp_count), targets, conv_weight.shape, buffer, f"write_taps{dp_shift}", after
+        )
+
+    def slices_of(parts, dtype):
+        piece = (parts, chans // tap, cols)
+        return [shape_of(piece, F32), shape_of(piece, dtype)], [pl.BlockSpec(piece, lambda i, s: (0, 0, 0))] * 2
+
+    sums_shape = (2, chans, cols)
+    sums_spec = pl.BlockSpec(sums_shape, lambda i, s: (0, 0, 0))
+
+    def oth_act(x, name, after=()):
         return call(
-            functools.partial(outer_body, steps, tap, len(extra)), device,
-            (*a_own, *a_oth, *a_oth_far, *a_own_far, u_own, u_oth[k], *extra),
-            [*[part_spec] * 8, u_own_spec, part_spec, *[WHOLE] * len(extra)], [shape_of(piece, F32), shape_of(piece, dtype)],
-            [pl.BlockSpec(piece, lambda i, s: (0, 0, 0))] * 2, grid=(steps,),
-            scratch=[pltpu.VMEM((2, chans, cols), F32)], name=f"outer_taps{k}",
-        )
-
-    def oth_act(x, name):
-        return call(
-            act_body, device, (x,), [part_spec], shape_of((half, cols), BF16), part_spec, grid=(steps,), name=name
+            act_body, device, (x,), [part_spec], shape_of((half, cols), BF16), part_spec, grid=(steps,), name=name,
+            after=after,
         )
 
     (x_send0,) = cut(device, (genome,), [(0, False, 0, half, cols)], "cut_first")
@@ -424,28 +449,34 @@
         "cut_rest",
     )
     x_oth1, u_oth = swap(x_send1), [swap(u_send0), swap(u_send1)]
-    u_oth_far = outward(u_own)
-
+    u_oth_far, u_own_far = outward(u_own), [inward(part) for part in u_oth]
     mid = call(
-        lambda meta, *refs: mid_body(*refs), device, (genome, upstream), [rows_spec] * 2,
-        shape_of((2, chans, cols), F32), pl.BlockSpec((2, chans, cols), lambda i, s: (0, 0, 0)), grid=(2 * steps,),
-        name="mid_tap",
+        lambda meta, *refs: mid_body(*refs), device, (genome, upstream), [rows_spec] * 2, shape_of(sums_shape, F32),
+        sums_spec, grid=(2 * steps,), name="mid_tap",
     )
     a_oth0 = oth_act(x_oth0, "oth_act0")
     a_own_far0 = inward(a_oth0)
     a_oth1 = oth_act(x_oth1, "oth_act1")
     a_own_far1 = inward(a_oth1)
-    a_oth, a_own_far = [a_oth0, a_oth1], [a_own_far0, a_own_far1]
     out = call(
-        oth_out_body, device, (x_oth0, x_oth1, *a_oth, *a_oth_far, *a_own, *weights),
-        [*[part_spec] * 8, *weight_specs], half_shape, rows_spec, grid=(steps,), name="oth_out", after=(a_own_far[0],),
+        oth_out_body, device, (x_oth0, x_oth1, a_oth0, a_oth1, *a_oth_far, *a_own, *weights),
+        [*[part_spec] * 8, *weight_specs], half_shape, rows_spec, grid=(steps,), name="oth_out", after=(a_own_far0,),
     )
     out = swap(out)
-    outer0 = outer_taps(0, [mid], BF16)
-    u_own_far0 = inward(u_oth[0])
-    outer1 = outer_taps(1)
-    u_own_far1 = inward(u_oth[1])
-    outer0 = core_stage(outer0, "outer0", after=(u_own_far0,))
+    slices, specs = slices_of(4, BF16)
+    *outer0, rest = call(
+        functools.partial(outer_first_body, steps, tap), device,
+        (*a_own, a_oth0, a_oth1, *a_oth_far, a_own_far0, a_own_far1, u_own, u_oth[0], mid),
+        [*[part_spec] * 8, rows_spec, part_spec, WHOLE], [*slices, shape_of(sums_shape, F32)], [*specs, sums_spec],
+        grid=(steps,), scratch=[pltpu.VMEM(sums_shape, F32)], name="outer_first",
+    )
+    slices, specs = slices_of(2, F32)
+    outer1 = call(
+        functools.partial(outer_second_body, steps, tap), device, (*a_own, *a_oth_far, u_oth[1], rest),
+        [*[part_spec] * 5, WHOLE], slices, specs, grid=(steps,), scratch=[pltpu.VMEM(sums_shape, F32)],
+        name="outer_second",
+    )
+    outer0 = core_stage(outer0, "outer0", after=(u_own_far[0],))
     outer1 = core_stage(outer1, "outer1")
     grad = call(
         oth_grad_body, device, (x_oth0, x_oth1, u_own, *u_oth, u_oth_far, *weights),
@@ -453,24 +484,26 @@
         grid=(steps,), name="oth_grad",
     )
     grad = swap(grad)
+    parts = along_stage([outer0, outer1], 0)
     output = call(
-        own_out_body, device, (genome, *a_own, *a_oth, *a_own_far, *weights),
+        own_out_body, device, (genome, *a_own, a_oth0, a_oth1, a_own_far0, a_own_far1, *weights),
         [own_spec, *[part_spec] * 6, *weight_specs], whole_shape, own_spec, grid=(steps,), name="own_out",
     )
-    parts = along_stage([outer0, outer1], 0)
+    output = place(device, out, output, 0, 0, "place_out")
+    parts = along_stage([parts], 1)
     grad_genome = call(
-        own_grad_body, device, (genome, u_own, *u_oth, u_own_far0, u_own_far1, *weights),
+        own_grad_body, device, (genome, u_own, *u_oth, *u_own_far, *weights),
         [own_spec, rows_spec, *[part_spec] * 4, *weight_specs], whole_shape, own_spec, grid=(steps,), name="own_grad",
     )
-    parts = along_stage([parts], 1)
-    output = place(device, out, output, 0, 0, "place_out")
     parts = side_stage([parts])
-    parts = round_and_spread(parts)
-    parts = gather_along(parts)
+    pieces = round_and_spread(parts)
+    far_pieces = [[to_dp(piece, s) for piece in pieces] for s in range(1, dp_count)]
+    joined = join(pieces, "join")
+    joined_far = [join(far, f"join_far{s}") for s, far in enumerate(far_pieces, 1)]
     grad_genome = place(device, grad, grad_genome, 0, 0, "place_grad")
-    parts = gather_dp(parts)
-    targets = [(1, 0), (1, cols), (0, 0), (2, 0), (0, cols), (2, cols)]
-    grad_weight = write_taps(device, parts, targets, conv_weight.shape, None, "write_taps")
+    grad_weight = write(joined, 0, None)
+    for s, far in enumerate(joined_far, 1):
+        grad_weight = write(far, s, grad_weight)
     return (output[None], grad_genome[None], grad_weight)
 
 

time: 119 us -> 114 us (0.958)
  waiting for transfers between devices: 28.7 us -> 16.1 us
  starting transfers between devices: 47.5 us -> 53.6 us
    ppermute x5, waiting for transfers between devices: 6.63 us -> 1.79 us  [to_along(): return lax.ppermute(value, 'seq', pairs)]
    ppermute x6, waiting for transfers between devices: 13.3 us -> 9.26 us  [swap(): return lax.ppermute(value, 'seq', swap_pairs)]
    ppermute x5, starting transfers between devices: 6.54 us -> 8.69 us  [to_along(): return lax.ppermute(value, 'seq', pairs)]
    ppermute x1, waiting for transfers between devices: 6.1 us -> 4.07 us  [to_side(): return lax.ppermute(value, 'seq', pairs)]
    ppermute x3 -> x4, waiting for transfers between devices: 1.92 us -> 0.01 us  [to_core(): lax.ppermute(value, 'seq', [(i, i - i % tap + (i % tap + shift) % tap) fo...]
    ppermute x3 -> x4, starting transfers between devices: 13.1 us -> 14.8 us  [to_core(): lax.ppermute(value, 'seq', [(i, i - i % tap + (i % tap + shift) % tap) fo...]
    ppermute x3 -> x6, starting transfers between devices: 2.88 us -> 4.62 us  [to_dp(): lax.ppermute(value, 'dp', [(i, (i + shift) % dp_count) for i in range(dp_...]
    ppermute x1, starting transfers between devices: 0.07 us -> 1.52 us  [to_side(): return lax.ppermute(value, 'seq', pairs)]
  transfers between devices with their start and end apart: 25 -> 29, of which waited for: 10 -> 8; matrix products, arithmetic and copies ran while one was open for 0% -> 0% of each run, Pallas kernels for 30% -> 34%
where the time goes in v4:
time: 114 us; the launch traced here: 113 us
  starting transfers between devices  53.6 us (47%)
  Pallas kernels  40.9 us (36%)
  waiting for transfers between devices  16.1 us (14%)
  local copies, waits for them, and re-layouts  1.69 us (1%)
    pallas_call x24, Pallas kernels, call(): pl.pallas_call(chained, grid_spec=pltpu.PrefetchScalarGridSpec(num_scalar...  40.9 us
    ppermute x4, starting transfers between devices, to_core(): lax.ppermute(value, 'seq', [(i, i - i % tap + (i % tap + shift) % tap) fo...  14.8 us
    ppermute x4, starting transfers between devices, inward(): return lax.ppermute(value, 'seq', inner_pairs)  12.7 us
    ppermute x6, waiting for transfers between devices, swap(): return lax.ppermute(value, 'seq', swap_pairs)  9.26 us
    ppermute x5, starting transfers between devices, to_along(): return lax.ppermute(value, 'seq', pairs)  8.69 us
    ppermute x6, starting transfers between devices, swap(): return lax.ppermute(value, 'seq', swap_pairs)  7.4 us
    ppermute x6, starting transfers between devices, to_dp(): lax.ppermute(value, 'dp', [(i, (i + shift) % dp_count) for i in range(dp_...  4.62 us
    ppermute x1, waiting for transfers between devices, to_side(): return lax.ppermute(value, 'seq', pairs)  4.07 us
  transfers between devices with their start and end apart: 29, of which 8 were waited for; matrix products, arithmetic and copies ran while one was open for 0% of the time, Pallas kernels for 34%

profile of v4, /device:TPU:1, one launch (start us, length us, event | category | flops | bytes accessed | tf_op | source)
XLA Modules:
  0.0 113.3 jit_solution(14212204131466727091)
XLA Ops:
  0.7 1.6 %copy-done.1 = bf16[1,2048,512]{2,1,0:T(8,128)(2,1)S(1)} copy-done((bf16[1,2048,512]{2,1,0:T(8,128)(2,1)S(1)}, bf16[1,2048,512]{2,1,0:T(8,128)(2,1)}, u32[]{:S(2)}) %copy-start.1) | copy-done | bytes 2097176
  2.9 2.1 %collective-permute-start = (bf16[1024,256]{1,0:T(8,128)(2,1)S(1)}, bf16[1024,256]{1,0:T(8,128)(2,1)S(1)}, u32[]{:S(2)}, u32[]{:S(2)}) collective-permute-start(bf16[1024,256]{1,0:T(8,128)(2,1)S(1)} %get-tuple-element.61), channel_id=1, source_target_pairs={{0,4},{2,6},{4,0},{6,2},{8,12},{10,14},{12,8},{14,10},{16,20},{18,... | collective-permute-start | bytes 1572872 | tf_op jit(solution)/shard_map/ppermute | solution.py:340
  9.9 4.0 %mid_tap.1 = (f32[2,512,256]{2,1,0:T(8,128)S(1)}, f32[8,128]{1,0:T(8,128)S(1)}) custom-call(s32[6]{0:T(128)S(1)} %stack.27.meta, bf16[2048,512]{1,0:T(8,128)(2,1)S(1)} %bitcast.13, bf16[2048,512]{1,0:T(8,128)(2,1)S(1)} %bitcast.17, f32[8,128]{1,0:T(8,128)S(1)} %get-tuple-element.65.refs_2_), custom_call_target="tpu_custom_call" | custom-call | flops 1 | bytes 200000 | tf_op jit(solution)/shard_map/mid_tap/pallas_call | solution.py:44
  13.9 2.8 %collective-permute-done.refs_0_ = bf16[1024,256]{1,0:T(8,128)(2,1)S(1)} collective-permute-done((bf16[1024,256]{1,0:T(8,128)(2,1)S(1)}, bf16[1024,256]{1,0:T(8,128)(2,1)S(1)}, u32[]{:S(2)}, u32[]{:S(2)}) %collective-permute-start) | collective-permute-done | bytes 524320 | tf_op jit(solution)/shard_map/ppermute | solution.py:340
  17.7 3.1 %collective-permute-start.4 = (bf16[1024,256]{1,0:T(8,128)(2,1)S(1)}, bf16[1024,256]{1,0:T(8,128)(2,1)S(1)}, u32[]{:S(2)}, u32[]{:S(2)}) collective-permute-start(bf16[1024,256]{1,0:T(8,128)(2,1)S(1)} %get-tuple-element.67.refs_2_.refs_3_), channel_id=1, source_target_pairs={{12,4},{14,6},{0,8},{2,10},{20,12},{22,14},{8,16},{10,18},{28,20},... | collective-permute-start | bytes 1572872 | tf_op jit(solution)/shard_map/ppermute | solution.py:346
  21.6 6.4 %collective-permute-done.1.refs_0_.refs_1_ = bf16[1024,256]{1,0:T(8,128)(2,1)S(1)} collective-permute-done((bf16[1024,256]{1,0:T(8,128)(2,1)S(1)}, bf16[1024,256]{1,0:T(8,128)(2,1)S(1)}, u32[]{:S(2)}, u32[]{:S(2)}) %collective-permute-start.1) | collective-permute-done | bytes 524320 | tf_op jit(solution)/shard_map/ppermute | solution.py:340
  29.0 3.1 %collective-permute-start.6 = (bf16[1024,256]{1,0:T(8,128)(2,1)S(1)}, bf16[1024,256]{1,0:T(8,128)(2,1)S(1)}, u32[]{:S(2)}, u32[]{:S(2)}) collective-permute-start(bf16[1024,256]{1,0:T(8,128)(2,1)S(1)} %get-tuple-element.69.refs_3_.refs_4_), channel_id=1, source_target_pairs={{12,4},{14,6},{0,8},{2,10},{20,12},{22,14},{8,16},{10,18},{28,20},... | collective-permute-start | bytes 1572872 | tf_op jit(solution)/shard_map/ppermute | solution.py:346
  34.3 2.9 %oth_out.1 = (bf16[1024,512]{1,0:T(8,128)(2,1)S(1)}, f32[8,128]{1,0:T(8,128)S(1)}) custom-call(s32[6]{0:T(128)S(1)} %stack.27.meta, bf16[1024,256]{1,0:T(8,128)(2,1)S(1)} %collective-permute-done.refs_0_, bf16[1024,256]{1,0:T(8,128)(2,1)S(1)} %collective-permute-done.1.refs_0_.refs_1_, bf16[1024,256]{1,0:T(8,128)(2,1)S(1)} %get-tuple-element.67.refs_2_.refs_3_, ...), custom_call_target="tpu_custom_call" | custom-call | flops 1 | bytes 200000 | tf_op jit(solution)/shard_map/oth_out/pallas_call | solution.py:44
  37.1 3.1 %collective-permute-start.5 = (bf16[1024,512]{1,0:T(8,128)(2,1)S(1)}, bf16[1024,512]{1,0:T(8,128)(2,1)S(1)}, u32[]{:S(2)}, u32[]{:S(2)}) collective-permute-start(bf16[1024,512]{1,0:T(8,128)(2,1)S(1)} %get-tuple-element.73), channel_id=1, source_target_pairs={{0,4},{2,6},{4,0},{6,2},{8,12},{10,14},{12,8},{14,10},{16,20},{18,... | collective-permute-start | bytes 3145736 | tf_op jit(solution)/shard_map/ppermute | solution.py:340
  40.3 3.2 %collective-permute-start.10 = (bf16[1024,256]{1,0:T(8,128)(2,1)S(1)}, bf16[1024,256]{1,0:T(8,128)(2,1)S(1)}, u32[]{:S(2)}, u32[]{:S(2)}) collective-permute-start(bf16[1024,256]{1,0:T(8,128)(2,1)S(1)} %collective-permute-done.7.refs_9_.refs_3_.refs_2_), channel_id=1, source_target_pairs={{12,4},{14,6},{0,8},{2,10},{20,12},{22,14},{8,16},{10,18},{28,20},... | collective-permute-start | bytes 1572872 | tf_op jit(solution)/shard_map/ppermute | solution.py:346
  43.5 3.4 %outer_first.1 = (f32[4,256,256]{2,1,0:T(8,128)S(1)}, bf16[4,256,256]{2,1,0:T(8,128)(2,1)S(1)}, f32[2,512,256]{2,1,0:T(8,128)S(1)}, f32[8,128]{1,0:T(8,128)S(1)}) custom-call(s32[6]{0:T(128)S(1)} %stack.27.meta, bf16[1024,256]{1,0:T(8,128)(2,1)S(1)} %get-tuple-element.70.refs_6_.refs_0_.refs_1_, ...), custom_call_target="tpu_custom_call" | custom-call | flops 1 | bytes 200000 | tf_op jit(solution)/shard_map/outer_first/pallas_call | solution.py:44
  46.9 3.7 %collective-permute-start.8 = (bf16[4,256,256]{2,1,0:T(8,128)(2,1)S(1)}, bf16[4,256,256]{2,1,0:T(8,128)(2,1)S(1)}, u32[]{:S(2)}, u32[]{:S(2)}) collective-permute-start(bf16[4,256,256]{2,1,0:T(8,128)(2,1)S(1)} %get-tuple-element.79), channel_id=1, source_target_pairs={{0,2},{2,0},{4,6},{6,4},{8,10},{10,8},{12,14},{14,12},{16,18},{18,... | collective-permute-start | bytes 1572872 | tf_op jit(solution)/shard_map/ppermute | solution.py:349
  50.6 2.1 %outer_second.1 = (f32[2,256,256]{2,1,0:T(8,128)S(1)}, f32[2,256,256]{2,1,0:T(8,128)S(1)}, f32[8,128]{1,0:T(8,128)S(1)}) custom-call(s32[6]{0:T(128)S(1)} %stack.27.meta, bf16[1024,256]{1,0:T(8,128)(2,1)S(1)} %get-tuple-element.70.refs_6_.refs_0_.refs_1_, bf16[1024,256]{1,0:T(8,128)(2,1)S(1)} %get-tuple-element.71.refs_7_.refs_1_.refs_2_, ...), custom_call_target="tpu_custom_call" | custom-call | flops 1 | bytes 200000 | tf_op jit(solution)/shard_map/outer_second/pallas_call | solution.py:44
  52.8 1.9 %collective-permute-start.12 = (f32[2,256,256]{2,1,0:T(8,128)S(1)}, f32[2,256,256]{2,1,0:T(8,128)S(1)}, u32[]{:S(2)}, u32[]{:S(2)}) collective-permute-start(f32[2,256,256]{2,1,0:T(8,128)S(1)} %get-tuple-element.87), channel_id=1, source_target_pairs={{0,2},{2,0},{4,6},{6,4},{8,10},{10,8},{12,14},{14,12},{16,18},{18,... | collective-permute-start | bytes 1572872 | tf_op jit(solution)/shard_map/ppermute | solution.py:349
  55.5 1.8 %collective-permute-start.11 = (bf16[4,128,256]{2,1,0:T(8,128)(2,1)S(1)}, bf16[4,128,256]{2,1,0:T(8,128)(2,1)S(1)}, u32[]{:S(2)}, u32[]{:S(2)}) collective-permute-start(bf16[4,128,256]{2,1,0:T(8,128)(2,1)S(1)} %get-tuple-element.85), channel_id=1, source_target_pairs={{0,1},{1,0},{2,3},{3,2},{4,5},{5,4},{6,7},{7,6},{8,9},{9,8},{10,11... | collective-permute-start | bytes 786440 | tf_op jit(solution)/shard_map/ppermute | solution.py:352
  57.3 3.2 %collective-permute-start.16 = (bf16[1024,256]{1,0:T(8,128)(2,1)S(1)}, bf16[1024,256]{1,0:T(8,128)(2,1)S(1)}, u32[]{:S(2)}, u32[]{:S(2)}) collective-permute-start(bf16[1024,256]{1,0:T(8,128)(2,1)S(1)} %collective-permute-done.9.refs_4_.refs_3_), channel_id=1, source_target_pairs={{12,4},{14,6},{0,8},{2,10},{20,12},{22,14},{8,16},{10,18},{28,20},... | collective-permute-start | bytes 1572872 | tf_op jit(solution)/shard_map/ppermute | solution.py:346
  61.5 3.8 %oth_grad.1 = (bf16[1024,512]{1,0:T(8,128)(2,1)S(1)}, f32[8,128]{1,0:T(8,128)S(1)}) custom-call(s32[6]{0:T(128)S(1)} %stack.27.meta, bf16[1024,256]{1,0:T(8,128)(2,1)S(1)} %collective-permute-done.refs_0_, bf16[1024,256]{1,0:T(8,128)(2,1)S(1)} %collective-permute-done.1.refs_0_.refs_1_, bf16[1024,512]{1,0:T(8,128)(2,1)S(1)} %get-tuple-element.74.refs_8_.refs_2_.refs_1_, ...), custom_call_target="tpu_custom_call" | custom-call | flops 1 | bytes 200000 | tf_op jit(solution)/shard_map/oth_grad/pallas_call | solution.py:44
  66.3 1.6 %collective-permute-start.17 = (bf16[6,64,256]{2,1,0:T(8,128)(2,1)S(1)}, bf16[6,64,256]{2,1,0:T(8,128)(2,1)S(1)}, u32[]{:S(2)}, u32[]{:S(2)}) collective-permute-start(bf16[6,64,256]{2,1,0:T(8,128)(2,1)S(1)} %get-tuple-element.99), channel_id=1, source_target_pairs={{0,8},{2,10},{4,12},{6,14},{8,0},{10,2},{12,4},{14,6},{16,24},{18,... | collective-permute-start | bytes 589832 | tf_op jit(solution)/shard_map/ppermute | solution.py:369
  69.2 3.7 %own_out.1 = (bf16[2048,512]{1,0:T(8,128)(2,1)}, f32[8,128]{1,0:T(8,128)S(1)}) custom-call(s32[6]{0:T(128)S(1)} %stack.27.meta, bf16[2048,512]{1,0:T(8,128)(2,1)S(1)} %bitcast.14, bf16[1024,256]{1,0:T(8,128)(2,1)S(1)} %get-tuple-element.70.refs_6_.refs_0_.refs_1_, bf16[1024,256]{1,0:T(8,128)(2,1)S(1)} %get-tuple-element.71.refs_7_.refs_1_.refs_2_, ...), custom_call_target="tpu_custom_call" | custom-call | flops 1 | bytes 200000 | tf_op jit(solution)/shard_map/own_out/pallas_call | solution.py:44
  72.9 1.5 %place_out.1 = (bf16[2048,512]{1,0:T(8,128)(2,1)}, f32[8,128]{1,0:T(8,128)S(1)}) custom-call(s32[6]{0:T(128)S(1)} %stack.27.meta, bf16[1024,512]{1,0:T(8,128)(2,1)S(1)} %collective-permute-done.5.refs_0_, bf16[2048,512]{1,0:T(8,128)(2,1)} %get-tuple-element.94.refs_1_, f32[8,128]{1,0:T(8,128)S(1)} %get-tuple-element.95.refs_2_), custom_call_target="tpu_custom_call", output_to_operand_aliasing={{0}: (2, {})} | custom-call | flops 1 | bytes 200000 | tf_op jit(solution)/shard_map/place_out/pallas_call | solution.py:44
  75.1 3.1 %collective-permute-start.18 = (bf16[6,32,256]{2,1,0:T(8,128)(2,1)S(1)}, bf16[6,32,256]{2,1,0:T(8,128)(2,1)S(1)}, u32[]{:S(2)}, u32[]{:S(2)}) collective-permute-start(bf16[6,32,256]{2,1,0:T(8,128)(2,1)S(1)} %get-tuple-element.104), channel_id=1, source_target_pairs={{0,16},{2,18},{4,20},{6,22},{8,24},{10,26},{12,28},{14,30},{16,0},... | collective-permute-start | bytes 294920 | tf_op jit(solution)/shard_map/ppermute | solution.py:369
  78.2 4.6 %own_grad.1 = (bf16[2048,512]{1,0:T(8,128)(2,1)}, f32[8,128]{1,0:T(8,128)S(1)}) custom-call(s32[6]{0:T(128)S(1)} %stack.27.meta, bf16[2048,512]{1,0:T(8,128)(2,1)S(1)} %bitcast.15, bf16[1024,512]{1,0:T(8,128)(2,1)S(1)} %get-tuple-element.74.refs_8_.refs_2_.refs_1_, bf16[1024,256]{1,0:T(8,128)(2,1)S(1)} %collective-permute-done.7.refs_9_.refs_3_.refs_2_, ...), custom_call_target="tpu_custom_call" | custom-call | flops 1 | bytes 200000 | tf_op jit(solution)/shard_map/own_grad/pallas_call | solution.py:44
  83.3 1.5 %collective-permute-start.19 = (f32[6,32,256]{2,1,0:T(8,128)S(1)}, f32[6,32,256]{2,1,0:T(8,128)S(1)}, u32[]{:S(2)}, u32[]{:S(2)}) collective-permute-start(f32[6,32,256]{2,1,0:T(8,128)S(1)} %get-tuple-element.106.refs_0_), channel_id=1, source_target_pairs={{0,12},{2,14},{4,8},{6,10},{8,4},{10,6},{12,0},{14,2},{16,28},{18,... | collective-permute-start | bytes 589832 | tf_op jit(solution)/shard_map/ppermute | solution.py:373
  84.8 4.1 %collective-permute-done.19.refs_1_ = f32[6,32,256]{2,1,0:T(8,128)S(1)} collective-permute-done((f32[6,32,256]{2,1,0:T(8,128)S(1)}, f32[6,32,256]{2,1,0:T(8,128)S(1)}, u32[]{:S(2)}, u32[]{:S(2)}) %collective-permute-start.19) | collective-permute-done | bytes 196640 | tf_op jit(solution)/shard_map/ppermute | solution.py:373
  89.5 2.0 %collective-permute-start.23 = (bf16[6,32,256]{2,1,0:T(8,128)(2,1)S(1)}, bf16[6,32,256]{2,1,0:T(8,128)(2,1)S(1)}, u32[]{:S(2)}, u32[]{:S(2)}) collective-permute-start(bf16[6,32,256]{2,1,0:T(8,128)(2,1)S(1)} %get-tuple-element.108.refs_0_), channel_id=1, source_target_pairs={{0,8},{2,10},{4,12},{6,14},{8,0},{10,2},{12,4},{14,6},{16,24},{18,... | collective-permute-start | bytes 294920 | tf_op jit(solution)/shard_map/ppermute | solution.py:369
  91.5 1.9 %collective-permute-start.25 = (bf16[6,32,256]{2,1,0:T(8,128)(2,1)S(1)}, bf16[6,32,256]{2,1,0:T(8,128)(2,1)S(1)}, u32[]{:S(2)}, u32[]{:S(2)}) collective-permute-start(bf16[6,32,256]{2,1,0:T(8,128)(2,1)S(1)} %get-tuple-element.108.refs_0_), channel_id=1, source_target_pairs={{0,24},{2,26},{4,28},{6,30},{8,16},{10,18},{12,20},{14,22},{16,0},... | collective-permute-start | bytes 294920 | tf_op jit(solution)/shard_map/ppermute | solution.py:369
  94.9 1.4 %collective-permute-start.22 = (bf16[6,32,256]{2,1,0:T(8,128)(2,1)S(1)}, bf16[6,32,256]{2,1,0:T(8,128)(2,1)S(1)}, u32[]{:S(2)}, u32[]{:S(2)}) collective-permute-start(bf16[6,32,256]{2,1,0:T(8,128)(2,1)S(1)} %collective-permute-done.21.refs_1_), channel_id=1, source_target_pairs={{0,1},{1,0},{2,3},{3,2},{4,5},{5,4},{6,7},{7,6},{8,9},{9,8},{10,11... | collective-permute-start | bytes 294920 | tf_op jit(solution)/shard_map/ppermute | solution.py:352
  98.3 6.3 %collective-permute-start.28 = (bf16[6,128,256]{2,1,0:T(8,128)(2,1)S(1)}, bf16[6,128,256]{2,1,0:T(8,128)(2,1)S(1)}, u32[]{:S(2)}, u32[]{:S(2)}) collective-permute-start(bf16[6,128,256]{2,1,0:T(8,128)(2,1)S(1)} %get-tuple-element.114.refs_0_), channel_id=1, source_target_pairs={{0,2},{2,0},{4,6},{6,4},{8,10},{10,8},{12,14},{14,12},{16,18},{18,... | collective-permute-start | bytes 1179656 | tf_op jit(solution)/shard_map/ppermute | solution.py:349
  105.2 2.9 %collective-permute-start.27 = (bf16[6,128,256]{2,1,0:T(8,128)(2,1)S(1)}, bf16[6,128,256]{2,1,0:T(8,128)(2,1)S(1)}, u32[]{:S(2)}, u32[]{:S(2)}) collective-permute-start(bf16[6,128,256]{2,1,0:T(8,128)(2,1)S(1)} %get-tuple-element.113.refs_0_), channel_id=1, source_target_pairs={{0,2},{2,0},{4,6},{6,4},{8,10},{10,8},{12,14},{14,12},{16,18},{18,... | collective-permute-start | bytes 1179656 | tf_op jit(solution)/shard_map/ppermute | solution.py:349
  108.1 1.5 %place_grad.1 = (bf16[2048,512]{1,0:T(8,128)(2,1)}, f32[8,128]{1,0:T(8,128)S(1)}) custom-call(s32[6]{0:T(128)S(1)} %stack.27.meta, bf16[1024,512]{1,0:T(8,128)(2,1)S(1)} %collective-permute-done.15.refs_0_, bf16[2048,512]{1,0:T(8,128)(2,1)} %get-tuple-element.102.refs_1_, f32[8,128]{1,0:T(8,128)S(1)} %get-tuple-element.111.refs_2_), custom_call_target="tpu_custom_call", output_to_operand_aliasing={{0}: (2, {})} | custom-call | flops 1 | bytes 200000 | tf_op jit(solution)/shard_map/place_grad/pallas_call | solution.py:44
  109.7 1.8 %write_taps0.1 = (f32[3,512,512]{2,1,0:T(8,128)}, f32[8,128]{1,0:T(8,128)S(1)}) custom-call(s32[6]{0:T(128)S(1)} %stack.27.meta, bf16[6,128,256]{2,1,0:T(8,128)(2,1)S(1)} %get-tuple-element.114.refs_0_, bf16[6,128,256]{2,1,0:T(8,128)(2,1)S(1)} %collective-permute-done.28.refs_1_, f32[8,128]{1,0:T(8,128)S(1)} %get-tuple-element.115.refs_2_), custom_call_target="tpu_custom_call" | custom-call | flops 1 | bytes 200000 | tf_op jit(solution)/shard_map/write_taps0/pallas_call | solution.py:44
  111.5 1.8 %write_taps1.1 = (f32[3,512,512]{2,1,0:T(8,128)}, f32[8,128]{1,0:T(8,128)}) custom-call(s32[6]{0:T(128)S(1)} %stack.27.meta, bf16[6,128,256]{2,1,0:T(8,128)(2,1)S(1)} %get-tuple-element.113.refs_0_, bf16[6,128,256]{2,1,0:T(8,128)(2,1)S(1)} %collective-permute-done.27.refs_1_, ...), custom_call_target="tpu_custom_call", output_to_operand_aliasing={{0}: (3, {})} | custom-call | flops 1 | bytes 200000 | tf_op jit(solution)/shard_map/write_taps1/pallas_call | solution.py:44
  (59 shorter events, 20.2 us)
Async XLA Ops:
  2.3 4.1 %copy-start.3 = (bf16[1,2048,512]{2,1,0:T(8,128)(2,1)S(1)}, bf16[1,2048,512]{2,1,0:T(8,128)(2,1)}, u32[]{:S(2)}) copy-start(bf16[1,2048,512]{2,1,0:T(8,128)(2,1)} %param.5) | copy-start | bytes 6291460
  2.9 13.8 %collective-permute-start = (bf16[1024,256]{1,0:T(8,128)(2,1)S(1)}, bf16[1024,256]{1,0:T(8,128)(2,1)S(1)}, u32[]{:S(2)}, u32[]{:S(2)}) collective-permute-start(bf16[1024,256]{1,0:T(8,128)(2,1)S(1)} %get-tuple-element.61), channel_id=1, source_target_pairs={{0,4},{2,6},{4,0},{6,2},{8,12},{10,14},{12,8},{14,10},{16,20},{18,... | collective-permute-start | bytes 1572872 | tf_op jit(solution)/shard_map/ppermute | solution.py:340
  7.2 20.7 %collective-permute-start.1 = (bf16[1024,256]{1,0:T(8,128)(2,1)S(1)}, bf16[1024,256]{1,0:T(8,128)(2,1)S(1)}, u32[]{:S(2)}, u32[]{:S(2)}) collective-permute-start(bf16[1024,256]{1,0:T(8,128)(2,1)S(1)} %get-tuple-element.64), channel_id=1, source_target_pairs={{0,4},{2,6},{4,0},{6,2},{8,12},{10,14},{12,8},{14,10},{16,20},{18,... | collective-permute-start | bytes 1572872 | tf_op jit(solution)/shard_map/ppermute | solution.py:340
  7.3 24.8 %collective-permute-start.2 = (bf16[1024,256]{1,0:T(8,128)(2,1)S(1)}, bf16[1024,256]{1,0:T(8,128)(2,1)S(1)}, u32[]{:S(2)}, u32[]{:S(2)}) collective-permute-start(bf16[1024,256]{1,0:T(8,128)(2,1)S(1)} %get-tuple-element.70.refs_6_.refs_0_.refs_1_), channel_id=1, source_target_pairs={{4,12},{6,14},{8,0},{10,2},{12,20},{14,22},{16,8},{18,10},{20,28},... | collective-permute-start | bytes 1572872 | tf_op jit(solution)/shard_map/ppermute | solution.py:343
  8.6 24.3 %collective-permute-start.3 = (bf16[1024,256]{1,0:T(8,128)(2,1)S(1)}, bf16[1024,256]{1,0:T(8,128)(2,1)S(1)}, u32[]{:S(2)}, u32[]{:S(2)}) collective-permute-start(bf16[1024,256]{1,0:T(8,128)(2,1)S(1)} %get-tuple-element.71.refs_7_.refs_1_.refs_2_), channel_id=1, source_target_pairs={{4,12},{6,14},{8,0},{10,2},{12,20},{14,22},{16,8},{18,10},{20,28},... | collective-permute-start | bytes 1572872 | tf_op jit(solution)/shard_map/ppermute | solution.py:343
  9.9 24.3 %copy-start = (bf16[3,512,512]{2,1,0:T(8,128)(2,1)S(1)}, bf16[3,512,512]{2,1,0:T(8,128)(2,1)}, u32[]{:S(2)}) copy-start(bf16[3,512,512]{2,1,0:T(8,128)(2,1)} %refs_8_.7) | copy-start | bytes 4718596
  17.7 16.5 %collective-permute-start.4 = (bf16[1024,256]{1,0:T(8,128)(2,1)S(1)}, bf16[1024,256]{1,0:T(8,128)(2,1)S(1)}, u32[]{:S(2)}, u32[]{:S(2)}) collective-permute-start(bf16[1024,256]{1,0:T(8,128)(2,1)S(1)} %get-tuple-element.67.refs_2_.refs_3_), channel_id=1, source_target_pairs={{12,4},{14,6},{0,8},{2,10},{20,12},{22,14},{8,16},{10,18},{28,20},... | collective-permute-start | bytes 1572872 | tf_op jit(solution)/shard_map/ppermute | solution.py:346
  20.9 19.4 %collective-permute-start.7 = (bf16[1024,256]{1,0:T(8,128)(2,1)S(1)}, bf16[1024,256]{1,0:T(8,128)(2,1)S(1)}, u32[]{:S(2)}, u32[]{:S(2)}) collective-permute-start(bf16[1024,256]{1,0:T(8,128)(2,1)S(1)} %get-tuple-element.75), channel_id=1, source_target_pairs={{0,4},{2,6},{4,0},{6,2},{8,12},{10,14},{12,8},{14,10},{16,20},{18,... | collective-permute-start | bytes 1572872 | tf_op jit(solution)/shard_map/ppermute | solution.py:340
  29.0 14.5 %collective-permute-start.6 = (bf16[1024,256]{1,0:T(8,128)(2,1)S(1)}, bf16[1024,256]{1,0:T(8,128)(2,1)S(1)}, u32[]{:S(2)}, u32[]{:S(2)}) collective-permute-start(bf16[1024,256]{1,0:T(8,128)(2,1)S(1)} %get-tuple-element.69.refs_3_.refs_4_), channel_id=1, source_target_pairs={{12,4},{14,6},{0,8},{2,10},{20,12},{22,14},{8,16},{10,18},{28,20},... | collective-permute-start | bytes 1572872 | tf_op jit(solution)/shard_map/ppermute | solution.py:346
  32.1 18.5 %collective-permute-start.9 = (bf16[1024,256]{1,0:T(8,128)(2,1)S(1)}, bf16[1024,256]{1,0:T(8,128)(2,1)S(1)}, u32[]{:S(2)}, u32[]{:S(2)}) collective-permute-start(bf16[1024,256]{1,0:T(8,128)(2,1)S(1)} %get-tuple-element.80), channel_id=1, source_target_pairs={{0,4},{2,6},{4,0},{6,2},{8,12},{10,14},{12,8},{14,10},{16,20},{18,... | collective-permute-start | bytes 1572872 | tf_op jit(solution)/shard_map/ppermute | solution.py:340
  33.0 28.6 %collective-permute-start.14 = (bf16[1024,512]{1,0:T(8,128)(2,1)S(1)}, bf16[1024,512]{1,0:T(8,128)(2,1)S(1)}, u32[]{:S(2)}, u32[]{:S(2)}) collective-permute-start(bf16[1024,512]{1,0:T(8,128)(2,1)S(1)} %get-tuple-element.74.refs_8_.refs_2_.refs_1_), channel_id=1, source_target_pairs={{4,12},{6,14},{8,0},{10,2},{12,20},{14,22},{16,8},{18,10},{20,28},... | collective-permute-start | bytes 3145736 | tf_op jit(solution)/shard_map/ppermute | solution.py:343
  37.1 35.8 %collective-permute-start.5 = (bf16[1024,512]{1,0:T(8,128)(2,1)S(1)}, bf16[1024,512]{1,0:T(8,128)(2,1)S(1)}, u32[]{:S(2)}, u32[]{:S(2)}) collective-permute-start(bf16[1024,512]{1,0:T(8,128)(2,1)S(1)} %get-tuple-element.73), channel_id=1, source_target_pairs={{0,4},{2,6},{4,0},{6,2},{8,12},{10,14},{12,8},{14,10},{16,20},{18,... | collective-permute-start | bytes 3145736 | tf_op jit(solution)/shard_map/ppermute | solution.py:340
  40.3 14.4 %collective-permute-start.10 = (bf16[1024,256]{1,0:T(8,128)(2,1)S(1)}, bf16[1024,256]{1,0:T(8,128)(2,1)S(1)}, u32[]{:S(2)}, u32[]{:S(2)}) collective-permute-start(bf16[1024,256]{1,0:T(8,128)(2,1)S(1)} %collective-permute-done.7.refs_9_.refs_3_.refs_2_), channel_id=1, source_target_pairs={{12,4},{14,6},{0,8},{2,10},{20,12},{22,14},{8,16},{10,18},{28,20},... | collective-permute-start | bytes 1572872 | tf_op jit(solution)/shard_map/ppermute | solution.py:346
  46.9 7.8 %collective-permute-start.8 = (bf16[4,256,256]{2,1,0:T(8,128)(2,1)S(1)}, bf16[4,256,256]{2,1,0:T(8,128)(2,1)S(1)}, u32[]{:S(2)}, u32[]{:S(2)}) collective-permute-start(bf16[4,256,256]{2,1,0:T(8,128)(2,1)S(1)} %get-tuple-element.79), channel_id=1, source_target_pairs={{0,2},{2,0},{4,6},{6,4},{8,10},{10,8},{12,14},{14,12},{16,18},{18,... | collective-permute-start | bytes 1572872 | tf_op jit(solution)/shard_map/ppermute | solution.py:349
  52.8 7.8 %collective-permute-start.12 = (f32[2,256,256]{2,1,0:T(8,128)S(1)}, f32[2,256,256]{2,1,0:T(8,128)S(1)}, u32[]{:S(2)}, u32[]{:S(2)}) collective-permute-start(f32[2,256,256]{2,1,0:T(8,128)S(1)} %get-tuple-element.87), channel_id=1, source_target_pairs={{0,2},{2,0},{4,6},{6,4},{8,10},{10,8},{12,14},{14,12},{16,18},{18,... | collective-permute-start | bytes 1572872 | tf_op jit(solution)/shard_map/ppermute | solution.py:349
  55.5 10.1 %collective-permute-start.11 = (bf16[4,128,256]{2,1,0:T(8,128)(2,1)S(1)}, bf16[4,128,256]{2,1,0:T(8,128)(2,1)S(1)}, u32[]{:S(2)}, u32[]{:S(2)}) collective-permute-start(bf16[4,128,256]{2,1,0:T(8,128)(2,1)S(1)} %get-tuple-element.85), channel_id=1, source_target_pairs={{0,1},{1,0},{2,3},{3,2},{4,5},{5,4},{6,7},{7,6},{8,9},{9,8},{10,11... | collective-permute-start | bytes 786440 | tf_op jit(solution)/shard_map/ppermute | solution.py:352
  57.3 20.8 %collective-permute-start.16 = (bf16[1024,256]{1,0:T(8,128)(2,1)S(1)}, bf16[1024,256]{1,0:T(8,128)(2,1)S(1)}, u32[]{:S(2)}, u32[]{:S(2)}) collective-permute-start(bf16[1024,256]{1,0:T(8,128)(2,1)S(1)} %collective-permute-done.9.refs_4_.refs_3_), channel_id=1, source_target_pairs={{12,4},{14,6},{0,8},{2,10},{20,12},{22,14},{8,16},{10,18},{28,20},... | collective-permute-start | bytes 1572872 | tf_op jit(solution)/shard_map/ppermute | solution.py:346
  61.2 4.4 %collective-permute-start.13 = (bf16[2,128,256]{2,1,0:T(8,128)(2,1)S(1)}, bf16[2,128,256]{2,1,0:T(8,128)(2,1)S(1)}, u32[]{:S(2)}, u32[]{:S(2)}) collective-permute-start(bf16[2,128,256]{2,1,0:T(8,128)(2,1)S(1)} %get-tuple-element.90), channel_id=1, source_target_pairs={{0,1},{1,0},{2,3},{3,2},{4,5},{5,4},{6,7},{7,6},{8,9},{9,8},{10,11... | collective-permute-start | bytes 393224 | tf_op jit(solution)/shard_map/ppermute | solution.py:352
  61.5 7.6 %copy-start.2 = (bf16[1,2048,512]{2,1,0:T(8,128)(2,1)S(1)}, bf16[1,2048,512]{2,1,0:T(8,128)(2,1)}, u32[]{:S(2)}) copy-start(bf16[1,2048,512]{2,1,0:T(8,128)(2,1)} %param.3) | copy-start | bytes 6291460
  66.3 8.1 %collective-permute-start.17 = (bf16[6,64,256]{2,1,0:T(8,128)(2,1)S(1)}, bf16[6,64,256]{2,1,0:T(8,128)(2,1)S(1)}, u32[]{:S(2)}, u32[]{:S(2)}) collective-permute-start(bf16[6,64,256]{2,1,0:T(8,128)(2,1)S(1)} %get-tuple-element.99), channel_id=1, source_target_pairs={{0,8},{2,10},{4,12},{6,14},{8,0},{10,2},{12,4},{14,6},{16,24},{18,... | collective-permute-start | bytes 589832 | tf_op jit(solution)/shard_map/ppermute | solution.py:369
  67.9 40.2 %collective-permute-start.15 = (bf16[1024,512]{1,0:T(8,128)(2,1)S(1)}, bf16[1024,512]{1,0:T(8,128)(2,1)S(1)}, u32[]{:S(2)}, u32[]{:S(2)}) collective-permute-start(bf16[1024,512]{1,0:T(8,128)(2,1)S(1)} %get-tuple-element.97), channel_id=1, source_target_pairs={{0,4},{2,6},{4,0},{6,2},{8,12},{10,14},{12,8},{14,10},{16,20},{18,... | collective-permute-start | bytes 3145736 | tf_op jit(solution)/shard_map/ppermute | solution.py:340
  75.1 7.6 %collective-permute-start.18 = (bf16[6,32,256]{2,1,0:T(8,128)(2,1)S(1)}, bf16[6,32,256]{2,1,0:T(8,128)(2,1)S(1)}, u32[]{:S(2)}, u32[]{:S(2)}) collective-permute-start(bf16[6,32,256]{2,1,0:T(8,128)(2,1)S(1)} %get-tuple-element.104), channel_id=1, source_target_pairs={{0,16},{2,18},{4,20},{6,22},{8,24},{10,26},{12,28},{14,30},{16,0},... | collective-permute-start | bytes 294920 | tf_op jit(solution)/shard_map/ppermute | solution.py:369
  83.3 5.6 %collective-permute-start.19 = (f32[6,32,256]{2,1,0:T(8,128)S(1)}, f32[6,32,256]{2,1,0:T(8,128)S(1)}, u32[]{:S(2)}, u32[]{:S(2)}) collective-permute-start(f32[6,32,256]{2,1,0:T(8,128)S(1)} %get-tuple-element.106.refs_0_), channel_id=1, source_target_pairs={{0,12},{2,14},{4,8},{6,10},{8,4},{10,6},{12,0},{14,2},{16,28},{18,... | collective-permute-start | bytes 589832 | tf_op jit(solution)/shard_map/ppermute | solution.py:373
  89.5 5.4 %collective-permute-start.21 = (bf16[6,32,256]{2,1,0:T(8,128)(2,1)S(1)}, bf16[6,32,256]{2,1,0:T(8,128)(2,1)S(1)}, u32[]{:S(2)}, u32[]{:S(2)}) collective-permute-start(bf16[6,32,256]{2,1,0:T(8,128)(2,1)S(1)} %get-tuple-element.108.refs_0_), channel_id=1, source_target_pairs={{0,16},{2,18},{4,20},{6,22},{8,24},{10,26},{12,28},{14,30},{16,8},... | collective-permute-start | bytes 294920 | tf_op jit(solution)/shard_map/ppermute | solution.py:369
  89.5 6.7 %collective-permute-start.23 = (bf16[6,32,256]{2,1,0:T(8,128)(2,1)S(1)}, bf16[6,32,256]{2,1,0:T(8,128)(2,1)S(1)}, u32[]{:S(2)}, u32[]{:S(2)}) collective-permute-start(bf16[6,32,256]{2,1,0:T(8,128)(2,1)S(1)} %get-tuple-element.108.refs_0_), channel_id=1, source_target_pairs={{0,8},{2,10},{4,12},{6,14},{8,0},{10,2},{12,4},{14,6},{16,24},{18,... | collective-permute-start | bytes 294920 | tf_op jit(solution)/shard_map/ppermute | solution.py:369
  91.5 5.9 %collective-permute-start.25 = (bf16[6,32,256]{2,1,0:T(8,128)(2,1)S(1)}, bf16[6,32,256]{2,1,0:T(8,128)(2,1)S(1)}, u32[]{:S(2)}, u32[]{:S(2)}) collective-permute-start(bf16[6,32,256]{2,1,0:T(8,128)(2,1)S(1)} %get-tuple-element.108.refs_0_), channel_id=1, source_target_pairs={{0,24},{2,26},{4,28},{6,30},{8,16},{10,18},{12,20},{14,22},{16,0},... | collective-permute-start | bytes 294920 | tf_op jit(solution)/shard_map/ppermute | solution.py:369
  93.5 4.9 %collective-permute-start.20 = (bf16[6,32,256]{2,1,0:T(8,128)(2,1)S(1)}, bf16[6,32,256]{2,1,0:T(8,128)(2,1)S(1)}, u32[]{:S(2)}, u32[]{:S(2)}) collective-permute-start(bf16[6,32,256]{2,1,0:T(8,128)(2,1)S(1)} %get-tuple-element.108.refs_0_), channel_id=1, source_target_pairs={{0,1},{1,0},{2,3},{3,2},{4,5},{5,4},{6,7},{7,6},{8,9},{9,8},{10,11... | collective-permute-start | bytes 294920 | tf_op jit(solution)/shard_map/ppermute | solution.py:352
  94.9 9.7 %collective-permute-start.22 = (bf16[6,32,256]{2,1,0:T(8,128)(2,1)S(1)}, bf16[6,32,256]{2,1,0:T(8,128)(2,1)S(1)}, u32[]{:S(2)}, u32[]{:S(2)}) collective-permute-start(bf16[6,32,256]{2,1,0:T(8,128)(2,1)S(1)} %collective-permute-done.21.refs_1_), channel_id=1, source_target_pairs={{0,1},{1,0},{2,3},{3,2},{4,5},{5,4},{6,7},{7,6},{8,9},{9,8},{10,11... | collective-permute-start | bytes 294920 | tf_op jit(solution)/shard_map/ppermute | solution.py:352
  96.3 8.3 %collective-permute-start.24 = (bf16[6,32,256]{2,1,0:T(8,128)(2,1)S(1)}, bf16[6,32,256]{2,1,0:T(8,128)(2,1)S(1)}, u32[]{:S(2)}, u32[]{:S(2)}) collective-permute-start(bf16[6,32,256]{2,1,0:T(8,128)(2,1)S(1)} %collective-permute-done.23.refs_2_), channel_id=1, source_target_pairs={{0,1},{1,0},{2,3},{3,2},{4,5},{5,4},{6,7},{7,6},{8,9},{9,8},{10,11... | collective-permute-start | bytes 294920 | tf_op jit(solution)/shard_map/ppermute | solution.py:352
  97.5 7.2 %collective-permute-start.26 = (bf16[6,32,256]{2,1,0:T(8,128)(2,1)S(1)}, bf16[6,32,256]{2,1,0:T(8,128)(2,1)S(1)}, u32[]{:S(2)}, u32[]{:S(2)}) collective-permute-start(bf16[6,32,256]{2,1,0:T(8,128)(2,1)S(1)} %collective-permute-done.25.refs_3_), channel_id=1, source_target_pairs={{0,1},{1,0},{2,3},{3,2},{4,5},{5,4},{6,7},{7,6},{8,9},{9,8},{10,11... | collective-permute-start | bytes 294920 | tf_op jit(solution)/shard_map/ppermute | solution.py:352
  98.3 11.3 %collective-permute-start.28 = (bf16[6,128,256]{2,1,0:T(8,128)(2,1)S(1)}, bf16[6,128,256]{2,1,0:T(8,128)(2,1)S(1)}, u32[]{:S(2)}, u32[]{:S(2)}) collective-permute-start(bf16[6,128,256]{2,1,0:T(8,128)(2,1)S(1)} %get-tuple-element.114.refs_0_), channel_id=1, source_target_pairs={{0,2},{2,0},{4,6},{6,4},{8,10},{10,8},{12,14},{14,12},{16,18},{18,... | collective-permute-start | bytes 1179656 | tf_op jit(solution)/shard_map/ppermute | solution.py:349
  105.2 6.3 %collective-permute-start.27 = (bf16[6,128,256]{2,1,0:T(8,128)(2,1)S(1)}, bf16[6,128,256]{2,1,0:T(8,128)(2,1)S(1)}, u32[]{:S(2)}, u32[]{:S(2)}) collective-permute-start(bf16[6,128,256]{2,1,0:T(8,128)(2,1)S(1)} %get-tuple-element.113.refs_0_), channel_id=1, source_target_pairs={{0,2},{2,0},{4,6},{6,4},{8,10},{10,8},{12,14},{14,12},{16,18},{18,... | collective-permute-start | bytes 1179656 | tf_op jit(solution)/shard_map/ppermute | solution.py:349
  (1 other events, 1.6 us)

commit v5 on v4

--- a/solution.py
+++ b/solution.py
@@ -10,7 +10,6 @@
 DILATION_BINS = 4096
 BF16, F32 = jnp.bfloat16, jnp.float32
 VMEM_BYTES = 40 * 1024 * 1024
-COSTS = {}
 SIDE, CORE, DP, ALONG, ALONG_BITS = range(5)
 HBM = pl.BlockSpec(memory_space=pltpu.HBM)
 WHOLE = pl.BlockSpec(memory_space=pltpu.VMEM)
@@ -50,7 +49,7 @@
         out_shape=[*outs, TOKEN],
         input_output_aliases=aliases or {},
         compiler_params=pltpu.CompilerParams(vmem_limit_bytes=VMEM_BYTES),
-        cost_estimate=pl.CostEstimate(flops=1, bytes_accessed=COSTS.get(name, 200_000), transcendentals=0),
+        cost_estimate=pl.CostEstimate(flops=1, bytes_accessed=200_000, transcendentals=0),
         name=name,
     )(device.meta, *operands, *tokens)
     device.token = results[-1]
@@ -177,18 +176,28 @@
     )
 
 
-def write_taps_body(shifts, groups, targets, aliased, meta, *refs):
-    parts = refs[: len(shifts)]
-    out, wide, sems = refs[len(shifts) + aliased :]
+def returned_copy(meta, part, out, sem):
+    rows = part.shape[0]
+    start = pl.multiple_of((1 - meta[SIDE]) * rows, rows)
+    return pltpu.make_async_copy(part, out.at[pl.ds(start, rows)], sem)
+
+
+def write_taps_body(shifts, groups, targets, aliased, placing, meta, *refs):
+    parts, refs = refs[: len(shifts)], refs[len(shifts) :]
+    returned, refs = refs[: 2 * placing], refs[2 * placing + aliased :]
+    out, wide, sems = refs[0], refs[-2 - placing], refs[-1 - placing]
     rows, cols = parts[0].shape[1:]
     cores, dps = groups
     copies = []
+    if placing:
+        copies.append(returned_copy(meta, returned[0], refs[1], refs[-1]))
+        copies[0].start()
     for m, (part, (core_shift, dp_shift)) in enumerate(zip(parts, shifts)):
         core = lax.rem(meta[CORE] + cores - core_shift, cores)
         dp = lax.rem(meta[DP] + dps - dp_shift, dps)
         first = pl.multiple_of((core * dps + dp) * rows, rows)
-        wide[m] = part[...].astype(F32)
         for n, (tap, col) in enumerate(targets):
+            wide[m, n] = part[n].astype(F32)
             window = out.at[tap, pl.ds(first, rows), pl.ds(col, cols)]
             copy = pltpu.make_async_copy(wide.at[m, n], window, sems.at[m, n])
             copy.start()
@@ -197,16 +206,24 @@
         copy.wait()
 
 
-def write_taps(device, parts, shifts, groups, targets, shape, buffer, name, after=()):
-    extra = [] if buffer is None else [buffer]
-    return call(
-        functools.partial(write_taps_body, shifts, groups, targets, len(extra)), device, (*parts, *extra),
-        [WHOLE] * len(parts) + [HBM] * len(extra), shape_of(shape, F32), HBM,
+def write_taps(device, parts, shifts, groups, targets, shape, buffer, name, returned=None, after=()):
+    extra, place = [] if buffer is None else [buffer], returned or []
+    outs, aliases = [shape_of(shape, F32)], {}
+    if place:
+        outs.append(shape_of(place[1].shape, place[1].dtype))
+        aliases[2 + len(parts)] = 1
+    if extra:
+        aliases[1 + len(parts) + len(place)] = 0
+    results = call(
+        functools.partial(write_taps_body, shifts, groups, targets, len(extra), len(place) // 2), device,
+        (*parts, *place, *extra), [WHOLE] * len(parts) + [HBM] * (len(place) + len(extra)), outs, [HBM] * len(outs),
         scratch=[
-            pltpu.VMEM((len(parts), *parts[0].shape), F32), pltpu.SemaphoreType.DMA((len(parts), len(targets)))
+            pltpu.VMEM((len(parts), *parts[0].shape), F32), pltpu.SemaphoreType.DMA((len(parts), len(targets))),
+            *[pltpu.SemaphoreType.DMA] * (len(place) // 2),
         ],
-        aliases={1 + len(parts): 0} if extra else None, name=name, after=after,
-    )
+        aliases=aliases, name=name, after=after,
+    )
+    return results
 
 
 def act_body(meta, x, *acts):
@@ -292,26 +309,24 @@
         grad[:, part] = (u[...].astype(F32) + slope * grad_act[:, part]).astype(BF16)
 
 
-def own_grad_body(meta, x, u_own, oth0, oth1, far0, far1, w_near, w_mid, w_far, grad):
+def own_grad_body(
+    steps, meta, x, u_own, oth0, oth1, far0, far1, w_near, w_mid, w_far, returned, buffer, grad, out, sem
+):
+    i = pl.program_id(0)
+    copy = returned_copy(meta, returned, out, sem)
+
+    @pl.when(i == 0)
+    def _():
+        copy.start()
+
     _, slope = gelu_and_slope(x[...].astype(F32))
     u = u_own[...]
     grad_act = mm_back(u, w_mid[0]) + mm_back_parts((oth0, oth1), w_far) + mm_back_parts((far0, far1), w_near)
     grad[...] = (u.astype(F32) + slope * grad_act).astype(BF16)
 
-
-def place_body(row, col, meta, part, buffer, out, sem):
-    rows, cols = part.shape
-    start = pl.multiple_of((1 - meta[SIDE]) * (buffer.shape[0] // 2), rows) + row
-    copy = pltpu.make_async_copy(part, out.at[pl.ds(pl.multiple_of(start, 16), rows), pl.ds(col, cols)], sem)
-    copy.start()
-    copy.wait()
-
-
-def place(device, part, buffer, row, col, name, after=()):
-    return call(
-        functools.partial(place_body, row, col), device, (part, buffer), [HBM, HBM],
-        shape_of(buffer.shape, buffer.dtype), HBM, scratch=[pltpu.SemaphoreType.DMA], aliases={2: 0}, name=name, after=after,
-    )
+    @pl.when(i == steps - 1)
+    def _():
+        copy.wait()
 
 
 def per_device(genome, conv_weight, upstream):
@@ -406,10 +421,12 @@
             total = lax.psum(total, "seq", axis_index_groups=together)
         return [total, to_side(total)]
 
-    def round_and_spread(parts, after=()):
-        (total,) = reduce(device, [parts], dtype=BF16, name="side", after=after)
+    def round_slice(parts, after=()):
+        return reduce(device, [parts], dtype=BF16, name="side", after=after)[0]
+
+    def spread(value):
         moves = [lambda position, s=s: (position + s) % along_count for s in range(1, along_count)]
-        return [total] + [to_along(total, move) for move in moves if staged]
+        return [value] + [to_along(value, move) for move in moves if staged]
 
     def join(pieces, name, after=()):
         total = gather(device, pieces, ALONG, name, after) if staged else pieces[0]
@@ -417,10 +434,11 @@
 
     targets = [(1, 0), (1, cols), (0, 0), (2, 0), (0, cols), (2, cols)]
 
-    def write(joined, dp_shift, buffer, after=()):
+    def write(joined, dp_shift, buffer, returned=None, after=()):
         shifts = [(core_shift, dp_shift) for core_shift in range(tap)]
         return write_taps(
-            device, joined, shifts, (tap, dp_count), targets, conv_weight.shape, buffer, f"write_taps{dp_shift}", after
+            device, joined, shifts, (tap, dp_count), targets, conv_weight.shape, buffer, f"write_taps{dp_shift}",
+            returned, after,
         )
 
     def slices_of(parts, dtype):
@@ -489,21 +507,23 @@
         own_out_body, device, (genome, *a_own, a_oth0, a_oth1, a_own_far0, a_own_far1, *weights),
         [own_spec, *[part_spec] * 6, *weight_specs], whole_shape, own_spec, grid=(steps,), name="own_out",
     )
-    output = place(device, out, output, 0, 0, "place_out")
     parts = along_stage([parts], 1)
-    grad_genome = call(
-        own_grad_body, device, (genome, u_own, *u_oth, *u_own_far, *weights),
-        [own_spec, rows_spec, *[part_spec] * 4, *weight_specs], whole_shape, own_spec, grid=(steps,), name="own_grad",
+    grad_genome, output = call(
+        functools.partial(own_grad_body, steps), device,
+        (genome, u_own, *u_oth, *u_own_far, *weights, out, output),
+        [own_spec, rows_spec, *[part_spec] * 4, *weight_specs, HBM, HBM], [whole_shape] * 2, [own_spec, HBM],
+        grid=(steps,), scratch=[pltpu.SemaphoreType.DMA], aliases={11: 1}, name="own_grad",
     )
     parts = side_stage([parts])
-    pieces = round_and_spread(parts)
-    far_pieces = [[to_dp(piece, s) for piece in pieces] for s in range(1, dp_count)]
+    last_slice = round_slice(parts)
+    far_slices = [to_dp(last_slice, s) for s in range(1, dp_count)]
+    pieces = spread(last_slice)
+    far_pieces = [[far] + [to_dp(piece, s) for piece in pieces[1:]] for s, far in enumerate(far_slices, 1)]
     joined = join(pieces, "join")
     joined_far = [join(far, f"join_far{s}") for s, far in enumerate(far_pieces, 1)]
-    grad_genome = place(device, grad, grad_genome, 0, 0, "place_grad")
-    grad_weight = write(joined, 0, None)
+    grad_weight, grad_genome = write(joined, 0, None, [grad, grad_genome])
     for s, far in enumerate(joined_far, 1):
-        grad_weight = write(far, s, grad_weight)
+        (grad_weight,) = write(far, s, grad_weight)
     return (output[None], grad_genome[None], grad_weight)
 
 

time: 114 us -> 113 us (level)
  Pallas kernels: 40.9 us -> 38.2 us
  starting transfers between devices: 53.6 us -> 55.4 us
    ppermute x4, starting transfers between devices: 14.8 us -> 9.96 us  [to_core(): lax.ppermute(value, 'seq', [(i, i - i % tap + (i % tap + shift) % tap) fo...]
    ppermute x6, starting transfers between devices: 4.62 us -> 9.25 us  [to_dp(): lax.ppermute(value, 'dp', [(i, (i + shift) % dp_count) for i in range(dp_...]
    pallas_call x24 -> x22, Pallas kernels: 40.9 us -> 38.2 us  [call(): pl.pallas_call(chained, grid_spec=pltpu.PrefetchScalarGridSpec(num_scalar...]
    ppermute x6, waiting for transfers between devices: 9.26 us -> 11.3 us  [swap(): return lax.ppermute(value, 'seq', swap_pairs)]
    ppermute x6, starting transfers between devices: 7.4 us -> 9.11 us  [swap(): return lax.ppermute(value, 'seq', swap_pairs)]
  transfers between devices with their start and end apart: 29 -> 29, of which waited for: 8 -> 7; matrix products, arithmetic and copies ran while one was open for 0% -> 0% of each run, Pallas kernels for 34% -> 32%
where the time goes in v5:
time: 113 us
  starting transfers between devices  55.4 us (49%)
  Pallas kernels  38.2 us (34%)
  waiting for transfers between devices  16.4 us (15%)
  local copies, waits for them, and re-layouts  1.69 us (1%)
    pallas_call x22, Pallas kernels, call(): pl.pallas_call(chained, grid_spec=pltpu.PrefetchScalarGridSpec(num_scalar...  38.2 us
    ppermute x4, starting transfers between devices, inward(): return lax.ppermute(value, 'seq', inner_pairs)  13.2 us
    ppermute x6, waiting for transfers between devices, swap(): return lax.ppermute(value, 'seq', swap_pairs)  11.3 us
    ppermute x4, starting transfers between devices, to_core(): lax.ppermute(value, 'seq', [(i, i - i % tap + (i % tap + shift) % tap) fo...  9.96 us
    ppermute x6, starting transfers between devices, to_dp(): lax.ppermute(value, 'dp', [(i, (i + shift) % dp_count) for i in range(dp_...  9.25 us
    ppermute x6, starting transfers between devices, swap(): return lax.ppermute(value, 'seq', swap_pairs)  9.11 us
    ppermute x5, starting transfers between devices, to_along(): return lax.ppermute(value, 'seq', pairs)  7.82 us
    ppermute x3, starting transfers between devices, outward(): return lax.ppermute(value, 'seq', outer_pairs)  3.86 us
  transfers between devices with their start and end apart: 29, of which 7 were waited for; matrix products, arithmetic and copies ran while one was open for 0% of the time, Pallas kernels for 32%

profile of v5, /device:TPU:1, one launch (start us, length us, event | category | flops | bytes accessed | tf_op | source)
XLA Modules:
  0.0 112.6 jit_solution(7882956672579779457)
XLA Ops:
  0.7 1.6 %copy-done.1 = bf16[1,2048,512]{2,1,0:T(8,128)(2,1)S(1)} copy-done((bf16[1,2048,512]{2,1,0:T(8,128)(2,1)S(1)}, bf16[1,2048,512]{2,1,0:T(8,128)(2,1)}, u32[]{:S(2)}) %copy-start.1) | copy-done | bytes 2097176
  2.9 2.1 %collective-permute-start.4 = (bf16[1024,256]{1,0:T(8,128)(2,1)S(1)}, bf16[1024,256]{1,0:T(8,128)(2,1)S(1)}, u32[]{:S(2)}, u32[]{:S(2)}) collective-permute-start(bf16[1024,256]{1,0:T(8,128)(2,1)S(1)} %get-tuple-element.64), channel_id=1, source_target_pairs={{0,4},{2,6},{4,0},{6,2},{8,12},{10,14},{12,8},{14,10},{16,20},{18,... | collective-permute-start | bytes 1572872 | tf_op jit(solution)/shard_map/ppermute | solution.py:355
  5.1 1.4 %own_act.1 = (bf16[1024,256]{1,0:T(8,128)(2,1)S(1)}, bf16[1024,256]{1,0:T(8,128)(2,1)S(1)}, f32[8,128]{1,0:T(8,128)S(1)}) custom-call(s32[6]{0:T(128)S(1)} %stack.27.meta, bf16[2048,512]{1,0:T(8,128)(2,1)S(1)} %bitcast.11, f32[8,128]{1,0:T(8,128)S(1)} %get-tuple-element.59.refs_1_), custom_call_target="tpu_custom_call" | custom-call | flops 1 | bytes 200000 | tf_op jit(solution)/shard_map/own_act/pallas_call | solution.py:43
  7.3 1.3 %collective-permute-start.6 = (bf16[1024,256]{1,0:T(8,128)(2,1)S(1)}, bf16[1024,256]{1,0:T(8,128)(2,1)S(1)}, u32[]{:S(2)}, u32[]{:S(2)}) collective-permute-start(bf16[1024,256]{1,0:T(8,128)(2,1)S(1)} %get-tuple-element.71.refs_6_.refs_0_.refs_1_), channel_id=1, source_target_pairs={{4,12},{6,14},{8,0},{10,2},{12,20},{14,22},{16,8},{18,10},{20,28},... | collective-permute-start | bytes 1572872 | tf_op jit(solution)/shard_map/ppermute | solution.py:358
  8.6 1.3 %collective-permute-start.7 = (bf16[1024,256]{1,0:T(8,128)(2,1)S(1)}, bf16[1024,256]{1,0:T(8,128)(2,1)S(1)}, u32[]{:S(2)}, u32[]{:S(2)}) collective-permute-start(bf16[1024,256]{1,0:T(8,128)(2,1)S(1)} %get-tuple-element.72.refs_7_.refs_1_.refs_2_), channel_id=1, source_target_pairs={{4,12},{6,14},{8,0},{10,2},{12,20},{14,22},{16,8},{18,10},{20,28},... | collective-permute-start | bytes 1572872 | tf_op jit(solution)/shard_map/ppermute | solution.py:358
  9.9 5.4 %collective-permute-start = (bf16[1024,256]{1,0:T(8,128)(2,1)S(1)}, bf16[1024,256]{1,0:T(8,128)(2,1)S(1)}, u32[]{:S(2)}, u32[]{:S(2)}) collective-permute-start(bf16[1024,256]{1,0:T(8,128)(2,1)S(1)} %get-tuple-element.62), channel_id=1, source_target_pairs={{0,4},{2,6},{4,0},{6,2},{8,12},{10,14},{12,8},{14,10},{16,20},{18,... | collective-permute-start | bytes 1572872 | tf_op jit(solution)/shard_map/ppermute | solution.py:355
  15.3 4.0 %mid_tap.1 = (f32[2,512,256]{2,1,0:T(8,128)S(1)}, f32[8,128]{1,0:T(8,128)S(1)}) custom-call(s32[6]{0:T(128)S(1)} %stack.27.meta, bf16[2048,512]{1,0:T(8,128)(2,1)S(1)} %bitcast.13, bf16[2048,512]{1,0:T(8,128)(2,1)S(1)} %bitcast.17, f32[8,128]{1,0:T(8,128)S(1)} %get-tuple-element.66.refs_2_), custom_call_target="tpu_custom_call" | custom-call | flops 1 | bytes 200000 | tf_op jit(solution)/shard_map/mid_tap/pallas_call | solution.py:43
  20.3 3.2 %collective-permute-start.8 = (bf16[1024,256]{1,0:T(8,128)(2,1)S(1)}, bf16[1024,256]{1,0:T(8,128)(2,1)S(1)}, u32[]{:S(2)}, u32[]{:S(2)}) collective-permute-start(bf16[1024,256]{1,0:T(8,128)(2,1)S(1)} %get-tuple-element.68.refs_2_.refs_3_), channel_id=1, source_target_pairs={{12,4},{14,6},{0,8},{2,10},{20,12},{22,14},{8,16},{10,18},{28,20},... | collective-permute-start | bytes 1572872 | tf_op jit(solution)/shard_map/ppermute | solution.py:361
  23.5 4.5 %collective-permute-done.5.refs_0_.refs_1_ = bf16[1024,256]{1,0:T(8,128)(2,1)S(1)} collective-permute-done((bf16[1024,256]{1,0:T(8,128)(2,1)S(1)}, bf16[1024,256]{1,0:T(8,128)(2,1)S(1)}, u32[]{:S(2)}, u32[]{:S(2)}) %collective-permute-start.5) | collective-permute-done | bytes 524320 | tf_op jit(solution)/shard_map/ppermute | solution.py:355
  29.0 3.1 %collective-permute-start.10 = (bf16[1024,256]{1,0:T(8,128)(2,1)S(1)}, bf16[1024,256]{1,0:T(8,128)(2,1)S(1)}, u32[]{:S(2)}, u32[]{:S(2)}) collective-permute-start(bf16[1024,256]{1,0:T(8,128)(2,1)S(1)} %get-tuple-element.70.refs_3_.refs_4_), channel_id=1, source_target_pairs={{12,4},{14,6},{0,8},{2,10},{20,12},{22,14},{8,16},{10,18},{28,20},... | collective-permute-start | bytes 1572872 | tf_op jit(solution)/shard_map/ppermute | solution.py:361
  34.2 5.0 %collective-permute-done.refs_9_.refs_3_.refs_2_ = bf16[1024,256]{1,0:T(8,128)(2,1)S(1)} collective-permute-done((bf16[1024,256]{1,0:T(8,128)(2,1)S(1)}, bf16[1024,256]{1,0:T(8,128)(2,1)S(1)}, u32[]{:S(2)}, u32[]{:S(2)}) %collective-permute-start) | collective-permute-done | bytes 524320 | tf_op jit(solution)/shard_map/ppermute | solution.py:355
  39.2 3.1 %collective-permute-start.2 = (bf16[1024,256]{1,0:T(8,128)(2,1)S(1)}, bf16[1024,256]{1,0:T(8,128)(2,1)S(1)}, u32[]{:S(2)}, u32[]{:S(2)}) collective-permute-start(bf16[1024,256]{1,0:T(8,128)(2,1)S(1)} %collective-permute-done.refs_9_.refs_3_.refs_2_), channel_id=1, source_target_pairs={{12,4},{14,6},{0,8},{2,10},{20,12},{22,14},{8,16},{10,18},{28,20},... | collective-permute-start | bytes 1572872 | tf_op jit(solution)/shard_map/ppermute | solution.py:361
  42.3 2.9 %oth_out.1 = (bf16[1024,512]{1,0:T(8,128)(2,1)S(1)}, f32[8,128]{1,0:T(8,128)S(1)}) custom-call(s32[6]{0:T(128)S(1)} %stack.27.meta, bf16[1024,256]{1,0:T(8,128)(2,1)S(1)} %collective-permute-done.4.refs_0_, bf16[1024,256]{1,0:T(8,128)(2,1)S(1)} %collective-permute-done.5.refs_0_.refs_1_, bf16[1024,256]{1,0:T(8,128)(2,1)S(1)} %get-tuple-element.68.refs_2_.refs_3_, ...), custom_call_target="tpu_custom_call" | custom-call | flops 1 | bytes 200000 | tf_op jit(solution)/shard_map/oth_out/pallas_call | solution.py:43
  45.2 3.4 %outer_first.1 = (f32[4,256,256]{2,1,0:T(8,128)S(1)}, bf16[4,256,256]{2,1,0:T(8,128)(2,1)S(1)}, f32[2,512,256]{2,1,0:T(8,128)S(1)}, f32[8,128]{1,0:T(8,128)S(1)}) custom-call(s32[6]{0:T(128)S(1)} %stack.27.meta, bf16[1024,256]{1,0:T(8,128)(2,1)S(1)} %get-tuple-element.71.refs_6_.refs_0_.refs_1_, ...), custom_call_target="tpu_custom_call" | custom-call | flops 1 | bytes 200000 | tf_op jit(solution)/shard_map/outer_first/pallas_call | solution.py:43
  48.7 4.2 %collective-permute-start.11 = (bf16[4,256,256]{2,1,0:T(8,128)(2,1)S(1)}, bf16[4,256,256]{2,1,0:T(8,128)(2,1)S(1)}, u32[]{:S(2)}, u32[]{:S(2)}) collective-permute-start(bf16[4,256,256]{2,1,0:T(8,128)(2,1)S(1)} %get-tuple-element.78), channel_id=1, source_target_pairs={{0,2},{2,0},{4,6},{6,4},{8,10},{10,8},{12,14},{14,12},{16,18},{18,... | collective-permute-start | bytes 1572872 | tf_op jit(solution)/shard_map/ppermute | solution.py:364
  53.1 2.1 %outer_second.1 = (f32[2,256,256]{2,1,0:T(8,128)S(1)}, f32[2,256,256]{2,1,0:T(8,128)S(1)}, f32[8,128]{1,0:T(8,128)S(1)}) custom-call(s32[6]{0:T(128)S(1)} %stack.27.meta, bf16[1024,256]{1,0:T(8,128)(2,1)S(1)} %get-tuple-element.71.refs_6_.refs_0_.refs_1_, bf16[1024,256]{1,0:T(8,128)(2,1)S(1)} %get-tuple-element.72.refs_7_.refs_1_.refs_2_, ...), custom_call_target="tpu_custom_call" | custom-call | flops 1 | bytes 200000 | tf_op jit(solution)/shard_map/outer_second/pallas_call | solution.py:43
  57.7 3.7 %collective-permute-start.3 = (bf16[1024,256]{1,0:T(8,128)(2,1)S(1)}, bf16[1024,256]{1,0:T(8,128)(2,1)S(1)}, u32[]{:S(2)}, u32[]{:S(2)}) collective-permute-start(bf16[1024,256]{1,0:T(8,128)(2,1)S(1)} %collective-permute-done.1.refs_4_.refs_3_), channel_id=1, source_target_pairs={{12,4},{14,6},{0,8},{2,10},{20,12},{22,14},{8,16},{10,18},{28,20},... | collective-permute-start | bytes 1572872 | tf_op jit(solution)/shard_map/ppermute | solution.py:361
  62.4 3.8 %oth_grad.1 = (bf16[1024,512]{1,0:T(8,128)(2,1)S(1)}, f32[8,128]{1,0:T(8,128)S(1)}) custom-call(s32[6]{0:T(128)S(1)} %stack.27.meta, bf16[1024,256]{1,0:T(8,128)(2,1)S(1)} %collective-permute-done.4.refs_0_, bf16[1024,256]{1,0:T(8,128)(2,1)S(1)} %collective-permute-done.5.refs_0_.refs_1_, bf16[1024,512]{1,0:T(8,128)(2,1)S(1)} %get-tuple-element.61.refs_8_.refs_2_.refs_1_, ...), custom_call_target="tpu_custom_call" | custom-call | flops 1 | bytes 200000 | tf_op jit(solution)/shard_map/oth_grad/pallas_call | solution.py:43
  67.0 2.0 %collective-permute-start.16 = (bf16[6,64,256]{2,1,0:T(8,128)(2,1)S(1)}, bf16[6,64,256]{2,1,0:T(8,128)(2,1)S(1)}, u32[]{:S(2)}, u32[]{:S(2)}) collective-permute-start(bf16[6,64,256]{2,1,0:T(8,128)(2,1)S(1)} %get-tuple-element.94), channel_id=1, source_target_pairs={{0,8},{2,10},{4,12},{6,14},{8,0},{10,2},{12,4},{14,6},{16,24},{18,... | collective-permute-start | bytes 589832 | tf_op jit(solution)/shard_map/ppermute | solution.py:384
  69.0 1.3 %collective-permute-start.23 = (bf16[1024,512]{1,0:T(8,128)(2,1)S(1)}, bf16[1024,512]{1,0:T(8,128)(2,1)S(1)}, u32[]{:S(2)}, u32[]{:S(2)}) collective-permute-start(bf16[1024,512]{1,0:T(8,128)(2,1)S(1)} %get-tuple-element.106), channel_id=1, source_target_pairs={{0,4},{2,6},{4,0},{6,2},{8,12},{10,14},{12,8},{14,10},{16,20},{18,... | collective-permute-start | bytes 3145736 | tf_op jit(solution)/shard_map/ppermute | solution.py:355
  70.3 3.7 %own_out.1 = (bf16[2048,512]{1,0:T(8,128)(2,1)}, f32[8,128]{1,0:T(8,128)S(1)}) custom-call(s32[6]{0:T(128)S(1)} %stack.27.meta, bf16[2048,512]{1,0:T(8,128)(2,1)S(1)} %bitcast.14, bf16[1024,256]{1,0:T(8,128)(2,1)S(1)} %get-tuple-element.71.refs_6_.refs_0_.refs_1_, bf16[1024,256]{1,0:T(8,128)(2,1)S(1)} %get-tuple-element.72.refs_7_.refs_1_.refs_2_, ...), custom_call_target="tpu_custom_call" | custom-call | flops 1 | bytes 200000 | tf_op jit(solution)/shard_map/own_out/pallas_call | solution.py:43
  75.8 1.8 %collective-permute-done.9.refs_9_ = bf16[1024,512]{1,0:T(8,128)(2,1)S(1)} collective-permute-done((bf16[1024,512]{1,0:T(8,128)(2,1)S(1)}, bf16[1024,512]{1,0:T(8,128)(2,1)S(1)}, u32[]{:S(2)}, u32[]{:S(2)}) %collective-permute-start.9) | collective-permute-done | bytes 1048608 | tf_op jit(solution)/shard_map/ppermute | solution.py:355
  77.6 4.6 %own_grad.1 = (bf16[2048,512]{1,0:T(8,128)(2,1)}, bf16[2048,512]{1,0:T(8,128)(2,1)}, f32[8,128]{1,0:T(8,128)S(1)}) custom-call(s32[6]{0:T(128)S(1)} %stack.27.meta, bf16[2048,512]{1,0:T(8,128)(2,1)S(1)} %bitcast.15, bf16[1024,512]{1,0:T(8,128)(2,1)S(1)} %get-tuple-element.61.refs_8_.refs_2_.refs_1_, ...), custom_call_target="tpu_custom_call", output_to_operand_aliasing={{1}: (11, {})} | custom-call | flops 1 | bytes 200000 | tf_op jit(solution)/shard_map/own_grad/pallas_call | solution.py:43
  82.8 2.2 %collective-permute-start.18 = (f32[6,32,256]{2,1,0:T(8,128)S(1)}, f32[6,32,256]{2,1,0:T(8,128)S(1)}, u32[]{:S(2)}, u32[]{:S(2)}) collective-permute-start(f32[6,32,256]{2,1,0:T(8,128)S(1)} %get-tuple-element.101.refs_0_), channel_id=1, source_target_pairs={{0,12},{2,14},{4,8},{6,10},{8,4},{10,6},{12,0},{14,2},{16,28},{18,... | collective-permute-start | bytes 589832 | tf_op jit(solution)/shard_map/ppermute | solution.py:388
  85.0 3.4 %collective-permute-done.18.refs_1_ = f32[6,32,256]{2,1,0:T(8,128)S(1)} collective-permute-done((f32[6,32,256]{2,1,0:T(8,128)S(1)}, f32[6,32,256]{2,1,0:T(8,128)S(1)}, u32[]{:S(2)}, u32[]{:S(2)}) %collective-permute-start.18) | collective-permute-done | bytes 196640 | tf_op jit(solution)/shard_map/ppermute | solution.py:388
  91.3 2.3 %collective-permute-start.21 = (bf16[6,32,256]{2,1,0:T(8,128)(2,1)S(1)}, bf16[6,32,256]{2,1,0:T(8,128)(2,1)S(1)}, u32[]{:S(2)}, u32[]{:S(2)}) collective-permute-start(bf16[6,32,256]{2,1,0:T(8,128)(2,1)S(1)} %get-tuple-element.103.refs_0_), channel_id=1, source_target_pairs={{0,24},{2,26},{4,28},{6,30},{8,16},{10,18},{12,20},{14,22},{16,0},... | collective-permute-start | bytes 294920 | tf_op jit(solution)/shard_map/ppermute | solution.py:384
  93.6 1.7 %collective-permute-start.24 = (bf16[6,32,256]{2,1,0:T(8,128)(2,1)S(1)}, bf16[6,32,256]{2,1,0:T(8,128)(2,1)S(1)}, u32[]{:S(2)}, u32[]{:S(2)}) collective-permute-start(bf16[6,32,256]{2,1,0:T(8,128)(2,1)S(1)} %get-tuple-element.103.refs_0_), channel_id=1, source_target_pairs={{0,1},{1,0},{2,3},{3,2},{4,5},{5,4},{6,7},{7,6},{8,9},{9,8},{10,11... | collective-permute-start | bytes 294920 | tf_op jit(solution)/shard_map/ppermute | solution.py:367
  97.5 4.5 %collective-permute-start.27 = (bf16[6,32,256]{2,1,0:T(8,128)(2,1)S(1)}, bf16[6,32,256]{2,1,0:T(8,128)(2,1)S(1)}, u32[]{:S(2)}, u32[]{:S(2)}) collective-permute-start(bf16[6,32,256]{2,1,0:T(8,128)(2,1)S(1)} %collective-permute-done.21.refs_3_), channel_id=1, source_target_pairs={{0,1},{1,0},{2,3},{3,2},{4,5},{5,4},{6,7},{7,6},{8,9},{9,8},{10,11... | collective-permute-start | bytes 294920 | tf_op jit(solution)/shard_map/ppermute | solution.py:367
  102.5 2.5 %collective-permute-start.22 = (bf16[6,128,256]{2,1,0:T(8,128)(2,1)S(1)}, bf16[6,128,256]{2,1,0:T(8,128)(2,1)S(1)}, u32[]{:S(2)}, u32[]{:S(2)}) collective-permute-start(bf16[6,128,256]{2,1,0:T(8,128)(2,1)S(1)} %get-tuple-element.105.refs_0_), channel_id=1, source_target_pairs={{0,2},{2,0},{4,6},{6,4},{8,10},{10,8},{12,14},{14,12},{16,18},{18,... | collective-permute-start | bytes 1179656 | tf_op jit(solution)/shard_map/ppermute | solution.py:364
  105.8 2.8 %collective-permute-start.28 = (bf16[6,128,256]{2,1,0:T(8,128)(2,1)S(1)}, bf16[6,128,256]{2,1,0:T(8,128)(2,1)S(1)}, u32[]{:S(2)}, u32[]{:S(2)}) collective-permute-start(bf16[6,128,256]{2,1,0:T(8,128)(2,1)S(1)} %get-tuple-element.111.refs_0_), channel_id=1, source_target_pairs={{0,2},{2,0},{4,6},{6,4},{8,10},{10,8},{12,14},{14,12},{16,18},{18,... | collective-permute-start | bytes 1179656 | tf_op jit(solution)/shard_map/ppermute | solution.py:364
  108.6 2.1 %write_taps0.1 = (f32[3,512,512]{2,1,0:T(8,128)}, bf16[2048,512]{1,0:T(8,128)(2,1)}, f32[8,128]{1,0:T(8,128)S(1)}) custom-call(s32[6]{0:T(128)S(1)} %stack.27.meta, bf16[6,128,256]{2,1,0:T(8,128)(2,1)S(1)} %get-tuple-element.105.refs_0_, bf16[6,128,256]{2,1,0:T(8,128)(2,1)S(1)} %collective-permute-done.22.refs_1_, ...), custom_call_target="tpu_custom_call", output_to_operand_aliasing={{1}: (4, {})} | custom-call | flops 1 | bytes 200000 | tf_op jit(solution)/shard_map/write_taps0/pallas_call | solution.py:43
  110.8 1.8 %write_taps1.1 = (f32[3,512,512]{2,1,0:T(8,128)}, f32[8,128]{1,0:T(8,128)}) custom-call(s32[6]{0:T(128)S(1)} %stack.27.meta, bf16[6,128,256]{2,1,0:T(8,128)(2,1)S(1)} %get-tuple-element.111.refs_0_, bf16[6,128,256]{2,1,0:T(8,128)(2,1)S(1)} %collective-permute-done.28.refs_1_, ...), custom_call_target="tpu_custom_call", output_to_operand_aliasing={{0}: (3, {})} | custom-call | flops 1 | bytes 200000 | tf_op jit(solution)/shard_map/write_taps1/pallas_call | solution.py:43
  (57 shorter events, 18.8 us)
Async XLA Ops:
  2.3 4.1 %copy-start.3 = (bf16[1,2048,512]{2,1,0:T(8,128)(2,1)S(1)}, bf16[1,2048,512]{2,1,0:T(8,128)(2,1)}, u32[]{:S(2)}) copy-start(bf16[1,2048,512]{2,1,0:T(8,128)(2,1)} %param.5) | copy-start | bytes 6291460
  2.9 16.3 %collective-permute-start.4 = (bf16[1024,256]{1,0:T(8,128)(2,1)S(1)}, bf16[1024,256]{1,0:T(8,128)(2,1)S(1)}, u32[]{:S(2)}, u32[]{:S(2)}) collective-permute-start(bf16[1024,256]{1,0:T(8,128)(2,1)S(1)} %get-tuple-element.64), channel_id=1, source_target_pairs={{0,4},{2,6},{4,0},{6,2},{8,12},{10,14},{12,8},{14,10},{16,20},{18,... | collective-permute-start | bytes 1572872 | tf_op jit(solution)/shard_map/ppermute | solution.py:355
  7.2 20.7 %collective-permute-start.5 = (bf16[1024,256]{1,0:T(8,128)(2,1)S(1)}, bf16[1024,256]{1,0:T(8,128)(2,1)S(1)}, u32[]{:S(2)}, u32[]{:S(2)}) collective-permute-start(bf16[1024,256]{1,0:T(8,128)(2,1)S(1)} %get-tuple-element.65), channel_id=1, source_target_pairs={{0,4},{2,6},{4,0},{6,2},{8,12},{10,14},{12,8},{14,10},{16,20},{18,... | collective-permute-start | bytes 1572872 | tf_op jit(solution)/shard_map/ppermute | solution.py:355
  7.3 24.8 %collective-permute-start.6 = (bf16[1024,256]{1,0:T(8,128)(2,1)S(1)}, bf16[1024,256]{1,0:T(8,128)(2,1)S(1)}, u32[]{:S(2)}, u32[]{:S(2)}) collective-permute-start(bf16[1024,256]{1,0:T(8,128)(2,1)S(1)} %get-tuple-element.71.refs_6_.refs_0_.refs_1_), channel_id=1, source_target_pairs={{4,12},{6,14},{8,0},{10,2},{12,20},{14,22},{16,8},{18,10},{20,28},... | collective-permute-start | bytes 1572872 | tf_op jit(solution)/shard_map/ppermute | solution.py:358
  8.6 24.3 %collective-permute-start.7 = (bf16[1024,256]{1,0:T(8,128)(2,1)S(1)}, bf16[1024,256]{1,0:T(8,128)(2,1)S(1)}, u32[]{:S(2)}, u32[]{:S(2)}) collective-permute-start(bf16[1024,256]{1,0:T(8,128)(2,1)S(1)} %get-tuple-element.72.refs_7_.refs_1_.refs_2_), channel_id=1, source_target_pairs={{4,12},{6,14},{8,0},{10,2},{12,20},{14,22},{16,8},{18,10},{20,28},... | collective-permute-start | bytes 1572872 | tf_op jit(solution)/shard_map/ppermute | solution.py:358
  9.9 29.3 %collective-permute-start = (bf16[1024,256]{1,0:T(8,128)(2,1)S(1)}, bf16[1024,256]{1,0:T(8,128)(2,1)S(1)}, u32[]{:S(2)}, u32[]{:S(2)}) collective-permute-start(bf16[1024,256]{1,0:T(8,128)(2,1)S(1)} %get-tuple-element.62), channel_id=1, source_target_pairs={{0,4},{2,6},{4,0},{6,2},{8,12},{10,14},{12,8},{14,10},{16,20},{18,... | collective-permute-start | bytes 1572872 | tf_op jit(solution)/shard_map/ppermute | solution.py:355
  15.3 27.1 %copy-start = (bf16[3,512,512]{2,1,0:T(8,128)(2,1)S(1)}, bf16[3,512,512]{2,1,0:T(8,128)(2,1)}, u32[]{:S(2)}) copy-start(bf16[3,512,512]{2,1,0:T(8,128)(2,1)} %refs_8_.7) | copy-start | bytes 4718596
  20.3 22.1 %collective-permute-start.8 = (bf16[1024,256]{1,0:T(8,128)(2,1)S(1)}, bf16[1024,256]{1,0:T(8,128)(2,1)S(1)}, u32[]{:S(2)}, u32[]{:S(2)}) collective-permute-start(bf16[1024,256]{1,0:T(8,128)(2,1)S(1)} %get-tuple-element.68.refs_2_.refs_3_), channel_id=1, source_target_pairs={{12,4},{14,6},{0,8},{2,10},{20,12},{22,14},{8,16},{10,18},{28,20},... | collective-permute-start | bytes 1572872 | tf_op jit(solution)/shard_map/ppermute | solution.py:361
  29.0 16.3 %collective-permute-start.10 = (bf16[1024,256]{1,0:T(8,128)(2,1)S(1)}, bf16[1024,256]{1,0:T(8,128)(2,1)S(1)}, u32[]{:S(2)}, u32[]{:S(2)}) collective-permute-start(bf16[1024,256]{1,0:T(8,128)(2,1)S(1)} %get-tuple-element.70.refs_3_.refs_4_), channel_id=1, source_target_pairs={{12,4},{14,6},{0,8},{2,10},{20,12},{22,14},{8,16},{10,18},{28,20},... | collective-permute-start | bytes 1572872 | tf_op jit(solution)/shard_map/ppermute | solution.py:361
  32.1 21.0 %collective-permute-start.1 = (bf16[1024,256]{1,0:T(8,128)(2,1)S(1)}, bf16[1024,256]{1,0:T(8,128)(2,1)S(1)}, u32[]{:S(2)}, u32[]{:S(2)}) collective-permute-start(bf16[1024,256]{1,0:T(8,128)(2,1)S(1)} %get-tuple-element.63), channel_id=1, source_target_pairs={{0,4},{2,6},{4,0},{6,2},{8,12},{10,14},{12,8},{14,10},{16,20},{18,... | collective-permute-start | bytes 1572872 | tf_op jit(solution)/shard_map/ppermute | solution.py:355
  33.0 29.5 %collective-permute-start.15 = (bf16[1024,512]{1,0:T(8,128)(2,1)S(1)}, bf16[1024,512]{1,0:T(8,128)(2,1)S(1)}, u32[]{:S(2)}, u32[]{:S(2)}) collective-permute-start(bf16[1024,512]{1,0:T(8,128)(2,1)S(1)} %get-tuple-element.61.refs_8_.refs_2_.refs_1_), channel_id=1, source_target_pairs={{4,12},{6,14},{8,0},{10,2},{12,20},{14,22},{16,8},{18,10},{20,28},... | collective-permute-start | bytes 3145736 | tf_op jit(solution)/shard_map/ppermute | solution.py:358
  39.2 16.4 %collective-permute-start.2 = (bf16[1024,256]{1,0:T(8,128)(2,1)S(1)}, bf16[1024,256]{1,0:T(8,128)(2,1)S(1)}, u32[]{:S(2)}, u32[]{:S(2)}) collective-permute-start(bf16[1024,256]{1,0:T(8,128)(2,1)S(1)} %collective-permute-done.refs_9_.refs_3_.refs_2_), channel_id=1, source_target_pairs={{12,4},{14,6},{0,8},{2,10},{20,12},{22,14},{8,16},{10,18},{28,20},... | collective-permute-start | bytes 1572872 | tf_op jit(solution)/shard_map/ppermute | solution.py:361
  48.7 7.0 %collective-permute-start.11 = (bf16[4,256,256]{2,1,0:T(8,128)(2,1)S(1)}, bf16[4,256,256]{2,1,0:T(8,128)(2,1)S(1)}, u32[]{:S(2)}, u32[]{:S(2)}) collective-permute-start(bf16[4,256,256]{2,1,0:T(8,128)(2,1)S(1)} %get-tuple-element.78), channel_id=1, source_target_pairs={{0,2},{2,0},{4,6},{6,4},{8,10},{10,8},{12,14},{14,12},{16,18},{18,... | collective-permute-start | bytes 1572872 | tf_op jit(solution)/shard_map/ppermute | solution.py:364
  52.9 24.7 %collective-permute-start.9 = (bf16[1024,512]{1,0:T(8,128)(2,1)S(1)}, bf16[1024,512]{1,0:T(8,128)(2,1)S(1)}, u32[]{:S(2)}, u32[]{:S(2)}) collective-permute-start(bf16[1024,512]{1,0:T(8,128)(2,1)S(1)} %get-tuple-element.74), channel_id=1, source_target_pairs={{0,4},{2,6},{4,0},{6,2},{8,12},{10,14},{12,8},{14,10},{16,20},{18,... | collective-permute-start | bytes 3145736 | tf_op jit(solution)/shard_map/ppermute | solution.py:355
  55.2 6.2 %collective-permute-start.13 = (f32[2,256,256]{2,1,0:T(8,128)S(1)}, f32[2,256,256]{2,1,0:T(8,128)S(1)}, u32[]{:S(2)}, u32[]{:S(2)}) collective-permute-start(f32[2,256,256]{2,1,0:T(8,128)S(1)} %get-tuple-element.85), channel_id=1, source_target_pairs={{0,2},{2,0},{4,6},{6,4},{8,10},{10,8},{12,14},{14,12},{16,18},{18,... | collective-permute-start | bytes 1572872 | tf_op jit(solution)/shard_map/ppermute | solution.py:364
  56.4 9.9 %collective-permute-start.12 = (bf16[4,128,256]{2,1,0:T(8,128)(2,1)S(1)}, bf16[4,128,256]{2,1,0:T(8,128)(2,1)S(1)}, u32[]{:S(2)}, u32[]{:S(2)}) collective-permute-start(bf16[4,128,256]{2,1,0:T(8,128)(2,1)S(1)} %get-tuple-element.83), channel_id=1, source_target_pairs={{0,1},{1,0},{2,3},{3,2},{4,5},{5,4},{6,7},{7,6},{8,9},{9,8},{10,11... | collective-permute-start | bytes 786440 | tf_op jit(solution)/shard_map/ppermute | solution.py:367
  57.7 18.1 %collective-permute-start.3 = (bf16[1024,256]{1,0:T(8,128)(2,1)S(1)}, bf16[1024,256]{1,0:T(8,128)(2,1)S(1)}, u32[]{:S(2)}, u32[]{:S(2)}) collective-permute-start(bf16[1024,256]{1,0:T(8,128)(2,1)S(1)} %collective-permute-done.1.refs_4_.refs_3_), channel_id=1, source_target_pairs={{12,4},{14,6},{0,8},{2,10},{20,12},{22,14},{8,16},{10,18},{28,20},... | collective-permute-start | bytes 1572872 | tf_op jit(solution)/shard_map/ppermute | solution.py:361
  62.1 4.2 %collective-permute-start.14 = (bf16[2,128,256]{2,1,0:T(8,128)(2,1)S(1)}, bf16[2,128,256]{2,1,0:T(8,128)(2,1)S(1)}, u32[]{:S(2)}, u32[]{:S(2)}) collective-permute-start(bf16[2,128,256]{2,1,0:T(8,128)(2,1)S(1)} %get-tuple-element.88), channel_id=1, source_target_pairs={{0,1},{1,0},{2,3},{3,2},{4,5},{5,4},{6,7},{7,6},{8,9},{9,8},{10,11... | collective-permute-start | bytes 393224 | tf_op jit(solution)/shard_map/ppermute | solution.py:367
  62.4 7.9 %copy-start.2 = (bf16[1,2048,512]{2,1,0:T(8,128)(2,1)S(1)}, bf16[1,2048,512]{2,1,0:T(8,128)(2,1)}, u32[]{:S(2)}) copy-start(bf16[1,2048,512]{2,1,0:T(8,128)(2,1)} %param.3) | copy-start | bytes 6291460
  67.0 7.0 %collective-permute-start.16 = (bf16[6,64,256]{2,1,0:T(8,128)(2,1)S(1)}, bf16[6,64,256]{2,1,0:T(8,128)(2,1)S(1)}, u32[]{:S(2)}, u32[]{:S(2)}) collective-permute-start(bf16[6,64,256]{2,1,0:T(8,128)(2,1)S(1)} %get-tuple-element.94), channel_id=1, source_target_pairs={{0,8},{2,10},{4,12},{6,14},{8,0},{10,2},{12,4},{14,6},{16,24},{18,... | collective-permute-start | bytes 589832 | tf_op jit(solution)/shard_map/ppermute | solution.py:384
  69.0 39.6 %collective-permute-start.23 = (bf16[1024,512]{1,0:T(8,128)(2,1)S(1)}, bf16[1024,512]{1,0:T(8,128)(2,1)S(1)}, u32[]{:S(2)}, u32[]{:S(2)}) collective-permute-start(bf16[1024,512]{1,0:T(8,128)(2,1)S(1)} %get-tuple-element.106), channel_id=1, source_target_pairs={{0,4},{2,6},{4,0},{6,2},{8,12},{10,14},{12,8},{14,10},{16,20},{18,... | collective-permute-start | bytes 3145736 | tf_op jit(solution)/shard_map/ppermute | solution.py:355
  74.6 7.7 %collective-permute-start.17 = (bf16[6,32,256]{2,1,0:T(8,128)(2,1)S(1)}, bf16[6,32,256]{2,1,0:T(8,128)(2,1)S(1)}, u32[]{:S(2)}, u32[]{:S(2)}) collective-permute-start(bf16[6,32,256]{2,1,0:T(8,128)(2,1)S(1)} %get-tuple-element.99), channel_id=1, source_target_pairs={{0,16},{2,18},{4,20},{6,22},{8,24},{10,26},{12,28},{14,30},{16,0},... | collective-permute-start | bytes 294920 | tf_op jit(solution)/shard_map/ppermute | solution.py:384
  82.8 5.6 %collective-permute-start.18 = (f32[6,32,256]{2,1,0:T(8,128)S(1)}, f32[6,32,256]{2,1,0:T(8,128)S(1)}, u32[]{:S(2)}, u32[]{:S(2)}) collective-permute-start(f32[6,32,256]{2,1,0:T(8,128)S(1)} %get-tuple-element.101.refs_0_), channel_id=1, source_target_pairs={{0,12},{2,14},{4,8},{6,10},{8,4},{10,6},{12,0},{14,2},{16,28},{18,... | collective-permute-start | bytes 589832 | tf_op jit(solution)/shard_map/ppermute | solution.py:388
  89.0 6.3 %collective-permute-start.19 = (bf16[6,32,256]{2,1,0:T(8,128)(2,1)S(1)}, bf16[6,32,256]{2,1,0:T(8,128)(2,1)S(1)}, u32[]{:S(2)}, u32[]{:S(2)}) collective-permute-start(bf16[6,32,256]{2,1,0:T(8,128)(2,1)S(1)} %get-tuple-element.103.refs_0_), channel_id=1, source_target_pairs={{0,16},{2,18},{4,20},{6,22},{8,24},{10,26},{12,28},{14,30},{16,8},... | collective-permute-start | bytes 294920 | tf_op jit(solution)/shard_map/ppermute | solution.py:384
  90.3 5.9 %collective-permute-start.20 = (bf16[6,32,256]{2,1,0:T(8,128)(2,1)S(1)}, bf16[6,32,256]{2,1,0:T(8,128)(2,1)S(1)}, u32[]{:S(2)}, u32[]{:S(2)}) collective-permute-start(bf16[6,32,256]{2,1,0:T(8,128)(2,1)S(1)} %get-tuple-element.103.refs_0_), channel_id=1, source_target_pairs={{0,8},{2,10},{4,12},{6,14},{8,0},{10,2},{12,4},{14,6},{16,24},{18,... | collective-permute-start | bytes 294920 | tf_op jit(solution)/shard_map/ppermute | solution.py:384
  91.3 6.1 %collective-permute-start.21 = (bf16[6,32,256]{2,1,0:T(8,128)(2,1)S(1)}, bf16[6,32,256]{2,1,0:T(8,128)(2,1)S(1)}, u32[]{:S(2)}, u32[]{:S(2)}) collective-permute-start(bf16[6,32,256]{2,1,0:T(8,128)(2,1)S(1)} %get-tuple-element.103.refs_0_), channel_id=1, source_target_pairs={{0,24},{2,26},{4,28},{6,30},{8,16},{10,18},{12,20},{14,22},{16,0},... | collective-permute-start | bytes 294920 | tf_op jit(solution)/shard_map/ppermute | solution.py:384
  93.6 8.9 %collective-permute-start.24 = (bf16[6,32,256]{2,1,0:T(8,128)(2,1)S(1)}, bf16[6,32,256]{2,1,0:T(8,128)(2,1)S(1)}, u32[]{:S(2)}, u32[]{:S(2)}) collective-permute-start(bf16[6,32,256]{2,1,0:T(8,128)(2,1)S(1)} %get-tuple-element.103.refs_0_), channel_id=1, source_target_pairs={{0,1},{1,0},{2,3},{3,2},{4,5},{5,4},{6,7},{7,6},{8,9},{9,8},{10,11... | collective-permute-start | bytes 294920 | tf_op jit(solution)/shard_map/ppermute | solution.py:367
  95.4 9.7 %collective-permute-start.25 = (bf16[6,32,256]{2,1,0:T(8,128)(2,1)S(1)}, bf16[6,32,256]{2,1,0:T(8,128)(2,1)S(1)}, u32[]{:S(2)}, u32[]{:S(2)}) collective-permute-start(bf16[6,32,256]{2,1,0:T(8,128)(2,1)S(1)} %collective-permute-done.19.refs_1_), channel_id=1, source_target_pairs={{0,1},{1,0},{2,3},{3,2},{4,5},{5,4},{6,7},{7,6},{8,9},{9,8},{10,11... | collective-permute-start | bytes 294920 | tf_op jit(solution)/shard_map/ppermute | solution.py:367
  96.2 8.9 %collective-permute-start.26 = (bf16[6,32,256]{2,1,0:T(8,128)(2,1)S(1)}, bf16[6,32,256]{2,1,0:T(8,128)(2,1)S(1)}, u32[]{:S(2)}, u32[]{:S(2)}) collective-permute-start(bf16[6,32,256]{2,1,0:T(8,128)(2,1)S(1)} %collective-permute-done.20.refs_2_), channel_id=1, source_target_pairs={{0,1},{1,0},{2,3},{3,2},{4,5},{5,4},{6,7},{7,6},{8,9},{9,8},{10,11... | collective-permute-start | bytes 294920 | tf_op jit(solution)/shard_map/ppermute | solution.py:367
  97.5 7.7 %collective-permute-start.27 = (bf16[6,32,256]{2,1,0:T(8,128)(2,1)S(1)}, bf16[6,32,256]{2,1,0:T(8,128)(2,1)S(1)}, u32[]{:S(2)}, u32[]{:S(2)}) collective-permute-start(bf16[6,32,256]{2,1,0:T(8,128)(2,1)S(1)} %collective-permute-done.21.refs_3_), channel_id=1, source_target_pairs={{0,1},{1,0},{2,3},{3,2},{4,5},{5,4},{6,7},{7,6},{8,9},{9,8},{10,11... | collective-permute-start | bytes 294920 | tf_op jit(solution)/shard_map/ppermute | solution.py:367
  102.5 6.1 %collective-permute-start.22 = (bf16[6,128,256]{2,1,0:T(8,128)(2,1)S(1)}, bf16[6,128,256]{2,1,0:T(8,128)(2,1)S(1)}, u32[]{:S(2)}, u32[]{:S(2)}) collective-permute-start(bf16[6,128,256]{2,1,0:T(8,128)(2,1)S(1)} %get-tuple-element.105.refs_0_), channel_id=1, source_target_pairs={{0,2},{2,0},{4,6},{6,4},{8,10},{10,8},{12,14},{14,12},{16,18},{18,... | collective-permute-start | bytes 1179656 | tf_op jit(solution)/shard_map/ppermute | solution.py:364
  105.8 5.0 %collective-permute-start.28 = (bf16[6,128,256]{2,1,0:T(8,128)(2,1)S(1)}, bf16[6,128,256]{2,1,0:T(8,128)(2,1)S(1)}, u32[]{:S(2)}, u32[]{:S(2)}) collective-permute-start(bf16[6,128,256]{2,1,0:T(8,128)(2,1)S(1)} %get-tuple-element.111.refs_0_), channel_id=1, source_target_pairs={{0,2},{2,0},{4,6},{6,4},{8,10},{10,8},{12,14},{14,12},{16,18},{18,... | collective-permute-start | bytes 1179656 | tf_op jit(solution)/shard_map/ppermute | solution.py:364
  (1 other events, 1.6 us)

commit v6 on v5

--- a/solution.py
+++ b/solution.py
@@ -399,6 +399,8 @@
     device = Device(meta)
 
     part_spec = pl.BlockSpec((block, cols), lambda i, s: (i, 0))
+    part_wide = pl.BlockSpec((2 * block, cols), lambda i, s: (i, 0))
+    rows_wide = pl.BlockSpec((2 * block, chans), lambda i, s: (i, 0))
     weights, weight_specs = (conv_weight,) * 3, [w_near, w_mid, w_far]
 
     staged = halving and (chans // tap // dp_count) % (16 * along_count) == 0
@@ -483,15 +485,15 @@
     out = swap(out)
     slices, specs = slices_of(4, BF16)
     *outer0, rest = call(
-        functools.partial(outer_first_body, steps, tap), device,
+        functools.partial(outer_first_body, steps // 2, tap), device,
         (*a_own, a_oth0, a_oth1, *a_oth_far, a_own_far0, a_own_far1, u_own, u_oth[0], mid),
-        [*[part_spec] * 8, rows_spec, part_spec, WHOLE], [*slices, shape_of(sums_shape, F32)], [*specs, sums_spec],
-        grid=(steps,), scratch=[pltpu.VMEM(sums_shape, F32)], name="outer_first",
+        [*[part_wide] * 8, rows_wide, part_wide, WHOLE], [*slices, shape_of(sums_shape, F32)], [*specs, sums_spec],
+        grid=(steps // 2,), scratch=[pltpu.VMEM(sums_shape, F32)], name="outer_first",
     )
     slices, specs = slices_of(2, F32)
     outer1 = call(
-        functools.partial(outer_second_body, steps, tap), device, (*a_own, *a_oth_far, u_oth[1], rest),
-        [*[part_spec] * 5, WHOLE], slices, specs, grid=(steps,), scratch=[pltpu.VMEM(sums_shape, F32)],
+        functools.partial(outer_second_body, steps // 2, tap), device, (*a_own, *a_oth_far, u_oth[1], rest),
+        [*[part_wide] * 5, WHOLE], slices, specs, grid=(steps // 2,), scratch=[pltpu.VMEM(sums_shape, F32)],
         name="outer_second",
     )
     outer0 = core_stage(outer0, "outer0", after=(u_own_far[0],))

time: 113 us -> 113 us (level)
  waiting for transfers between devices: 16.4 us -> 18.1 us
    ppermute x4, starting transfers between devices: 9.96 us -> 13.1 us  [to_core(): lax.ppermute(value, 'seq', [(i, i - i % tap + (i % tap + shift) % tap) fo...]
    ppermute x6, starting transfers between devices: 9.25 us -> 6.86 us  [to_dp(): lax.ppermute(value, 'dp', [(i, (i + shift) % dp_count) for i in range(dp_...]
    ppermute x5, waiting for transfers between devices: 0.67 us -> 1.92 us  [to_along(): return lax.ppermute(value, 'seq', pairs)]
  transfers between devices with their start and end apart: 29 -> 29, of which waited for: 7 -> 9; matrix products, arithmetic and copies ran while one was open for 0% -> 0% of each run, Pallas kernels for 32% -> 31%
where the time goes in v6:
time: 113 us
  starting transfers between devices  55.1 us (49%)
  Pallas kernels  37.3 us (33%)
  waiting for transfers between devices  18.1 us (16%)
  local copies, waits for them, and re-layouts  1.69 us (1%)
    pallas_call x22, Pallas kernels, call(): pl.pallas_call(chained, grid_spec=pltpu.PrefetchScalarGridSpec(num_scalar...  37.3 us
    ppermute x4, starting transfers between devices, inward(): return lax.ppermute(value, 'seq', inner_pairs)  13.6 us
    ppermute x4, starting transfers between devices, to_core(): lax.ppermute(value, 'seq', [(i, i - i % tap + (i % tap + shift) % tap) fo...  13.1 us
    ppermute x6, waiting for transfers between devices, swap(): return lax.ppermute(value, 'seq', swap_pairs)  11.4 us
    ppermute x6, starting transfers between devices, swap(): return lax.ppermute(value, 'seq', swap_pairs)  8.17 us
    ppermute x5, starting transfers between devices, to_along(): return lax.ppermute(value, 'seq', pairs)  7.41 us
    ppermute x6, starting transfers between devices, to_dp(): lax.ppermute(value, 'dp', [(i, (i + shift) % dp_count) for i in range(dp_...  6.86 us
    ppermute x3, starting transfers between devices, outward(): return lax.ppermute(value, 'seq', outer_pairs)  3.86 us
  transfers between devices with their start and end apart: 29, of which 9 were waited for; matrix products, arithmetic and copies ran while one was open for 0% of the time, Pallas kernels for 31%

profile of v6, /device:TPU:1, one launch (start us, length us, event | category | flops | bytes accessed | tf_op | source)
XLA Modules:
  0.0 113.1 jit_solution(17648798511182436731)
XLA Ops:
  0.7 1.6 %copy-done.1 = bf16[1,2048,512]{2,1,0:T(8,128)(2,1)S(1)} copy-done((bf16[1,2048,512]{2,1,0:T(8,128)(2,1)S(1)}, bf16[1,2048,512]{2,1,0:T(8,128)(2,1)}, u32[]{:S(2)}) %copy-start.1) | copy-done | bytes 2097176
  2.9 2.1 %collective-permute-start.4 = (bf16[1024,256]{1,0:T(8,128)(2,1)S(1)}, bf16[1024,256]{1,0:T(8,128)(2,1)S(1)}, u32[]{:S(2)}, u32[]{:S(2)}) collective-permute-start(bf16[1024,256]{1,0:T(8,128)(2,1)S(1)} %get-tuple-element.64), channel_id=1, source_target_pairs={{0,4},{2,6},{4,0},{6,2},{8,12},{10,14},{12,8},{14,10},{16,20},{18,... | collective-permute-start | bytes 1572872 | tf_op jit(solution)/shard_map/ppermute | solution.py:355
  5.1 1.4 %own_act.1 = (bf16[1024,256]{1,0:T(8,128)(2,1)S(1)}, bf16[1024,256]{1,0:T(8,128)(2,1)S(1)}, f32[8,128]{1,0:T(8,128)S(1)}) custom-call(s32[6]{0:T(128)S(1)} %stack.27.meta, bf16[2048,512]{1,0:T(8,128)(2,1)S(1)} %bitcast.11, f32[8,128]{1,0:T(8,128)S(1)} %get-tuple-element.59.refs_1_), custom_call_target="tpu_custom_call" | custom-call | flops 1 | bytes 200000 | tf_op jit(solution)/shard_map/own_act/pallas_call | solution.py:43
  7.3 1.3 %collective-permute-start.6 = (bf16[1024,256]{1,0:T(8,128)(2,1)S(1)}, bf16[1024,256]{1,0:T(8,128)(2,1)S(1)}, u32[]{:S(2)}, u32[]{:S(2)}) collective-permute-start(bf16[1024,256]{1,0:T(8,128)(2,1)S(1)} %get-tuple-element.71.refs_6_.refs_0_.refs_1_), channel_id=1, source_target_pairs={{4,12},{6,14},{8,0},{10,2},{12,20},{14,22},{16,8},{18,10},{20,28},... | collective-permute-start | bytes 1572872 | tf_op jit(solution)/shard_map/ppermute | solution.py:358
  8.6 1.3 %collective-permute-start.7 = (bf16[1024,256]{1,0:T(8,128)(2,1)S(1)}, bf16[1024,256]{1,0:T(8,128)(2,1)S(1)}, u32[]{:S(2)}, u32[]{:S(2)}) collective-permute-start(bf16[1024,256]{1,0:T(8,128)(2,1)S(1)} %get-tuple-element.72.refs_7_.refs_1_.refs_2_), channel_id=1, source_target_pairs={{4,12},{6,14},{8,0},{10,2},{12,20},{14,22},{16,8},{18,10},{20,28},... | collective-permute-start | bytes 1572872 | tf_op jit(solution)/shard_map/ppermute | solution.py:358
  9.9 5.4 %collective-permute-start = (bf16[1024,256]{1,0:T(8,128)(2,1)S(1)}, bf16[1024,256]{1,0:T(8,128)(2,1)S(1)}, u32[]{:S(2)}, u32[]{:S(2)}) collective-permute-start(bf16[1024,256]{1,0:T(8,128)(2,1)S(1)} %get-tuple-element.62), channel_id=1, source_target_pairs={{0,4},{2,6},{4,0},{6,2},{8,12},{10,14},{12,8},{14,10},{16,20},{18,... | collective-permute-start | bytes 1572872 | tf_op jit(solution)/shard_map/ppermute | solution.py:355
  15.3 4.0 %mid_tap.1 = (f32[2,512,256]{2,1,0:T(8,128)S(1)}, f32[8,128]{1,0:T(8,128)S(1)}) custom-call(s32[6]{0:T(128)S(1)} %stack.27.meta, bf16[2048,512]{1,0:T(8,128)(2,1)S(1)} %bitcast.13, bf16[2048,512]{1,0:T(8,128)(2,1)S(1)} %bitcast.17, f32[8,128]{1,0:T(8,128)S(1)} %get-tuple-element.66.refs_2_), custom_call_target="tpu_custom_call" | custom-call | flops 1 | bytes 200000 | tf_op jit(solution)/shard_map/mid_tap/pallas_call | solution.py:43
  20.3 3.2 %collective-permute-start.8 = (bf16[1024,256]{1,0:T(8,128)(2,1)S(1)}, bf16[1024,256]{1,0:T(8,128)(2,1)S(1)}, u32[]{:S(2)}, u32[]{:S(2)}) collective-permute-start(bf16[1024,256]{1,0:T(8,128)(2,1)S(1)} %get-tuple-element.68.refs_2_.refs_3_), channel_id=1, source_target_pairs={{12,4},{14,6},{0,8},{2,10},{20,12},{22,14},{8,16},{10,18},{28,20},... | collective-permute-start | bytes 1572872 | tf_op jit(solution)/shard_map/ppermute | solution.py:361
  23.5 4.5 %collective-permute-done.5.refs_0_.refs_1_ = bf16[1024,256]{1,0:T(8,128)(2,1)S(1)} collective-permute-done((bf16[1024,256]{1,0:T(8,128)(2,1)S(1)}, bf16[1024,256]{1,0:T(8,128)(2,1)S(1)}, u32[]{:S(2)}, u32[]{:S(2)}) %collective-permute-start.5) | collective-permute-done | bytes 524320 | tf_op jit(solution)/shard_map/ppermute | solution.py:355
  29.0 3.1 %collective-permute-start.10 = (bf16[1024,256]{1,0:T(8,128)(2,1)S(1)}, bf16[1024,256]{1,0:T(8,128)(2,1)S(1)}, u32[]{:S(2)}, u32[]{:S(2)}) collective-permute-start(bf16[1024,256]{1,0:T(8,128)(2,1)S(1)} %get-tuple-element.70.refs_3_.refs_4_), channel_id=1, source_target_pairs={{12,4},{14,6},{0,8},{2,10},{20,12},{22,14},{8,16},{10,18},{28,20},... | collective-permute-start | bytes 1572872 | tf_op jit(solution)/shard_map/ppermute | solution.py:361
  33.0 1.3 %collective-permute-start.15 = (bf16[1024,512]{1,0:T(8,128)(2,1)S(1)}, bf16[1024,512]{1,0:T(8,128)(2,1)S(1)}, u32[]{:S(2)}, u32[]{:S(2)}) collective-permute-start(bf16[1024,512]{1,0:T(8,128)(2,1)S(1)} %get-tuple-element.61.refs_8_.refs_2_.refs_1_), channel_id=1, source_target_pairs={{4,12},{6,14},{8,0},{10,2},{12,20},{14,22},{16,8},{18,10},{20,28},... | collective-permute-start | bytes 3145736 | tf_op jit(solution)/shard_map/ppermute | solution.py:358
  34.2 5.0 %collective-permute-done.refs_9_.refs_3_.refs_2_ = bf16[1024,256]{1,0:T(8,128)(2,1)S(1)} collective-permute-done((bf16[1024,256]{1,0:T(8,128)(2,1)S(1)}, bf16[1024,256]{1,0:T(8,128)(2,1)S(1)}, u32[]{:S(2)}, u32[]{:S(2)}) %collective-permute-start) | collective-permute-done | bytes 524320 | tf_op jit(solution)/shard_map/ppermute | solution.py:355
  39.2 3.1 %collective-permute-start.2 = (bf16[1024,256]{1,0:T(8,128)(2,1)S(1)}, bf16[1024,256]{1,0:T(8,128)(2,1)S(1)}, u32[]{:S(2)}, u32[]{:S(2)}) collective-permute-start(bf16[1024,256]{1,0:T(8,128)(2,1)S(1)} %collective-permute-done.refs_9_.refs_3_.refs_2_), channel_id=1, source_target_pairs={{12,4},{14,6},{0,8},{2,10},{20,12},{22,14},{8,16},{10,18},{28,20},... | collective-permute-start | bytes 1572872 | tf_op jit(solution)/shard_map/ppermute | solution.py:361
  42.3 2.9 %oth_out.1 = (bf16[1024,512]{1,0:T(8,128)(2,1)S(1)}, f32[8,128]{1,0:T(8,128)S(1)}) custom-call(s32[6]{0:T(128)S(1)} %stack.27.meta, bf16[1024,256]{1,0:T(8,128)(2,1)S(1)} %collective-permute-done.4.refs_0_, bf16[1024,256]{1,0:T(8,128)(2,1)S(1)} %collective-permute-done.5.refs_0_.refs_1_, bf16[1024,256]{1,0:T(8,128)(2,1)S(1)} %get-tuple-element.68.refs_2_.refs_3_, ...), custom_call_target="tpu_custom_call" | custom-call | flops 1 | bytes 200000 | tf_op jit(solution)/shard_map/oth_out/pallas_call | solution.py:43
  45.2 3.0 %outer_first.1 = (f32[4,256,256]{2,1,0:T(8,128)S(1)}, bf16[4,256,256]{2,1,0:T(8,128)(2,1)S(1)}, f32[2,512,256]{2,1,0:T(8,128)S(1)}, f32[8,128]{1,0:T(8,128)S(1)}) custom-call(s32[6]{0:T(128)S(1)} %stack.27.meta, bf16[1024,256]{1,0:T(8,128)(2,1)S(1)} %get-tuple-element.71.refs_6_.refs_0_.refs_1_, ...), custom_call_target="tpu_custom_call" | custom-call | flops 1 | bytes 200000 | tf_op jit(solution)/shard_map/outer_first/pallas_call | solution.py:43
  48.2 4.2 %collective-permute-start.11 = (bf16[4,256,256]{2,1,0:T(8,128)(2,1)S(1)}, bf16[4,256,256]{2,1,0:T(8,128)(2,1)S(1)}, u32[]{:S(2)}, u32[]{:S(2)}) collective-permute-start(bf16[4,256,256]{2,1,0:T(8,128)(2,1)S(1)} %get-tuple-element.78), channel_id=1, source_target_pairs={{0,2},{2,0},{4,6},{6,4},{8,10},{10,8},{12,14},{14,12},{16,18},{18,... | collective-permute-start | bytes 1572872 | tf_op jit(solution)/shard_map/ppermute | solution.py:364
  52.6 1.7 %outer_second.1 = (f32[2,256,256]{2,1,0:T(8,128)S(1)}, f32[2,256,256]{2,1,0:T(8,128)S(1)}, f32[8,128]{1,0:T(8,128)S(1)}) custom-call(s32[6]{0:T(128)S(1)} %stack.27.meta, bf16[1024,256]{1,0:T(8,128)(2,1)S(1)} %get-tuple-element.71.refs_6_.refs_0_.refs_1_, bf16[1024,256]{1,0:T(8,128)(2,1)S(1)} %get-tuple-element.72.refs_7_.refs_1_.refs_2_, ...), custom_call_target="tpu_custom_call" | custom-call | flops 1 | bytes 200000 | tf_op jit(solution)/shard_map/outer_second/pallas_call | solution.py:43
  55.8 1.3 %collective-permute-start.12 = (bf16[4,128,256]{2,1,0:T(8,128)(2,1)S(1)}, bf16[4,128,256]{2,1,0:T(8,128)(2,1)S(1)}, u32[]{:S(2)}, u32[]{:S(2)}) collective-permute-start(bf16[4,128,256]{2,1,0:T(8,128)(2,1)S(1)} %get-tuple-element.83), channel_id=1, source_target_pairs={{0,1},{1,0},{2,3},{3,2},{4,5},{5,4},{6,7},{7,6},{8,9},{9,8},{10,11... | collective-permute-start | bytes 786440 | tf_op jit(solution)/shard_map/ppermute | solution.py:367
  57.1 4.1 %collective-permute-start.3 = (bf16[1024,256]{1,0:T(8,128)(2,1)S(1)}, bf16[1024,256]{1,0:T(8,128)(2,1)S(1)}, u32[]{:S(2)}, u32[]{:S(2)}) collective-permute-start(bf16[1024,256]{1,0:T(8,128)(2,1)S(1)} %collective-permute-done.1.refs_4_.refs_3_), channel_id=1, source_target_pairs={{12,4},{14,6},{0,8},{2,10},{20,12},{22,14},{8,16},{10,18},{28,20},... | collective-permute-start | bytes 1572872 | tf_op jit(solution)/shard_map/ppermute | solution.py:361
  62.2 3.8 %oth_grad.1 = (bf16[1024,512]{1,0:T(8,128)(2,1)S(1)}, f32[8,128]{1,0:T(8,128)S(1)}) custom-call(s32[6]{0:T(128)S(1)} %stack.27.meta, bf16[1024,256]{1,0:T(8,128)(2,1)S(1)} %collective-permute-done.4.refs_0_, bf16[1024,256]{1,0:T(8,128)(2,1)S(1)} %collective-permute-done.5.refs_0_.refs_1_, bf16[1024,512]{1,0:T(8,128)(2,1)S(1)} %get-tuple-element.61.refs_8_.refs_2_.refs_1_, ...), custom_call_target="tpu_custom_call" | custom-call | flops 1 | bytes 200000 | tf_op jit(solution)/shard_map/oth_grad/pallas_call | solution.py:43
  67.0 2.0 %collective-permute-start.16 = (bf16[6,64,256]{2,1,0:T(8,128)(2,1)S(1)}, bf16[6,64,256]{2,1,0:T(8,128)(2,1)S(1)}, u32[]{:S(2)}, u32[]{:S(2)}) collective-permute-start(bf16[6,64,256]{2,1,0:T(8,128)(2,1)S(1)} %get-tuple-element.94), channel_id=1, source_target_pairs={{0,8},{2,10},{4,12},{6,14},{8,0},{10,2},{12,4},{14,6},{16,24},{18,... | collective-permute-start | bytes 589832 | tf_op jit(solution)/shard_map/ppermute | solution.py:384
  69.3 3.7 %own_out.1 = (bf16[2048,512]{1,0:T(8,128)(2,1)}, f32[8,128]{1,0:T(8,128)S(1)}) custom-call(s32[6]{0:T(128)S(1)} %stack.27.meta, bf16[2048,512]{1,0:T(8,128)(2,1)S(1)} %bitcast.14, bf16[1024,256]{1,0:T(8,128)(2,1)S(1)} %get-tuple-element.71.refs_6_.refs_0_.refs_1_, bf16[1024,256]{1,0:T(8,128)(2,1)S(1)} %get-tuple-element.72.refs_7_.refs_1_.refs_2_, ...), custom_call_target="tpu_custom_call" | custom-call | flops 1 | bytes 200000 | tf_op jit(solution)/shard_map/own_out/pallas_call | solution.py:43
  75.2 1.9 %collective-permute-done.9.refs_9_ = bf16[1024,512]{1,0:T(8,128)(2,1)S(1)} collective-permute-done((bf16[1024,512]{1,0:T(8,128)(2,1)S(1)}, bf16[1024,512]{1,0:T(8,128)(2,1)S(1)}, u32[]{:S(2)}, u32[]{:S(2)}) %collective-permute-start.9) | collective-permute-done | bytes 1048608 | tf_op jit(solution)/shard_map/ppermute | solution.py:355
  77.2 4.6 %own_grad.1 = (bf16[2048,512]{1,0:T(8,128)(2,1)}, bf16[2048,512]{1,0:T(8,128)(2,1)}, f32[8,128]{1,0:T(8,128)S(1)}) custom-call(s32[6]{0:T(128)S(1)} %stack.27.meta, bf16[2048,512]{1,0:T(8,128)(2,1)S(1)} %bitcast.15, bf16[1024,512]{1,0:T(8,128)(2,1)S(1)} %get-tuple-element.61.refs_8_.refs_2_.refs_1_, ...), custom_call_target="tpu_custom_call", output_to_operand_aliasing={{1}: (11, {})} | custom-call | flops 1 | bytes 200000 | tf_op jit(solution)/shard_map/own_grad/pallas_call | solution.py:43
  82.4 2.2 %collective-permute-start.18 = (f32[6,32,256]{2,1,0:T(8,128)S(1)}, f32[6,32,256]{2,1,0:T(8,128)S(1)}, u32[]{:S(2)}, u32[]{:S(2)}) collective-permute-start(f32[6,32,256]{2,1,0:T(8,128)S(1)} %get-tuple-element.101.refs_0_), channel_id=1, source_target_pairs={{0,12},{2,14},{4,8},{6,10},{8,4},{10,6},{12,0},{14,2},{16,28},{18,... | collective-permute-start | bytes 589832 | tf_op jit(solution)/shard_map/ppermute | solution.py:388
  84.5 3.4 %collective-permute-done.18.refs_1_ = f32[6,32,256]{2,1,0:T(8,128)S(1)} collective-permute-done((f32[6,32,256]{2,1,0:T(8,128)S(1)}, f32[6,32,256]{2,1,0:T(8,128)S(1)}, u32[]{:S(2)}, u32[]{:S(2)}) %collective-permute-start.18) | collective-permute-done | bytes 196640 | tf_op jit(solution)/shard_map/ppermute | solution.py:388
  90.9 2.3 %collective-permute-start.21 = (bf16[6,32,256]{2,1,0:T(8,128)(2,1)S(1)}, bf16[6,32,256]{2,1,0:T(8,128)(2,1)S(1)}, u32[]{:S(2)}, u32[]{:S(2)}) collective-permute-start(bf16[6,32,256]{2,1,0:T(8,128)(2,1)S(1)} %get-tuple-element.103.refs_0_), channel_id=1, source_target_pairs={{0,24},{2,26},{4,28},{6,30},{8,16},{10,18},{12,20},{14,22},{16,0},... | collective-permute-start | bytes 294920 | tf_op jit(solution)/shard_map/ppermute | solution.py:384
  97.0 2.6 %collective-permute-start.27 = (bf16[6,32,256]{2,1,0:T(8,128)(2,1)S(1)}, bf16[6,32,256]{2,1,0:T(8,128)(2,1)S(1)}, u32[]{:S(2)}, u32[]{:S(2)}) collective-permute-start(bf16[6,32,256]{2,1,0:T(8,128)(2,1)S(1)} %collective-permute-done.21.refs_3_), channel_id=1, source_target_pairs={{0,1},{1,0},{2,3},{3,2},{4,5},{5,4},{6,7},{7,6},{8,9},{9,8},{10,11... | collective-permute-start | bytes 294920 | tf_op jit(solution)/shard_map/ppermute | solution.py:367
  100.2 4.4 %collective-permute-start.22 = (bf16[6,128,256]{2,1,0:T(8,128)(2,1)S(1)}, bf16[6,128,256]{2,1,0:T(8,128)(2,1)S(1)}, u32[]{:S(2)}, u32[]{:S(2)}) collective-permute-start(bf16[6,128,256]{2,1,0:T(8,128)(2,1)S(1)} %get-tuple-element.105.refs_0_), channel_id=1, source_target_pairs={{0,2},{2,0},{4,6},{6,4},{8,10},{10,8},{12,14},{14,12},{16,18},{18,... | collective-permute-start | bytes 1179656 | tf_op jit(solution)/shard_map/ppermute | solution.py:364
  105.2 4.0 %collective-permute-start.28 = (bf16[6,128,256]{2,1,0:T(8,128)(2,1)S(1)}, bf16[6,128,256]{2,1,0:T(8,128)(2,1)S(1)}, u32[]{:S(2)}, u32[]{:S(2)}) collective-permute-start(bf16[6,128,256]{2,1,0:T(8,128)(2,1)S(1)} %get-tuple-element.111.refs_0_), channel_id=1, source_target_pairs={{0,2},{2,0},{4,6},{6,4},{8,10},{10,8},{12,14},{14,12},{16,18},{18,... | collective-permute-start | bytes 1179656 | tf_op jit(solution)/shard_map/ppermute | solution.py:364
  109.2 2.1 %write_taps0.1 = (f32[3,512,512]{2,1,0:T(8,128)}, bf16[2048,512]{1,0:T(8,128)(2,1)}, f32[8,128]{1,0:T(8,128)S(1)}) custom-call(s32[6]{0:T(128)S(1)} %stack.27.meta, bf16[6,128,256]{2,1,0:T(8,128)(2,1)S(1)} %get-tuple-element.105.refs_0_, bf16[6,128,256]{2,1,0:T(8,128)(2,1)S(1)} %collective-permute-done.22.refs_1_, ...), custom_call_target="tpu_custom_call", output_to_operand_aliasing={{1}: (4, {})} | custom-call | flops 1 | bytes 200000 | tf_op jit(solution)/shard_map/write_taps0/pallas_call | solution.py:43
  111.4 1.8 %write_taps1.1 = (f32[3,512,512]{2,1,0:T(8,128)}, f32[8,128]{1,0:T(8,128)}) custom-call(s32[6]{0:T(128)S(1)} %stack.27.meta, bf16[6,128,256]{2,1,0:T(8,128)(2,1)S(1)} %get-tuple-element.111.refs_0_, bf16[6,128,256]{2,1,0:T(8,128)(2,1)S(1)} %collective-permute-done.28.refs_1_, ...), custom_call_target="tpu_custom_call", output_to_operand_aliasing={{0}: (3, {})} | custom-call | flops 1 | bytes 200000 | tf_op jit(solution)/shard_map/write_taps1/pallas_call | solution.py:43
  (57 shorter events, 19.0 us)
Async XLA Ops:
  2.3 4.1 %copy-start.3 = (bf16[1,2048,512]{2,1,0:T(8,128)(2,1)S(1)}, bf16[1,2048,512]{2,1,0:T(8,128)(2,1)}, u32[]{:S(2)}) copy-start(bf16[1,2048,512]{2,1,0:T(8,128)(2,1)} %param.5) | copy-start | bytes 6291460
  2.9 16.3 %collective-permute-start.4 = (bf16[1024,256]{1,0:T(8,128)(2,1)S(1)}, bf16[1024,256]{1,0:T(8,128)(2,1)S(1)}, u32[]{:S(2)}, u32[]{:S(2)}) collective-permute-start(bf16[1024,256]{1,0:T(8,128)(2,1)S(1)} %get-tuple-element.64), channel_id=1, source_target_pairs={{0,4},{2,6},{4,0},{6,2},{8,12},{10,14},{12,8},{14,10},{16,20},{18,... | collective-permute-start | bytes 1572872 | tf_op jit(solution)/shard_map/ppermute | solution.py:355
  7.2 20.7 %collective-permute-start.5 = (bf16[1024,256]{1,0:T(8,128)(2,1)S(1)}, bf16[1024,256]{1,0:T(8,128)(2,1)S(1)}, u32[]{:S(2)}, u32[]{:S(2)}) collective-permute-start(bf16[1024,256]{1,0:T(8,128)(2,1)S(1)} %get-tuple-element.65), channel_id=1, source_target_pairs={{0,4},{2,6},{4,0},{6,2},{8,12},{10,14},{12,8},{14,10},{16,20},{18,... | collective-permute-start | bytes 1572872 | tf_op jit(solution)/shard_map/ppermute | solution.py:355
  7.3 24.8 %collective-permute-start.6 = (bf16[1024,256]{1,0:T(8,128)(2,1)S(1)}, bf16[1024,256]{1,0:T(8,128)(2,1)S(1)}, u32[]{:S(2)}, u32[]{:S(2)}) collective-permute-start(bf16[1024,256]{1,0:T(8,128)(2,1)S(1)} %get-tuple-element.71.refs_6_.refs_0_.refs_1_), channel_id=1, source_target_pairs={{4,12},{6,14},{8,0},{10,2},{12,20},{14,22},{16,8},{18,10},{20,28},... | collective-permute-start | bytes 1572872 | tf_op jit(solution)/shard_map/ppermute | solution.py:358
  8.6 24.3 %collective-permute-start.7 = (bf16[1024,256]{1,0:T(8,128)(2,1)S(1)}, bf16[1024,256]{1,0:T(8,128)(2,1)S(1)}, u32[]{:S(2)}, u32[]{:S(2)}) collective-permute-start(bf16[1024,256]{1,0:T(8,128)(2,1)S(1)} %get-tuple-element.72.refs_7_.refs_1_.refs_2_), channel_id=1, source_target_pairs={{4,12},{6,14},{8,0},{10,2},{12,20},{14,22},{16,8},{18,10},{20,28},... | collective-permute-start | bytes 1572872 | tf_op jit(solution)/shard_map/ppermute | solution.py:358
  9.9 29.3 %collective-permute-start = (bf16[1024,256]{1,0:T(8,128)(2,1)S(1)}, bf16[1024,256]{1,0:T(8,128)(2,1)S(1)}, u32[]{:S(2)}, u32[]{:S(2)}) collective-permute-start(bf16[1024,256]{1,0:T(8,128)(2,1)S(1)} %get-tuple-element.62), channel_id=1, source_target_pairs={{0,4},{2,6},{4,0},{6,2},{8,12},{10,14},{12,8},{14,10},{16,20},{18,... | collective-permute-start | bytes 1572872 | tf_op jit(solution)/shard_map/ppermute | solution.py:355
  15.3 27.1 %copy-start = (bf16[3,512,512]{2,1,0:T(8,128)(2,1)S(1)}, bf16[3,512,512]{2,1,0:T(8,128)(2,1)}, u32[]{:S(2)}) copy-start(bf16[3,512,512]{2,1,0:T(8,128)(2,1)} %refs_8_.7) | copy-start | bytes 4718596
  20.3 22.1 %collective-permute-start.8 = (bf16[1024,256]{1,0:T(8,128)(2,1)S(1)}, bf16[1024,256]{1,0:T(8,128)(2,1)S(1)}, u32[]{:S(2)}, u32[]{:S(2)}) collective-permute-start(bf16[1024,256]{1,0:T(8,128)(2,1)S(1)} %get-tuple-element.68.refs_2_.refs_3_), channel_id=1, source_target_pairs={{12,4},{14,6},{0,8},{2,10},{20,12},{22,14},{8,16},{10,18},{28,20},... | collective-permute-start | bytes 1572872 | tf_op jit(solution)/shard_map/ppermute | solution.py:361
  29.0 16.3 %collective-permute-start.10 = (bf16[1024,256]{1,0:T(8,128)(2,1)S(1)}, bf16[1024,256]{1,0:T(8,128)(2,1)S(1)}, u32[]{:S(2)}, u32[]{:S(2)}) collective-permute-start(bf16[1024,256]{1,0:T(8,128)(2,1)S(1)} %get-tuple-element.70.refs_3_.refs_4_), channel_id=1, source_target_pairs={{12,4},{14,6},{0,8},{2,10},{20,12},{22,14},{8,16},{10,18},{28,20},... | collective-permute-start | bytes 1572872 | tf_op jit(solution)/shard_map/ppermute | solution.py:361
  32.1 20.5 %collective-permute-start.1 = (bf16[1024,256]{1,0:T(8,128)(2,1)S(1)}, bf16[1024,256]{1,0:T(8,128)(2,1)S(1)}, u32[]{:S(2)}, u32[]{:S(2)}) collective-permute-start(bf16[1024,256]{1,0:T(8,128)(2,1)S(1)} %get-tuple-element.63), channel_id=1, source_target_pairs={{0,4},{2,6},{4,0},{6,2},{8,12},{10,14},{12,8},{14,10},{16,20},{18,... | collective-permute-start | bytes 1572872 | tf_op jit(solution)/shard_map/ppermute | solution.py:355
  33.0 29.3 %collective-permute-start.15 = (bf16[1024,512]{1,0:T(8,128)(2,1)S(1)}, bf16[1024,512]{1,0:T(8,128)(2,1)S(1)}, u32[]{:S(2)}, u32[]{:S(2)}) collective-permute-start(bf16[1024,512]{1,0:T(8,128)(2,1)S(1)} %get-tuple-element.61.refs_8_.refs_2_.refs_1_), channel_id=1, source_target_pairs={{4,12},{6,14},{8,0},{10,2},{12,20},{14,22},{16,8},{18,10},{20,28},... | collective-permute-start | bytes 3145736 | tf_op jit(solution)/shard_map/ppermute | solution.py:358
  39.2 15.8 %collective-permute-start.2 = (bf16[1024,256]{1,0:T(8,128)(2,1)S(1)}, bf16[1024,256]{1,0:T(8,128)(2,1)S(1)}, u32[]{:S(2)}, u32[]{:S(2)}) collective-permute-start(bf16[1024,256]{1,0:T(8,128)(2,1)S(1)} %collective-permute-done.refs_9_.refs_3_.refs_2_), channel_id=1, source_target_pairs={{12,4},{14,6},{0,8},{2,10},{20,12},{22,14},{8,16},{10,18},{28,20},... | collective-permute-start | bytes 1572872 | tf_op jit(solution)/shard_map/ppermute | solution.py:361
  48.2 6.9 %collective-permute-start.11 = (bf16[4,256,256]{2,1,0:T(8,128)(2,1)S(1)}, bf16[4,256,256]{2,1,0:T(8,128)(2,1)S(1)}, u32[]{:S(2)}, u32[]{:S(2)}) collective-permute-start(bf16[4,256,256]{2,1,0:T(8,128)(2,1)S(1)} %get-tuple-element.78), channel_id=1, source_target_pairs={{0,2},{2,0},{4,6},{6,4},{8,10},{10,8},{12,14},{14,12},{16,18},{18,... | collective-permute-start | bytes 1572872 | tf_op jit(solution)/shard_map/ppermute | solution.py:364
  52.4 24.7 %collective-permute-start.9 = (bf16[1024,512]{1,0:T(8,128)(2,1)S(1)}, bf16[1024,512]{1,0:T(8,128)(2,1)S(1)}, u32[]{:S(2)}, u32[]{:S(2)}) collective-permute-start(bf16[1024,512]{1,0:T(8,128)(2,1)S(1)} %get-tuple-element.74), channel_id=1, source_target_pairs={{0,4},{2,6},{4,0},{6,2},{8,12},{10,14},{12,8},{14,10},{16,20},{18,... | collective-permute-start | bytes 3145736 | tf_op jit(solution)/shard_map/ppermute | solution.py:355
  54.3 7.0 %collective-permute-start.13 = (f32[2,256,256]{2,1,0:T(8,128)S(1)}, f32[2,256,256]{2,1,0:T(8,128)S(1)}, u32[]{:S(2)}, u32[]{:S(2)}) collective-permute-start(f32[2,256,256]{2,1,0:T(8,128)S(1)} %get-tuple-element.85), channel_id=1, source_target_pairs={{0,2},{2,0},{4,6},{6,4},{8,10},{10,8},{12,14},{14,12},{16,18},{18,... | collective-permute-start | bytes 1572872 | tf_op jit(solution)/shard_map/ppermute | solution.py:364
  55.8 10.4 %collective-permute-start.12 = (bf16[4,128,256]{2,1,0:T(8,128)(2,1)S(1)}, bf16[4,128,256]{2,1,0:T(8,128)(2,1)S(1)}, u32[]{:S(2)}, u32[]{:S(2)}) collective-permute-start(bf16[4,128,256]{2,1,0:T(8,128)(2,1)S(1)} %get-tuple-element.83), channel_id=1, source_target_pairs={{0,1},{1,0},{2,3},{3,2},{4,5},{5,4},{6,7},{7,6},{8,9},{9,8},{10,11... | collective-permute-start | bytes 786440 | tf_op jit(solution)/shard_map/ppermute | solution.py:367
  57.1 18.1 %collective-permute-start.3 = (bf16[1024,256]{1,0:T(8,128)(2,1)S(1)}, bf16[1024,256]{1,0:T(8,128)(2,1)S(1)}, u32[]{:S(2)}, u32[]{:S(2)}) collective-permute-start(bf16[1024,256]{1,0:T(8,128)(2,1)S(1)} %collective-permute-done.1.refs_4_.refs_3_), channel_id=1, source_target_pairs={{12,4},{14,6},{0,8},{2,10},{20,12},{22,14},{8,16},{10,18},{28,20},... | collective-permute-start | bytes 1572872 | tf_op jit(solution)/shard_map/ppermute | solution.py:361
  61.9 4.4 %collective-permute-start.14 = (bf16[2,128,256]{2,1,0:T(8,128)(2,1)S(1)}, bf16[2,128,256]{2,1,0:T(8,128)(2,1)S(1)}, u32[]{:S(2)}, u32[]{:S(2)}) collective-permute-start(bf16[2,128,256]{2,1,0:T(8,128)(2,1)S(1)} %get-tuple-element.88), channel_id=1, source_target_pairs={{0,1},{1,0},{2,3},{3,2},{4,5},{5,4},{6,7},{7,6},{8,9},{9,8},{10,11... | collective-permute-start | bytes 393224 | tf_op jit(solution)/shard_map/ppermute | solution.py:367
  62.2 7.1 %copy-start.2 = (bf16[1,2048,512]{2,1,0:T(8,128)(2,1)S(1)}, bf16[1,2048,512]{2,1,0:T(8,128)(2,1)}, u32[]{:S(2)}) copy-start(bf16[1,2048,512]{2,1,0:T(8,128)(2,1)} %param.3) | copy-start | bytes 6291460
  67.0 6.8 %collective-permute-start.16 = (bf16[6,64,256]{2,1,0:T(8,128)(2,1)S(1)}, bf16[6,64,256]{2,1,0:T(8,128)(2,1)S(1)}, u32[]{:S(2)}, u32[]{:S(2)}) collective-permute-start(bf16[6,64,256]{2,1,0:T(8,128)(2,1)S(1)} %get-tuple-element.94), channel_id=1, source_target_pairs={{0,8},{2,10},{4,12},{6,14},{8,0},{10,2},{12,4},{14,6},{16,24},{18,... | collective-permute-start | bytes 589832 | tf_op jit(solution)/shard_map/ppermute | solution.py:384
  69.0 40.2 %collective-permute-start.23 = (bf16[1024,512]{1,0:T(8,128)(2,1)S(1)}, bf16[1024,512]{1,0:T(8,128)(2,1)S(1)}, u32[]{:S(2)}, u32[]{:S(2)}) collective-permute-start(bf16[1024,512]{1,0:T(8,128)(2,1)S(1)} %get-tuple-element.106), channel_id=1, source_target_pairs={{0,4},{2,6},{4,0},{6,2},{8,12},{10,14},{12,8},{14,10},{16,20},{18,... | collective-permute-start | bytes 3145736 | tf_op jit(solution)/shard_map/ppermute | solution.py:355
  74.4 7.4 %collective-permute-start.17 = (bf16[6,32,256]{2,1,0:T(8,128)(2,1)S(1)}, bf16[6,32,256]{2,1,0:T(8,128)(2,1)S(1)}, u32[]{:S(2)}, u32[]{:S(2)}) collective-permute-start(bf16[6,32,256]{2,1,0:T(8,128)(2,1)S(1)} %get-tuple-element.99), channel_id=1, source_target_pairs={{0,16},{2,18},{4,20},{6,22},{8,24},{10,26},{12,28},{14,30},{16,0},... | collective-permute-start | bytes 294920 | tf_op jit(solution)/shard_map/ppermute | solution.py:384
  82.4 5.6 %collective-permute-start.18 = (f32[6,32,256]{2,1,0:T(8,128)S(1)}, f32[6,32,256]{2,1,0:T(8,128)S(1)}, u32[]{:S(2)}, u32[]{:S(2)}) collective-permute-start(f32[6,32,256]{2,1,0:T(8,128)S(1)} %get-tuple-element.101.refs_0_), channel_id=1, source_target_pairs={{0,12},{2,14},{4,8},{6,10},{8,4},{10,6},{12,0},{14,2},{16,28},{18,... | collective-permute-start | bytes 589832 | tf_op jit(solution)/shard_map/ppermute | solution.py:388
  88.5 5.8 %collective-permute-start.19 = (bf16[6,32,256]{2,1,0:T(8,128)(2,1)S(1)}, bf16[6,32,256]{2,1,0:T(8,128)(2,1)S(1)}, u32[]{:S(2)}, u32[]{:S(2)}) collective-permute-start(bf16[6,32,256]{2,1,0:T(8,128)(2,1)S(1)} %get-tuple-element.103.refs_0_), channel_id=1, source_target_pairs={{0,16},{2,18},{4,20},{6,22},{8,24},{10,26},{12,28},{14,30},{16,8},... | collective-permute-start | bytes 294920 | tf_op jit(solution)/shard_map/ppermute | solution.py:384
  89.8 5.4 %collective-permute-start.20 = (bf16[6,32,256]{2,1,0:T(8,128)(2,1)S(1)}, bf16[6,32,256]{2,1,0:T(8,128)(2,1)S(1)}, u32[]{:S(2)}, u32[]{:S(2)}) collective-permute-start(bf16[6,32,256]{2,1,0:T(8,128)(2,1)S(1)} %get-tuple-element.103.refs_0_), channel_id=1, source_target_pairs={{0,8},{2,10},{4,12},{6,14},{8,0},{10,2},{12,4},{14,6},{16,24},{18,... | collective-permute-start | bytes 294920 | tf_op jit(solution)/shard_map/ppermute | solution.py:384
  90.9 6.1 %collective-permute-start.21 = (bf16[6,32,256]{2,1,0:T(8,128)(2,1)S(1)}, bf16[6,32,256]{2,1,0:T(8,128)(2,1)S(1)}, u32[]{:S(2)}, u32[]{:S(2)}) collective-permute-start(bf16[6,32,256]{2,1,0:T(8,128)(2,1)S(1)} %get-tuple-element.103.refs_0_), channel_id=1, source_target_pairs={{0,24},{2,26},{4,28},{6,30},{8,16},{10,18},{12,20},{14,22},{16,0},... | collective-permute-start | bytes 294920 | tf_op jit(solution)/shard_map/ppermute | solution.py:384
  93.1 7.0 %collective-permute-start.24 = (bf16[6,32,256]{2,1,0:T(8,128)(2,1)S(1)}, bf16[6,32,256]{2,1,0:T(8,128)(2,1)S(1)}, u32[]{:S(2)}, u32[]{:S(2)}) collective-permute-start(bf16[6,32,256]{2,1,0:T(8,128)(2,1)S(1)} %get-tuple-element.103.refs_0_), channel_id=1, source_target_pairs={{0,1},{1,0},{2,3},{3,2},{4,5},{5,4},{6,7},{7,6},{8,9},{9,8},{10,11... | collective-permute-start | bytes 294920 | tf_op jit(solution)/shard_map/ppermute | solution.py:367
  94.4 10.2 %collective-permute-start.25 = (bf16[6,32,256]{2,1,0:T(8,128)(2,1)S(1)}, bf16[6,32,256]{2,1,0:T(8,128)(2,1)S(1)}, u32[]{:S(2)}, u32[]{:S(2)}) collective-permute-start(bf16[6,32,256]{2,1,0:T(8,128)(2,1)S(1)} %collective-permute-done.19.refs_1_), channel_id=1, source_target_pairs={{0,1},{1,0},{2,3},{3,2},{4,5},{5,4},{6,7},{7,6},{8,9},{9,8},{10,11... | collective-permute-start | bytes 294920 | tf_op jit(solution)/shard_map/ppermute | solution.py:367
  95.2 9.4 %collective-permute-start.26 = (bf16[6,32,256]{2,1,0:T(8,128)(2,1)S(1)}, bf16[6,32,256]{2,1,0:T(8,128)(2,1)S(1)}, u32[]{:S(2)}, u32[]{:S(2)}) collective-permute-start(bf16[6,32,256]{2,1,0:T(8,128)(2,1)S(1)} %collective-permute-done.20.refs_2_), channel_id=1, source_target_pairs={{0,1},{1,0},{2,3},{3,2},{4,5},{5,4},{6,7},{7,6},{8,9},{9,8},{10,11... | collective-permute-start | bytes 294920 | tf_op jit(solution)/shard_map/ppermute | solution.py:367
  97.0 7.6 %collective-permute-start.27 = (bf16[6,32,256]{2,1,0:T(8,128)(2,1)S(1)}, bf16[6,32,256]{2,1,0:T(8,128)(2,1)S(1)}, u32[]{:S(2)}, u32[]{:S(2)}) collective-permute-start(bf16[6,32,256]{2,1,0:T(8,128)(2,1)S(1)} %collective-permute-done.21.refs_3_), channel_id=1, source_target_pairs={{0,1},{1,0},{2,3},{3,2},{4,5},{5,4},{6,7},{7,6},{8,9},{9,8},{10,11... | collective-permute-start | bytes 294920 | tf_op jit(solution)/shard_map/ppermute | solution.py:367
  100.2 9.0 %collective-permute-start.22 = (bf16[6,128,256]{2,1,0:T(8,128)(2,1)S(1)}, bf16[6,128,256]{2,1,0:T(8,128)(2,1)S(1)}, u32[]{:S(2)}, u32[]{:S(2)}) collective-permute-start(bf16[6,128,256]{2,1,0:T(8,128)(2,1)S(1)} %get-tuple-element.105.refs_0_), channel_id=1, source_target_pairs={{0,2},{2,0},{4,6},{6,4},{8,10},{10,8},{12,14},{14,12},{16,18},{18,... | collective-permute-start | bytes 1179656 | tf_op jit(solution)/shard_map/ppermute | solution.py:364
  105.2 6.2 %collective-permute-start.28 = (bf16[6,128,256]{2,1,0:T(8,128)(2,1)S(1)}, bf16[6,128,256]{2,1,0:T(8,128)(2,1)S(1)}, u32[]{:S(2)}, u32[]{:S(2)}) collective-permute-start(bf16[6,128,256]{2,1,0:T(8,128)(2,1)S(1)} %get-tuple-element.111.refs_0_), channel_id=1, source_target_pairs={{0,2},{2,0},{4,6},{6,4},{8,10},{10,8},{12,14},{14,12},{16,18},{18,... | collective-permute-start | bytes 1179656 | tf_op jit(solution)/shard_map/ppermute | solution.py:364
  (1 other events, 1.6 us)

commit v7 on v5

--- a/solution.py
+++ b/solution.py
@@ -399,6 +399,9 @@
     device = Device(meta)
 
     part_spec = pl.BlockSpec((block, cols), lambda i, s: (i, 0))
+    part_wide = pl.BlockSpec((2 * block, cols), lambda i, s: (i, 0))
+    rows_wide = pl.BlockSpec((2 * block, chans), lambda i, s: (i, 0))
+    own_wide = pl.BlockSpec((2 * block, chans), lambda i, s: (s[SIDE] * (steps // 2) + i, 0))
     weights, weight_specs = (conv_weight,) * 3, [w_near, w_mid, w_far]
 
     staged = halving and (chans // tap // dp_count) % (16 * along_count) == 0
@@ -509,10 +512,10 @@
     )
     parts = along_stage([parts], 1)
     grad_genome, output = call(
-        functools.partial(own_grad_body, steps), device,
+        functools.partial(own_grad_body, steps // 2), device,
         (genome, u_own, *u_oth, *u_own_far, *weights, out, output),
-        [own_spec, rows_spec, *[part_spec] * 4, *weight_specs, HBM, HBM], [whole_shape] * 2, [own_spec, HBM],
-        grid=(steps,), scratch=[pltpu.SemaphoreType.DMA], aliases={11: 1}, name="own_grad",
+        [own_wide, rows_wide, *[part_wide] * 4, *weight_specs, HBM, HBM], [whole_shape] * 2, [own_wide, HBM],
+        grid=(steps // 2,), scratch=[pltpu.SemaphoreType.DMA], aliases={11: 1}, name="own_grad",
     )
     parts = side_stage([parts])
     last_slice = round_slice(parts)

time: 113 us -> 114 us (level)
    ppermute x4, starting transfers between devices: 9.96 us -> 11.5 us  [to_core(): lax.ppermute(value, 'seq', [(i, i - i % tap + (i % tap + shift) % tap) fo...]
  transfers between devices with their start and end apart: 29 -> 29, of which waited for: 7 -> 6; matrix products, arithmetic and copies ran while one was open for 0% -> 0% of each run, Pallas kernels for 32% -> 31%
where the time goes in v7:
time: 114 us; the launch traced here: 113 us
  starting transfers between devices  56.4 us (49%)
  Pallas kernels  38 us (33%)
  waiting for transfers between devices  16.4 us (14%)
  local copies, waits for them, and re-layouts  1.69 us (1%)
    pallas_call x22, Pallas kernels, call(): pl.pallas_call(chained, grid_spec=pltpu.PrefetchScalarGridSpec(num_scalar...  38 us
    ppermute x4, starting transfers between devices, inward(): return lax.ppermute(value, 'seq', inner_pairs)  13.2 us
    ppermute x4, starting transfers between devices, to_core(): lax.ppermute(value, 'seq', [(i, i - i % tap + (i % tap + shift) % tap) fo...  11.5 us
    ppermute x6, waiting for transfers between devices, swap(): return lax.ppermute(value, 'seq', swap_pairs)  11.3 us
    ppermute x6, starting transfers between devices, swap(): return lax.ppermute(value, 'seq', swap_pairs)  9.11 us
    ppermute x6, starting transfers between devices, to_dp(): lax.ppermute(value, 'dp', [(i, (i + shift) % dp_count) for i in range(dp_...  8.82 us
    ppermute x5, starting transfers between devices, to_along(): return lax.ppermute(value, 'seq', pairs)  7.82 us
    ppermute x3, starting transfers between devices, outward(): return lax.ppermute(value, 'seq', outer_pairs)  3.86 us
  transfers between devices with their start and end apart: 29, of which 6 were waited for; matrix products, arithmetic and copies ran while one was open for 0% of the time, Pallas kernels for 31%

profile of v7, /device:TPU:1, one launch (start us, length us, event | category | flops | bytes accessed | tf_op | source)
XLA Modules:
  0.0 113.5 jit_solution(5194376116607278314)
XLA Ops:
  0.7 1.6 %copy-done.1 = bf16[1,2048,512]{2,1,0:T(8,128)(2,1)S(1)} copy-done((bf16[1,2048,512]{2,1,0:T(8,128)(2,1)S(1)}, bf16[1,2048,512]{2,1,0:T(8,128)(2,1)}, u32[]{:S(2)}) %copy-start.1) | copy-done | bytes 2097176
  2.9 2.1 %collective-permute-start.4 = (bf16[1024,256]{1,0:T(8,128)(2,1)S(1)}, bf16[1024,256]{1,0:T(8,128)(2,1)S(1)}, u32[]{:S(2)}, u32[]{:S(2)}) collective-permute-start(bf16[1024,256]{1,0:T(8,128)(2,1)S(1)} %get-tuple-element.64), channel_id=1, source_target_pairs={{0,4},{2,6},{4,0},{6,2},{8,12},{10,14},{12,8},{14,10},{16,20},{18,... | collective-permute-start | bytes 1572872 | tf_op jit(solution)/shard_map/ppermute | solution.py:355
  5.1 1.4 %own_act.1 = (bf16[1024,256]{1,0:T(8,128)(2,1)S(1)}, bf16[1024,256]{1,0:T(8,128)(2,1)S(1)}, f32[8,128]{1,0:T(8,128)S(1)}) custom-call(s32[6]{0:T(128)S(1)} %stack.27.meta, bf16[2048,512]{1,0:T(8,128)(2,1)S(1)} %bitcast.11, f32[8,128]{1,0:T(8,128)S(1)} %get-tuple-element.59.refs_1_), custom_call_target="tpu_custom_call" | custom-call | flops 1 | bytes 200000 | tf_op jit(solution)/shard_map/own_act/pallas_call | solution.py:43
  7.3 1.3 %collective-permute-start.6 = (bf16[1024,256]{1,0:T(8,128)(2,1)S(1)}, bf16[1024,256]{1,0:T(8,128)(2,1)S(1)}, u32[]{:S(2)}, u32[]{:S(2)}) collective-permute-start(bf16[1024,256]{1,0:T(8,128)(2,1)S(1)} %get-tuple-element.71.refs_6_.refs_0_.refs_1_), channel_id=1, source_target_pairs={{4,12},{6,14},{8,0},{10,2},{12,20},{14,22},{16,8},{18,10},{20,28},... | collective-permute-start | bytes 1572872 | tf_op jit(solution)/shard_map/ppermute | solution.py:358
  8.6 1.3 %collective-permute-start.7 = (bf16[1024,256]{1,0:T(8,128)(2,1)S(1)}, bf16[1024,256]{1,0:T(8,128)(2,1)S(1)}, u32[]{:S(2)}, u32[]{:S(2)}) collective-permute-start(bf16[1024,256]{1,0:T(8,128)(2,1)S(1)} %get-tuple-element.72.refs_7_.refs_1_.refs_2_), channel_id=1, source_target_pairs={{4,12},{6,14},{8,0},{10,2},{12,20},{14,22},{16,8},{18,10},{20,28},... | collective-permute-start | bytes 1572872 | tf_op jit(solution)/shard_map/ppermute | solution.py:358
  9.9 5.4 %collective-permute-start = (bf16[1024,256]{1,0:T(8,128)(2,1)S(1)}, bf16[1024,256]{1,0:T(8,128)(2,1)S(1)}, u32[]{:S(2)}, u32[]{:S(2)}) collective-permute-start(bf16[1024,256]{1,0:T(8,128)(2,1)S(1)} %get-tuple-element.62), channel_id=1, source_target_pairs={{0,4},{2,6},{4,0},{6,2},{8,12},{10,14},{12,8},{14,10},{16,20},{18,... | collective-permute-start | bytes 1572872 | tf_op jit(solution)/shard_map/ppermute | solution.py:355
  15.3 4.0 %mid_tap.1 = (f32[2,512,256]{2,1,0:T(8,128)S(1)}, f32[8,128]{1,0:T(8,128)S(1)}) custom-call(s32[6]{0:T(128)S(1)} %stack.27.meta, bf16[2048,512]{1,0:T(8,128)(2,1)S(1)} %bitcast.13, bf16[2048,512]{1,0:T(8,128)(2,1)S(1)} %bitcast.17, f32[8,128]{1,0:T(8,128)S(1)} %get-tuple-element.66.refs_2_), custom_call_target="tpu_custom_call" | custom-call | flops 1 | bytes 200000 | tf_op jit(solution)/shard_map/mid_tap/pallas_call | solution.py:43
  20.3 3.2 %collective-permute-start.8 = (bf16[1024,256]{1,0:T(8,128)(2,1)S(1)}, bf16[1024,256]{1,0:T(8,128)(2,1)S(1)}, u32[]{:S(2)}, u32[]{:S(2)}) collective-permute-start(bf16[1024,256]{1,0:T(8,128)(2,1)S(1)} %get-tuple-element.68.refs_2_.refs_3_), channel_id=1, source_target_pairs={{12,4},{14,6},{0,8},{2,10},{20,12},{22,14},{8,16},{10,18},{28,20},... | collective-permute-start | bytes 1572872 | tf_op jit(solution)/shard_map/ppermute | solution.py:361
  23.5 4.5 %collective-permute-done.5.refs_0_.refs_1_ = bf16[1024,256]{1,0:T(8,128)(2,1)S(1)} collective-permute-done((bf16[1024,256]{1,0:T(8,128)(2,1)S(1)}, bf16[1024,256]{1,0:T(8,128)(2,1)S(1)}, u32[]{:S(2)}, u32[]{:S(2)}) %collective-permute-start.5) | collective-permute-done | bytes 524320 | tf_op jit(solution)/shard_map/ppermute | solution.py:355
  29.0 3.1 %collective-permute-start.10 = (bf16[1024,256]{1,0:T(8,128)(2,1)S(1)}, bf16[1024,256]{1,0:T(8,128)(2,1)S(1)}, u32[]{:S(2)}, u32[]{:S(2)}) collective-permute-start(bf16[1024,256]{1,0:T(8,128)(2,1)S(1)} %get-tuple-element.70.refs_3_.refs_4_), channel_id=1, source_target_pairs={{12,4},{14,6},{0,8},{2,10},{20,12},{22,14},{8,16},{10,18},{28,20},... | collective-permute-start | bytes 1572872 | tf_op jit(solution)/shard_map/ppermute | solution.py:361
  34.2 5.0 %collective-permute-done.refs_9_.refs_3_.refs_2_ = bf16[1024,256]{1,0:T(8,128)(2,1)S(1)} collective-permute-done((bf16[1024,256]{1,0:T(8,128)(2,1)S(1)}, bf16[1024,256]{1,0:T(8,128)(2,1)S(1)}, u32[]{:S(2)}, u32[]{:S(2)}) %collective-permute-start) | collective-permute-done | bytes 524320 | tf_op jit(solution)/shard_map/ppermute | solution.py:355
  39.2 3.1 %collective-permute-start.2 = (bf16[1024,256]{1,0:T(8,128)(2,1)S(1)}, bf16[1024,256]{1,0:T(8,128)(2,1)S(1)}, u32[]{:S(2)}, u32[]{:S(2)}) collective-permute-start(bf16[1024,256]{1,0:T(8,128)(2,1)S(1)} %collective-permute-done.refs_9_.refs_3_.refs_2_), channel_id=1, source_target_pairs={{12,4},{14,6},{0,8},{2,10},{20,12},{22,14},{8,16},{10,18},{28,20},... | collective-permute-start | bytes 1572872 | tf_op jit(solution)/shard_map/ppermute | solution.py:361
  42.3 2.9 %oth_out.1 = (bf16[1024,512]{1,0:T(8,128)(2,1)S(1)}, f32[8,128]{1,0:T(8,128)S(1)}) custom-call(s32[6]{0:T(128)S(1)} %stack.27.meta, bf16[1024,256]{1,0:T(8,128)(2,1)S(1)} %collective-permute-done.4.refs_0_, bf16[1024,256]{1,0:T(8,128)(2,1)S(1)} %collective-permute-done.5.refs_0_.refs_1_, bf16[1024,256]{1,0:T(8,128)(2,1)S(1)} %get-tuple-element.68.refs_2_.refs_3_, ...), custom_call_target="tpu_custom_call" | custom-call | flops 1 | bytes 200000 | tf_op jit(solution)/shard_map/oth_out/pallas_call | solution.py:43
  45.2 3.4 %outer_first.1 = (f32[4,256,256]{2,1,0:T(8,128)S(1)}, bf16[4,256,256]{2,1,0:T(8,128)(2,1)S(1)}, f32[2,512,256]{2,1,0:T(8,128)S(1)}, f32[8,128]{1,0:T(8,128)S(1)}) custom-call(s32[6]{0:T(128)S(1)} %stack.27.meta, bf16[1024,256]{1,0:T(8,128)(2,1)S(1)} %get-tuple-element.71.refs_6_.refs_0_.refs_1_, ...), custom_call_target="tpu_custom_call" | custom-call | flops 1 | bytes 200000 | tf_op jit(solution)/shard_map/outer_first/pallas_call | solution.py:43
  48.7 4.2 %collective-permute-start.11 = (bf16[4,256,256]{2,1,0:T(8,128)(2,1)S(1)}, bf16[4,256,256]{2,1,0:T(8,128)(2,1)S(1)}, u32[]{:S(2)}, u32[]{:S(2)}) collective-permute-start(bf16[4,256,256]{2,1,0:T(8,128)(2,1)S(1)} %get-tuple-element.78), channel_id=1, source_target_pairs={{0,2},{2,0},{4,6},{6,4},{8,10},{10,8},{12,14},{14,12},{16,18},{18,... | collective-permute-start | bytes 1572872 | tf_op jit(solution)/shard_map/ppermute | solution.py:364
  53.1 2.1 %outer_second.1 = (f32[2,256,256]{2,1,0:T(8,128)S(1)}, f32[2,256,256]{2,1,0:T(8,128)S(1)}, f32[8,128]{1,0:T(8,128)S(1)}) custom-call(s32[6]{0:T(128)S(1)} %stack.27.meta, bf16[1024,256]{1,0:T(8,128)(2,1)S(1)} %get-tuple-element.71.refs_6_.refs_0_.refs_1_, bf16[1024,256]{1,0:T(8,128)(2,1)S(1)} %get-tuple-element.72.refs_7_.refs_1_.refs_2_, ...), custom_call_target="tpu_custom_call" | custom-call | flops 1 | bytes 200000 | tf_op jit(solution)/shard_map/outer_second/pallas_call | solution.py:43
  57.7 3.7 %collective-permute-start.3 = (bf16[1024,256]{1,0:T(8,128)(2,1)S(1)}, bf16[1024,256]{1,0:T(8,128)(2,1)S(1)}, u32[]{:S(2)}, u32[]{:S(2)}) collective-permute-start(bf16[1024,256]{1,0:T(8,128)(2,1)S(1)} %collective-permute-done.1.refs_4_.refs_3_), channel_id=1, source_target_pairs={{12,4},{14,6},{0,8},{2,10},{20,12},{22,14},{8,16},{10,18},{28,20},... | collective-permute-start | bytes 1572872 | tf_op jit(solution)/shard_map/ppermute | solution.py:361
  62.4 3.8 %oth_grad.1 = (bf16[1024,512]{1,0:T(8,128)(2,1)S(1)}, f32[8,128]{1,0:T(8,128)S(1)}) custom-call(s32[6]{0:T(128)S(1)} %stack.27.meta, bf16[1024,256]{1,0:T(8,128)(2,1)S(1)} %collective-permute-done.4.refs_0_, bf16[1024,256]{1,0:T(8,128)(2,1)S(1)} %collective-permute-done.5.refs_0_.refs_1_, bf16[1024,512]{1,0:T(8,128)(2,1)S(1)} %get-tuple-element.61.refs_8_.refs_2_.refs_1_, ...), custom_call_target="tpu_custom_call" | custom-call | flops 1 | bytes 200000 | tf_op jit(solution)/shard_map/oth_grad/pallas_call | solution.py:43
  67.0 2.0 %collective-permute-start.16 = (bf16[6,64,256]{2,1,0:T(8,128)(2,1)S(1)}, bf16[6,64,256]{2,1,0:T(8,128)(2,1)S(1)}, u32[]{:S(2)}, u32[]{:S(2)}) collective-permute-start(bf16[6,64,256]{2,1,0:T(8,128)(2,1)S(1)} %get-tuple-element.94), channel_id=1, source_target_pairs={{0,8},{2,10},{4,12},{6,14},{8,0},{10,2},{12,4},{14,6},{16,24},{18,... | collective-permute-start | bytes 589832 | tf_op jit(solution)/shard_map/ppermute | solution.py:384
  69.0 1.3 %collective-permute-start.23 = (bf16[1024,512]{1,0:T(8,128)(2,1)S(1)}, bf16[1024,512]{1,0:T(8,128)(2,1)S(1)}, u32[]{:S(2)}, u32[]{:S(2)}) collective-permute-start(bf16[1024,512]{1,0:T(8,128)(2,1)S(1)} %get-tuple-element.106), channel_id=1, source_target_pairs={{0,4},{2,6},{4,0},{6,2},{8,12},{10,14},{12,8},{14,10},{16,20},{18,... | collective-permute-start | bytes 3145736 | tf_op jit(solution)/shard_map/ppermute | solution.py:355
  70.3 3.7 %own_out.1 = (bf16[2048,512]{1,0:T(8,128)(2,1)}, f32[8,128]{1,0:T(8,128)S(1)}) custom-call(s32[6]{0:T(128)S(1)} %stack.27.meta, bf16[2048,512]{1,0:T(8,128)(2,1)S(1)} %bitcast.14, bf16[1024,256]{1,0:T(8,128)(2,1)S(1)} %get-tuple-element.71.refs_6_.refs_0_.refs_1_, bf16[1024,256]{1,0:T(8,128)(2,1)S(1)} %get-tuple-element.72.refs_7_.refs_1_.refs_2_, ...), custom_call_target="tpu_custom_call" | custom-call | flops 1 | bytes 200000 | tf_op jit(solution)/shard_map/own_out/pallas_call | solution.py:43
  75.8 1.8 %collective-permute-done.9.refs_9_ = bf16[1024,512]{1,0:T(8,128)(2,1)S(1)} collective-permute-done((bf16[1024,512]{1,0:T(8,128)(2,1)S(1)}, bf16[1024,512]{1,0:T(8,128)(2,1)S(1)}, u32[]{:S(2)}, u32[]{:S(2)}) %collective-permute-start.9) | collective-permute-done | bytes 1048608 | tf_op jit(solution)/shard_map/ppermute | solution.py:355
  77.6 4.4 %own_grad.1 = (bf16[2048,512]{1,0:T(8,128)(2,1)}, bf16[2048,512]{1,0:T(8,128)(2,1)}, f32[8,128]{1,0:T(8,128)S(1)}) custom-call(s32[6]{0:T(128)S(1)} %stack.27.meta, bf16[2048,512]{1,0:T(8,128)(2,1)S(1)} %bitcast.15, bf16[1024,512]{1,0:T(8,128)(2,1)S(1)} %get-tuple-element.61.refs_8_.refs_2_.refs_1_, ...), custom_call_target="tpu_custom_call", output_to_operand_aliasing={{1}: (11, {})} | custom-call | flops 1 | bytes 200000 | tf_op jit(solution)/shard_map/own_grad/pallas_call | solution.py:43
  82.6 2.2 %collective-permute-start.18 = (f32[6,32,256]{2,1,0:T(8,128)S(1)}, f32[6,32,256]{2,1,0:T(8,128)S(1)}, u32[]{:S(2)}, u32[]{:S(2)}) collective-permute-start(f32[6,32,256]{2,1,0:T(8,128)S(1)} %get-tuple-element.101.refs_0_), channel_id=1, source_target_pairs={{0,12},{2,14},{4,8},{6,10},{8,4},{10,6},{12,0},{14,2},{16,28},{18,... | collective-permute-start | bytes 589832 | tf_op jit(solution)/shard_map/ppermute | solution.py:388
  84.8 3.4 %collective-permute-done.18.refs_1_ = f32[6,32,256]{2,1,0:T(8,128)S(1)} collective-permute-done((f32[6,32,256]{2,1,0:T(8,128)S(1)}, f32[6,32,256]{2,1,0:T(8,128)S(1)}, u32[]{:S(2)}, u32[]{:S(2)}) %collective-permute-start.18) | collective-permute-done | bytes 196640 | tf_op jit(solution)/shard_map/ppermute | solution.py:388
  91.1 2.3 %collective-permute-start.21 = (bf16[6,32,256]{2,1,0:T(8,128)(2,1)S(1)}, bf16[6,32,256]{2,1,0:T(8,128)(2,1)S(1)}, u32[]{:S(2)}, u32[]{:S(2)}) collective-permute-start(bf16[6,32,256]{2,1,0:T(8,128)(2,1)S(1)} %get-tuple-element.103.refs_0_), channel_id=1, source_target_pairs={{0,24},{2,26},{4,28},{6,30},{8,16},{10,18},{12,20},{14,22},{16,0},... | collective-permute-start | bytes 294920 | tf_op jit(solution)/shard_map/ppermute | solution.py:384
  93.4 1.5 %collective-permute-start.24 = (bf16[6,32,256]{2,1,0:T(8,128)(2,1)S(1)}, bf16[6,32,256]{2,1,0:T(8,128)(2,1)S(1)}, u32[]{:S(2)}, u32[]{:S(2)}) collective-permute-start(bf16[6,32,256]{2,1,0:T(8,128)(2,1)S(1)} %get-tuple-element.103.refs_0_), channel_id=1, source_target_pairs={{0,1},{1,0},{2,3},{3,2},{4,5},{5,4},{6,7},{7,6},{8,9},{9,8},{10,11... | collective-permute-start | bytes 294920 | tf_op jit(solution)/shard_map/ppermute | solution.py:367
  97.3 4.3 %collective-permute-start.27 = (bf16[6,32,256]{2,1,0:T(8,128)(2,1)S(1)}, bf16[6,32,256]{2,1,0:T(8,128)(2,1)S(1)}, u32[]{:S(2)}, u32[]{:S(2)}) collective-permute-start(bf16[6,32,256]{2,1,0:T(8,128)(2,1)S(1)} %collective-permute-done.21.refs_3_), channel_id=1, source_target_pairs={{0,1},{1,0},{2,3},{3,2},{4,5},{5,4},{6,7},{7,6},{8,9},{9,8},{10,11... | collective-permute-start | bytes 294920 | tf_op jit(solution)/shard_map/ppermute | solution.py:367
  102.1 2.8 %collective-permute-start.22 = (bf16[6,128,256]{2,1,0:T(8,128)(2,1)S(1)}, bf16[6,128,256]{2,1,0:T(8,128)(2,1)S(1)}, u32[]{:S(2)}, u32[]{:S(2)}) collective-permute-start(bf16[6,128,256]{2,1,0:T(8,128)(2,1)S(1)} %get-tuple-element.105.refs_0_), channel_id=1, source_target_pairs={{0,2},{2,0},{4,6},{6,4},{8,10},{10,8},{12,14},{14,12},{16,18},{18,... | collective-permute-start | bytes 1179656 | tf_op jit(solution)/shard_map/ppermute | solution.py:364
  105.5 4.0 %collective-permute-start.28 = (bf16[6,128,256]{2,1,0:T(8,128)(2,1)S(1)}, bf16[6,128,256]{2,1,0:T(8,128)(2,1)S(1)}, u32[]{:S(2)}, u32[]{:S(2)}) collective-permute-start(bf16[6,128,256]{2,1,0:T(8,128)(2,1)S(1)} %get-tuple-element.111.refs_0_), channel_id=1, source_target_pairs={{0,2},{2,0},{4,6},{6,4},{8,10},{10,8},{12,14},{14,12},{16,18},{18,... | collective-permute-start | bytes 1179656 | tf_op jit(solution)/shard_map/ppermute | solution.py:364
  109.5 2.1 %write_taps0.1 = (f32[3,512,512]{2,1,0:T(8,128)}, bf16[2048,512]{1,0:T(8,128)(2,1)}, f32[8,128]{1,0:T(8,128)S(1)}) custom-call(s32[6]{0:T(128)S(1)} %stack.27.meta, bf16[6,128,256]{2,1,0:T(8,128)(2,1)S(1)} %get-tuple-element.105.refs_0_, bf16[6,128,256]{2,1,0:T(8,128)(2,1)S(1)} %collective-permute-done.22.refs_1_, ...), custom_call_target="tpu_custom_call", output_to_operand_aliasing={{1}: (4, {})} | custom-call | flops 1 | bytes 200000 | tf_op jit(solution)/shard_map/write_taps0/pallas_call | solution.py:43
  111.7 1.8 %write_taps1.1 = (f32[3,512,512]{2,1,0:T(8,128)}, f32[8,128]{1,0:T(8,128)}) custom-call(s32[6]{0:T(128)S(1)} %stack.27.meta, bf16[6,128,256]{2,1,0:T(8,128)(2,1)S(1)} %get-tuple-element.111.refs_0_, bf16[6,128,256]{2,1,0:T(8,128)(2,1)S(1)} %collective-permute-done.28.refs_1_, ...), custom_call_target="tpu_custom_call", output_to_operand_aliasing={{0}: (3, {})} | custom-call | flops 1 | bytes 200000 | tf_op jit(solution)/shard_map/write_taps1/pallas_call | solution.py:43
  (57 shorter events, 18.9 us)
Async XLA Ops:
  2.3 4.1 %copy-start.3 = (bf16[1,2048,512]{2,1,0:T(8,128)(2,1)S(1)}, bf16[1,2048,512]{2,1,0:T(8,128)(2,1)}, u32[]{:S(2)}) copy-start(bf16[1,2048,512]{2,1,0:T(8,128)(2,1)} %param.5) | copy-start | bytes 6291460
  2.9 16.3 %collective-permute-start.4 = (bf16[1024,256]{1,0:T(8,128)(2,1)S(1)}, bf16[1024,256]{1,0:T(8,128)(2,1)S(1)}, u32[]{:S(2)}, u32[]{:S(2)}) collective-permute-start(bf16[1024,256]{1,0:T(8,128)(2,1)S(1)} %get-tuple-element.64), channel_id=1, source_target_pairs={{0,4},{2,6},{4,0},{6,2},{8,12},{10,14},{12,8},{14,10},{16,20},{18,... | collective-permute-start | bytes 1572872 | tf_op jit(solution)/shard_map/ppermute | solution.py:355
  7.2 20.7 %collective-permute-start.5 = (bf16[1024,256]{1,0:T(8,128)(2,1)S(1)}, bf16[1024,256]{1,0:T(8,128)(2,1)S(1)}, u32[]{:S(2)}, u32[]{:S(2)}) collective-permute-start(bf16[1024,256]{1,0:T(8,128)(2,1)S(1)} %get-tuple-element.65), channel_id=1, source_target_pairs={{0,4},{2,6},{4,0},{6,2},{8,12},{10,14},{12,8},{14,10},{16,20},{18,... | collective-permute-start | bytes 1572872 | tf_op jit(solution)/shard_map/ppermute | solution.py:355
  7.3 24.8 %collective-permute-start.6 = (bf16[1024,256]{1,0:T(8,128)(2,1)S(1)}, bf16[1024,256]{1,0:T(8,128)(2,1)S(1)}, u32[]{:S(2)}, u32[]{:S(2)}) collective-permute-start(bf16[1024,256]{1,0:T(8,128)(2,1)S(1)} %get-tuple-element.71.refs_6_.refs_0_.refs_1_), channel_id=1, source_target_pairs={{4,12},{6,14},{8,0},{10,2},{12,20},{14,22},{16,8},{18,10},{20,28},... | collective-permute-start | bytes 1572872 | tf_op jit(solution)/shard_map/ppermute | solution.py:358
  8.6 24.3 %collective-permute-start.7 = (bf16[1024,256]{1,0:T(8,128)(2,1)S(1)}, bf16[1024,256]{1,0:T(8,128)(2,1)S(1)}, u32[]{:S(2)}, u32[]{:S(2)}) collective-permute-start(bf16[1024,256]{1,0:T(8,128)(2,1)S(1)} %get-tuple-element.72.refs_7_.refs_1_.refs_2_), channel_id=1, source_target_pairs={{4,12},{6,14},{8,0},{10,2},{12,20},{14,22},{16,8},{18,10},{20,28},... | collective-permute-start | bytes 1572872 | tf_op jit(solution)/shard_map/ppermute | solution.py:358
  9.9 29.3 %collective-permute-start = (bf16[1024,256]{1,0:T(8,128)(2,1)S(1)}, bf16[1024,256]{1,0:T(8,128)(2,1)S(1)}, u32[]{:S(2)}, u32[]{:S(2)}) collective-permute-start(bf16[1024,256]{1,0:T(8,128)(2,1)S(1)} %get-tuple-element.62), channel_id=1, source_target_pairs={{0,4},{2,6},{4,0},{6,2},{8,12},{10,14},{12,8},{14,10},{16,20},{18,... | collective-permute-start | bytes 1572872 | tf_op jit(solution)/shard_map/ppermute | solution.py:355
  15.3 27.1 %copy-start = (bf16[3,512,512]{2,1,0:T(8,128)(2,1)S(1)}, bf16[3,512,512]{2,1,0:T(8,128)(2,1)}, u32[]{:S(2)}) copy-start(bf16[3,512,512]{2,1,0:T(8,128)(2,1)} %refs_8_.7) | copy-start | bytes 4718596
  20.3 22.1 %collective-permute-start.8 = (bf16[1024,256]{1,0:T(8,128)(2,1)S(1)}, bf16[1024,256]{1,0:T(8,128)(2,1)S(1)}, u32[]{:S(2)}, u32[]{:S(2)}) collective-permute-start(bf16[1024,256]{1,0:T(8,128)(2,1)S(1)} %get-tuple-element.68.refs_2_.refs_3_), channel_id=1, source_target_pairs={{12,4},{14,6},{0,8},{2,10},{20,12},{22,14},{8,16},{10,18},{28,20},... | collective-permute-start | bytes 1572872 | tf_op jit(solution)/shard_map/ppermute | solution.py:361
  29.0 16.3 %collective-permute-start.10 = (bf16[1024,256]{1,0:T(8,128)(2,1)S(1)}, bf16[1024,256]{1,0:T(8,128)(2,1)S(1)}, u32[]{:S(2)}, u32[]{:S(2)}) collective-permute-start(bf16[1024,256]{1,0:T(8,128)(2,1)S(1)} %get-tuple-element.70.refs_3_.refs_4_), channel_id=1, source_target_pairs={{12,4},{14,6},{0,8},{2,10},{20,12},{22,14},{8,16},{10,18},{28,20},... | collective-permute-start | bytes 1572872 | tf_op jit(solution)/shard_map/ppermute | solution.py:361
  32.1 21.0 %collective-permute-start.1 = (bf16[1024,256]{1,0:T(8,128)(2,1)S(1)}, bf16[1024,256]{1,0:T(8,128)(2,1)S(1)}, u32[]{:S(2)}, u32[]{:S(2)}) collective-permute-start(bf16[1024,256]{1,0:T(8,128)(2,1)S(1)} %get-tuple-element.63), channel_id=1, source_target_pairs={{0,4},{2,6},{4,0},{6,2},{8,12},{10,14},{12,8},{14,10},{16,20},{18,... | collective-permute-start | bytes 1572872 | tf_op jit(solution)/shard_map/ppermute | solution.py:355
  33.0 29.5 %collective-permute-start.15 = (bf16[1024,512]{1,0:T(8,128)(2,1)S(1)}, bf16[1024,512]{1,0:T(8,128)(2,1)S(1)}, u32[]{:S(2)}, u32[]{:S(2)}) collective-permute-start(bf16[1024,512]{1,0:T(8,128)(2,1)S(1)} %get-tuple-element.61.refs_8_.refs_2_.refs_1_), channel_id=1, source_target_pairs={{4,12},{6,14},{8,0},{10,2},{12,20},{14,22},{16,8},{18,10},{20,28},... | collective-permute-start | bytes 3145736 | tf_op jit(solution)/shard_map/ppermute | solution.py:358
  39.2 16.4 %collective-permute-start.2 = (bf16[1024,256]{1,0:T(8,128)(2,1)S(1)}, bf16[1024,256]{1,0:T(8,128)(2,1)S(1)}, u32[]{:S(2)}, u32[]{:S(2)}) collective-permute-start(bf16[1024,256]{1,0:T(8,128)(2,1)S(1)} %collective-permute-done.refs_9_.refs_3_.refs_2_), channel_id=1, source_target_pairs={{12,4},{14,6},{0,8},{2,10},{20,12},{22,14},{8,16},{10,18},{28,20},... | collective-permute-start | bytes 1572872 | tf_op jit(solution)/shard_map/ppermute | solution.py:361
  48.7 7.0 %collective-permute-start.11 = (bf16[4,256,256]{2,1,0:T(8,128)(2,1)S(1)}, bf16[4,256,256]{2,1,0:T(8,128)(2,1)S(1)}, u32[]{:S(2)}, u32[]{:S(2)}) collective-permute-start(bf16[4,256,256]{2,1,0:T(8,128)(2,1)S(1)} %get-tuple-element.78), channel_id=1, source_target_pairs={{0,2},{2,0},{4,6},{6,4},{8,10},{10,8},{12,14},{14,12},{16,18},{18,... | collective-permute-start | bytes 1572872 | tf_op jit(solution)/shard_map/ppermute | solution.py:364
  52.9 24.7 %collective-permute-start.9 = (bf16[1024,512]{1,0:T(8,128)(2,1)S(1)}, bf16[1024,512]{1,0:T(8,128)(2,1)S(1)}, u32[]{:S(2)}, u32[]{:S(2)}) collective-permute-start(bf16[1024,512]{1,0:T(8,128)(2,1)S(1)} %get-tuple-element.74), channel_id=1, source_target_pairs={{0,4},{2,6},{4,0},{6,2},{8,12},{10,14},{12,8},{14,10},{16,20},{18,... | collective-permute-start | bytes 3145736 | tf_op jit(solution)/shard_map/ppermute | solution.py:355
  55.2 6.2 %collective-permute-start.13 = (f32[2,256,256]{2,1,0:T(8,128)S(1)}, f32[2,256,256]{2,1,0:T(8,128)S(1)}, u32[]{:S(2)}, u32[]{:S(2)}) collective-permute-start(f32[2,256,256]{2,1,0:T(8,128)S(1)} %get-tuple-element.85), channel_id=1, source_target_pairs={{0,2},{2,0},{4,6},{6,4},{8,10},{10,8},{12,14},{14,12},{16,18},{18,... | collective-permute-start | bytes 1572872 | tf_op jit(solution)/shard_map/ppermute | solution.py:364
  56.4 9.9 %collective-permute-start.12 = (bf16[4,128,256]{2,1,0:T(8,128)(2,1)S(1)}, bf16[4,128,256]{2,1,0:T(8,128)(2,1)S(1)}, u32[]{:S(2)}, u32[]{:S(2)}) collective-permute-start(bf16[4,128,256]{2,1,0:T(8,128)(2,1)S(1)} %get-tuple-element.83), channel_id=1, source_target_pairs={{0,1},{1,0},{2,3},{3,2},{4,5},{5,4},{6,7},{7,6},{8,9},{9,8},{10,11... | collective-permute-start | bytes 786440 | tf_op jit(solution)/shard_map/ppermute | solution.py:367
  57.7 18.1 %collective-permute-start.3 = (bf16[1024,256]{1,0:T(8,128)(2,1)S(1)}, bf16[1024,256]{1,0:T(8,128)(2,1)S(1)}, u32[]{:S(2)}, u32[]{:S(2)}) collective-permute-start(bf16[1024,256]{1,0:T(8,128)(2,1)S(1)} %collective-permute-done.1.refs_4_.refs_3_), channel_id=1, source_target_pairs={{12,4},{14,6},{0,8},{2,10},{20,12},{22,14},{8,16},{10,18},{28,20},... | collective-permute-start | bytes 1572872 | tf_op jit(solution)/shard_map/ppermute | solution.py:361
  62.1 4.2 %collective-permute-start.14 = (bf16[2,128,256]{2,1,0:T(8,128)(2,1)S(1)}, bf16[2,128,256]{2,1,0:T(8,128)(2,1)S(1)}, u32[]{:S(2)}, u32[]{:S(2)}) collective-permute-start(bf16[2,128,256]{2,1,0:T(8,128)(2,1)S(1)} %get-tuple-element.88), channel_id=1, source_target_pairs={{0,1},{1,0},{2,3},{3,2},{4,5},{5,4},{6,7},{7,6},{8,9},{9,8},{10,11... | collective-permute-start | bytes 393224 | tf_op jit(solution)/shard_map/ppermute | solution.py:367
  62.4 7.9 %copy-start.2 = (bf16[1,2048,512]{2,1,0:T(8,128)(2,1)S(1)}, bf16[1,2048,512]{2,1,0:T(8,128)(2,1)}, u32[]{:S(2)}) copy-start(bf16[1,2048,512]{2,1,0:T(8,128)(2,1)} %param.3) | copy-start | bytes 6291460
  67.0 7.0 %collective-permute-start.16 = (bf16[6,64,256]{2,1,0:T(8,128)(2,1)S(1)}, bf16[6,64,256]{2,1,0:T(8,128)(2,1)S(1)}, u32[]{:S(2)}, u32[]{:S(2)}) collective-permute-start(bf16[6,64,256]{2,1,0:T(8,128)(2,1)S(1)} %get-tuple-element.94), channel_id=1, source_target_pairs={{0,8},{2,10},{4,12},{6,14},{8,0},{10,2},{12,4},{14,6},{16,24},{18,... | collective-permute-start | bytes 589832 | tf_op jit(solution)/shard_map/ppermute | solution.py:384
  69.0 40.5 %collective-permute-start.23 = (bf16[1024,512]{1,0:T(8,128)(2,1)S(1)}, bf16[1024,512]{1,0:T(8,128)(2,1)S(1)}, u32[]{:S(2)}, u32[]{:S(2)}) collective-permute-start(bf16[1024,512]{1,0:T(8,128)(2,1)S(1)} %get-tuple-element.106), channel_id=1, source_target_pairs={{0,4},{2,6},{4,0},{6,2},{8,12},{10,14},{12,8},{14,10},{16,20},{18,... | collective-permute-start | bytes 3145736 | tf_op jit(solution)/shard_map/ppermute | solution.py:355
  74.6 7.4 %collective-permute-start.17 = (bf16[6,32,256]{2,1,0:T(8,128)(2,1)S(1)}, bf16[6,32,256]{2,1,0:T(8,128)(2,1)S(1)}, u32[]{:S(2)}, u32[]{:S(2)}) collective-permute-start(bf16[6,32,256]{2,1,0:T(8,128)(2,1)S(1)} %get-tuple-element.99), channel_id=1, source_target_pairs={{0,16},{2,18},{4,20},{6,22},{8,24},{10,26},{12,28},{14,30},{16,0},... | collective-permute-start | bytes 294920 | tf_op jit(solution)/shard_map/ppermute | solution.py:384
  82.6 5.6 %collective-permute-start.18 = (f32[6,32,256]{2,1,0:T(8,128)S(1)}, f32[6,32,256]{2,1,0:T(8,128)S(1)}, u32[]{:S(2)}, u32[]{:S(2)}) collective-permute-start(f32[6,32,256]{2,1,0:T(8,128)S(1)} %get-tuple-element.101.refs_0_), channel_id=1, source_target_pairs={{0,12},{2,14},{4,8},{6,10},{8,4},{10,6},{12,0},{14,2},{16,28},{18,... | collective-permute-start | bytes 589832 | tf_op jit(solution)/shard_map/ppermute | solution.py:388
  88.8 6.1 %collective-permute-start.19 = (bf16[6,32,256]{2,1,0:T(8,128)(2,1)S(1)}, bf16[6,32,256]{2,1,0:T(8,128)(2,1)S(1)}, u32[]{:S(2)}, u32[]{:S(2)}) collective-permute-start(bf16[6,32,256]{2,1,0:T(8,128)(2,1)S(1)} %get-tuple-element.103.refs_0_), channel_id=1, source_target_pairs={{0,16},{2,18},{4,20},{6,22},{8,24},{10,26},{12,28},{14,30},{16,8},... | collective-permute-start | bytes 294920 | tf_op jit(solution)/shard_map/ppermute | solution.py:384
  90.1 5.7 %collective-permute-start.20 = (bf16[6,32,256]{2,1,0:T(8,128)(2,1)S(1)}, bf16[6,32,256]{2,1,0:T(8,128)(2,1)S(1)}, u32[]{:S(2)}, u32[]{:S(2)}) collective-permute-start(bf16[6,32,256]{2,1,0:T(8,128)(2,1)S(1)} %get-tuple-element.103.refs_0_), channel_id=1, source_target_pairs={{0,8},{2,10},{4,12},{6,14},{8,0},{10,2},{12,4},{14,6},{16,24},{18,... | collective-permute-start | bytes 294920 | tf_op jit(solution)/shard_map/ppermute | solution.py:384
  91.1 6.1 %collective-permute-start.21 = (bf16[6,32,256]{2,1,0:T(8,128)(2,1)S(1)}, bf16[6,32,256]{2,1,0:T(8,128)(2,1)S(1)}, u32[]{:S(2)}, u32[]{:S(2)}) collective-permute-start(bf16[6,32,256]{2,1,0:T(8,128)(2,1)S(1)} %get-tuple-element.103.refs_0_), channel_id=1, source_target_pairs={{0,24},{2,26},{4,28},{6,30},{8,16},{10,18},{12,20},{14,22},{16,0},... | collective-permute-start | bytes 294920 | tf_op jit(solution)/shard_map/ppermute | solution.py:384
  93.4 8.7 %collective-permute-start.24 = (bf16[6,32,256]{2,1,0:T(8,128)(2,1)S(1)}, bf16[6,32,256]{2,1,0:T(8,128)(2,1)S(1)}, u32[]{:S(2)}, u32[]{:S(2)}) collective-permute-start(bf16[6,32,256]{2,1,0:T(8,128)(2,1)S(1)} %get-tuple-element.103.refs_0_), channel_id=1, source_target_pairs={{0,1},{1,0},{2,3},{3,2},{4,5},{5,4},{6,7},{7,6},{8,9},{9,8},{10,11... | collective-permute-start | bytes 294920 | tf_op jit(solution)/shard_map/ppermute | solution.py:367
  94.9 10.0 %collective-permute-start.25 = (bf16[6,32,256]{2,1,0:T(8,128)(2,1)S(1)}, bf16[6,32,256]{2,1,0:T(8,128)(2,1)S(1)}, u32[]{:S(2)}, u32[]{:S(2)}) collective-permute-start(bf16[6,32,256]{2,1,0:T(8,128)(2,1)S(1)} %collective-permute-done.19.refs_1_), channel_id=1, source_target_pairs={{0,1},{1,0},{2,3},{3,2},{4,5},{5,4},{6,7},{7,6},{8,9},{9,8},{10,11... | collective-permute-start | bytes 294920 | tf_op jit(solution)/shard_map/ppermute | solution.py:367
  95.8 9.2 %collective-permute-start.26 = (bf16[6,32,256]{2,1,0:T(8,128)(2,1)S(1)}, bf16[6,32,256]{2,1,0:T(8,128)(2,1)S(1)}, u32[]{:S(2)}, u32[]{:S(2)}) collective-permute-start(bf16[6,32,256]{2,1,0:T(8,128)(2,1)S(1)} %collective-permute-done.20.refs_2_), channel_id=1, source_target_pairs={{0,1},{1,0},{2,3},{3,2},{4,5},{5,4},{6,7},{7,6},{8,9},{9,8},{10,11... | collective-permute-start | bytes 294920 | tf_op jit(solution)/shard_map/ppermute | solution.py:367
  97.3 7.7 %collective-permute-start.27 = (bf16[6,32,256]{2,1,0:T(8,128)(2,1)S(1)}, bf16[6,32,256]{2,1,0:T(8,128)(2,1)S(1)}, u32[]{:S(2)}, u32[]{:S(2)}) collective-permute-start(bf16[6,32,256]{2,1,0:T(8,128)(2,1)S(1)} %collective-permute-done.21.refs_3_), channel_id=1, source_target_pairs={{0,1},{1,0},{2,3},{3,2},{4,5},{5,4},{6,7},{7,6},{8,9},{9,8},{10,11... | collective-permute-start | bytes 294920 | tf_op jit(solution)/shard_map/ppermute | solution.py:367
  102.1 7.4 %collective-permute-start.22 = (bf16[6,128,256]{2,1,0:T(8,128)(2,1)S(1)}, bf16[6,128,256]{2,1,0:T(8,128)(2,1)S(1)}, u32[]{:S(2)}, u32[]{:S(2)}) collective-permute-start(bf16[6,128,256]{2,1,0:T(8,128)(2,1)S(1)} %get-tuple-element.105.refs_0_), channel_id=1, source_target_pairs={{0,2},{2,0},{4,6},{6,4},{8,10},{10,8},{12,14},{14,12},{16,18},{18,... | collective-permute-start | bytes 1179656 | tf_op jit(solution)/shard_map/ppermute | solution.py:364
  105.5 6.2 %collective-permute-start.28 = (bf16[6,128,256]{2,1,0:T(8,128)(2,1)S(1)}, bf16[6,128,256]{2,1,0:T(8,128)(2,1)S(1)}, u32[]{:S(2)}, u32[]{:S(2)}) collective-permute-start(bf16[6,128,256]{2,1,0:T(8,128)(2,1)S(1)} %get-tuple-element.111.refs_0_), channel_id=1, source_target_pairs={{0,2},{2,0},{4,6},{6,4},{8,10},{10,8},{12,14},{14,12},{16,18},{18,... | collective-permute-start | bytes 1179656 | tf_op jit(solution)/shard_map/ppermute | solution.py:364
  (1 other events, 1.6 us)
